TPU v7x, 32 devices: a whole 2x2x4 slice. The times are simulated.
32 devices in a mesh: row: 4 (over x, core), col: 2 (over y), env: 4 (over z).
Axes of the slice: x: 2, y: 2, z: 4, core: 2. Of those that a mesh axis runs over, the one named last changes fastest.
Arguments:
- corner: bfloat16 [4, 2, 1024, 1024], P('row', 'col'), may hold values from -0.1875 to 0.1875
- top_edge: bfloat16 [4, 2, 1024, 32768], P('row', 'col', 'env'), may hold values from -0.03125 to 0.03125
- half_system: bfloat16 [4, 2, 1024, 32768], P('row', 'col', 'env'), may hold values from -0.03125 to 0.03125
- values: float32 [4, 2, 1024], P('row', 'col'), may hold values from 0.5 to 4
- cotangent: bfloat16 [4, 2, 1024, 1024], P('row', 'col'), may hold values from -32 to 32
- parity: int32 [4, 2, 4, 8], P('row', 'col'), may hold values 0 or 1
Outputs:
- grad_corner: bfloat16 [4, 2, 1024, 1024], P('row', 'col', 'env')
- grad_edge: bfloat16 [4, 2, 1024, 32768], P('row', 'col', 'env')
- grad_half: bfloat16 [4, 2, 1024, 32768], P('row', 'col', 'env')
- grad_values: float32 [4, 2, 1024], P('row', 'col', 'env')
Inputs may be any that keep to these rules, and one draw needn't show every extreme that they name: `parity`: each entry is the Z2 charge of one block of 128 environment indices.
All inputs are finite; a program needn't handle non-finite values.
Results may differ from a plain program's by a relative error of at most 0.0058.
Values may be sent and summed in bfloat16 or wider, within the bound.
No kernel may reach another device: no remote copies, remote signals or barrier semaphores. Data moves between devices by JAX's collectives and lax.ppermute only.
A program may use at most 192 MiB of HBM per device.

v0:
```python
import jax
import jax.numpy as jnp
from jax import lax
from jax.sharding import PartitionSpec as P

CHI = 1024
HALF = 32
BLK = 128


def passed_along(x, axis, by):
    size = lax.axis_size(axis)
    return lax.ppermute(x, axis, [(i, (i + by) % size) for i in range(size)])


def side_column(tensor, direction):
    return passed_along(tensor, "col", direction)


def side_row(tensor, direction):
    return passed_along(tensor, "row", direction)


def row_sums(term_fn, shard_rows):
    return lax.psum_scatter(
        term_fn(jnp.int32(0), shard_rows * lax.axis_size("env")),
        "env",
        scatter_dimension=0,
        tiled=True,
    )


def shards(corner, top_edge, half_system, values, cotangent, parity):
    shard_rows = top_edge.shape[2]
    row_start = lax.axis_index("env") * shard_rows
    charges = jnp.repeat(parity[0, 0], BLK, axis=1)
    corner_mask = charges[0][:, None] == charges[1][None, :]
    out_mask = charges[2][:, None] == charges[3][None, :]
    near_corner = side_column(corner[0, 0], 1)
    near_corner = jnp.where(corner_mask, near_corner, jnp.zeros_like(near_corner))
    lower_half = side_row(half_system[0, 0], -1).reshape(shard_rows, CHI, HALF)
    absorbed = jnp.einsum(
        "ab,iak->ibk", near_corner, lower_half, preferred_element_type=jnp.float32
    )
    absorbed = absorbed.astype(jnp.bfloat16).reshape(shard_rows, CHI * HALF)
    gathered = lax.all_to_all(absorbed, "env", split_axis=1, concat_axis=0, tiled=True)
    edge_mat = top_edge[0, 0].reshape(shard_rows * HALF, CHI)
    weight = values[0, 0] ** (-0.5)
    grad_new = jnp.where(
        out_mask, weight[:, None] * cotangent[0, 0].astype(jnp.float32), 0.0
    ).astype(jnp.bfloat16)
    grad_edge = jnp.einsum("ij,ie->je", gathered, grad_new, preferred_element_type=jnp.float32)
    grad_edge = grad_edge.astype(jnp.bfloat16).reshape(shard_rows, HALF * CHI)
    grad_full = jnp.einsum("ie,je->ij", grad_new, edge_mat, preferred_element_type=jnp.float32)
    totals = lax.psum(jnp.sum(gathered * grad_full, axis=1), "env")
    pair_sums = lax.dynamic_slice_in_dim(totals, row_start, shard_rows, 0)
    own_values = lax.dynamic_slice_in_dim(values[0, 0], row_start, shard_rows, 0)
    grad_values = -0.5 * pair_sums / own_values
    grad_back = lax.all_to_all(
        grad_full.astype(jnp.bfloat16), "env", split_axis=0, concat_axis=1, tiled=True
    )
    grad_back = grad_back.reshape(shard_rows, CHI, HALF)
    grad_half = jnp.einsum(
        "ab,ibk->iak", near_corner, grad_back, preferred_element_type=jnp.float32
    )
    grad_half = grad_half.astype(jnp.bfloat16).reshape(shard_rows, CHI * HALF)

    def corner_terms(offset, length):
        return jnp.einsum("iak,ibk->ab", lower_half, grad_back, preferred_element_type=jnp.float32)

    summed = row_sums(corner_terms, shard_rows)
    own_mask = lax.dynamic_slice_in_dim(corner_mask, row_start, shard_rows, 0)
    grad_corner = jnp.where(own_mask, summed, 0.0).astype(jnp.bfloat16)
    grad_corner = side_column(grad_corner, -1)
    grad_half = side_row(grad_half, 1)
    return (
        grad_corner[None, None],
        grad_edge[None, None],
        grad_half[None, None],
        grad_values[None, None],
    )


def solution(mesh):
    placed = (
        P("row", "col", None, None),
        P("row", "col", "env", None),
        P("row", "col", "env", None),
        P("row", "col", None),
        P("row", "col", None, None),
        P("row", "col", None, None),
    )
    return jax.shard_map(
        shards,
        mesh=mesh,
        in_specs=placed,
        out_specs=(
            P("row", "col", "env", None),
            P("row", "col", "env", None),
            P("row", "col", "env", None),
            P("row", "col", "env"),
        ),
        check_vma=False,
    )
```

profile of v0, /device:TPU:9, one launch (start us, length us, event | category | flops | bytes accessed | tf_op | source)
XLA Modules:
  0.0 1383.3 jit_solution(3680317878180812675)
XLA Ops:
  7.2 22.5 %copy.15 = bf16[1,1,256,32768]{2,3,1,0:T(8,128)(2,1)} copy(bf16[1,1,256,32768]{3,2,1,0:T(8,128)(2,1)} %param.8) | data formatting | bytes 33554432 | tf_op args[2]
  30.4 2.5 copy.18
  34.2 178.6 %collective-permute-done = bf16[256,32768]{0,1:T(8,128)(2,1)} collective-permute-done((bf16[256,32768]{0,1:T(8,128)(2,1)}, bf16[256,32768]{0,1:T(8,128)(2,1)}, u32[]{:S(2)}, u32[]{:S(2)}) %collective-permute-start) | collective-permute-done | bytes 16777248 | tf_op jit(solution)/shard_map/ppermute | solution.py:13
  212.8 23.0 %copy.17 = bf16[256,1024,32]{1,0,2:T(8,128)(2,1)} copy(bf16[256,1024,32]{0,2,1:T(8,128)(2,1)} %bitcast.14) | data formatting | bytes 33554432 | tf_op jit(solution)/shard_map/reshape | solution.py:41
  235.8 24.4 %convert_bitcast_fusion.1 = bf16[256,1024,32]{0,1,2:T(8,128)(2,1)} fusion(bf16[256,1024,32]{1,0,2:T(8,128)(2,1)} %copy.17, bf16[1024,1024]{0,1:T(8,128)(2,1)} %collective-permute-done.2, s32[1024]{0:T(1024)S(1)} %get-tuple-element.22, s32[1024]{0:T(1024)S(1)} %get-tuple-element.21), kind=kOutput, calls=%fused_computation.2 | convolution fusion | flops 17190354944 | bytes 35659776 | tf_op jit(solution)/shard_map/ab,iak->ibk/dot_general | solution.py:42
  260.2 17.9 %copy.20 = bf16[256,1024,32]{0,2,1:T(8,128)(2,1)} copy(bf16[256,1024,32]{0,1,2:T(8,128)(2,1)} %convert_bitcast_fusion.1) | data formatting | bytes 33554432 | tf_op jit(solution)/shard_map/convert_element_type | solution.py:45
  278.1 7.1 all-to-all-start.1
  285.4 25.6 %reshape_squeeze.3 = bf16[8192,1024]{1,0:T(8,128)(2,1)} reshape(bf16[1,1,256,32768]{3,2,1,0:T(8,128)(2,1)} %param.7) | data formatting | bytes 33554432 | tf_op jit(solution)/shard_map/reshape;squeeze | solution.py:47
  311.1 334.2 %all-to-all-done.1 = bf16[256,4,8192]{0,2,1:T(8,128)(2,1)} async-done(((bf16[256,4,8192]{0,2,1:T(8,128)(2,1)}), bf16[256,4,8192]{0,2,1:T(8,128)(2,1)}, u32[]{:S(2)}, u32[]{:S(2)}) %all-to-all-start.1) | async-done | bytes 16777248 | tf_op jit(solution)/shard_map/all_to_all | solution.py:46
  645.4 21.2 %copy.21 = bf16[4,256,8192]{2,1,0:T(8,128)(2,1)} copy(bf16[4,256,8192]{1,2,0:T(8,128)(2,1)} %bitcast.22) | data formatting | bytes 33554432 | tf_op jit(solution)/shard_map/all_to_all | solution.py:46
  666.6 24.9 %multiply_reduce_fusion = (f32[1024]{0:T(1024)S(1)}, bf16[1024,8192]{1,0:T(8,128)(2,1)}) fusion(bf16[4,256,8192]{2,1,0:T(8,128)(2,1)} %copy.21, bf16[8192,1024]{1,0:T(8,128)(2,1)} %reshape_squeeze.3, bf16[1,1,1024,1024]{3,2,1,0:T(8,128)(2,1)} %param.10, f32[1024]{0:T(1024)S(1)} %bitcast.70, s32[1024]{0:T(1024)S(1)} %get-tuple-element.19, ...), kind=kOutput, calls=%fused_computation | convolution fusion | flops 17218666496 | bytes 52445184 | tf_op jit(solution)/shard_map/ie,je->ij/dot_general | solution.py:54
  691.4 21.2 %copy.14 = bf16[4,256,8192]{1,2,0:T(8,128)(2,1)} copy(bf16[4,256,8192]{2,1,0:T(8,128)(2,1)} %bitcast.66) | data formatting | bytes 33554432 | tf_op jit(solution)/shard_map/all_to_all | solution.py:59
  712.6 374.7 %all_to_all.35 = bf16[4,256,8192]{1,2,0:T(8,128)(2,1)} all-to-all(bf16[4,256,8192]{1,2,0:T(8,128)(2,1)} %copy.14), channel_id=1, replica_groups=mesh['row'=4,'col'=2,'env'=4] {'env'}, dimensions={0} | all-to-all | bytes 33554432 | tf_op jit(solution)/shard_map/all_to_all | solution.py:59
  1087.3 23.2 %copy.22 = bf16[256,1024,32]{1,0,2:T(8,128)(2,1)} copy(bf16[256,1024,32]{0,2,1:T(8,128)(2,1)} %bitcast.62) | data formatting | bytes 33554432 | tf_op jit(solution)/shard_map/reshape | solution.py:62
  1110.5 27.5 %convert_bitcast_fusion = bf16[256,1024,32]{1,0,2:T(8,128)(2,1)} fusion(bf16[256,1024,32]{1,0,2:T(8,128)(2,1)} %copy.22, bf16[1024,1024]{0,1:T(8,128)(2,1)} %collective-permute-done.2, s32[1024]{0:T(1024)S(1)} %get-tuple-element.22, s32[1024]{0:T(1024)S(1)} %get-tuple-element.21), kind=kOutput, calls=%fused_computation.1 | convolution fusion | flops 17190354944 | bytes 35659776 | tf_op jit(solution)/shard_map/ab,ibk->iak/dot_general | solution.py:63
  1138.0 23.9 %copy.24 = bf16[256,1024,32]{0,2,1:T(8,128)(2,1)} copy(bf16[256,1024,32]{1,0,2:T(8,128)(2,1)} %convert_bitcast_fusion) | data formatting | bytes 33554432 | tf_op jit(solution)/shard_map/convert_element_type | solution.py:66
  1161.9 12.5 collective-permute-start.3
  1174.5 23.9 %convolution_bitcast_fusion = f32[1024,1024]{0,1:T(8,128)} fusion(bf16[256,1024,32]{1,0,2:T(8,128)(2,1)} %copy.22, bf16[256,1024,32]{1,0,2:T(8,128)(2,1)} %copy.17), kind=kOutput, calls=%fused_computation.5 | convolution fusion | flops 17179869184 | bytes 37748736 | tf_op jit(solution)/shard_map/iak,ibk->ab/dot_general | solution.py:69
  1199.0 76.2 %reduce-scatter.2.cloned.1.call-done = f32[256,1024]{0,1:T(8,128)} async-done(((f32[1024,1024]{0,1:T(8,128)}), f32[256,1024]{0,1:T(8,128)}) %reduce-scatter.2.cloned.1.call-update) | async-done | bytes 1048592 | tf_op jit(solution)/shard_map/reduce_scatter | solution.py:25
  1277.8 25.9 %convolution_convert_fusion = bf16[8192,1024]{1,0:T(8,128)(2,1)} fusion(bf16[1024,8192]{1,0:T(8,128)(2,1)} %bitcast.64, bf16[1,1,1024,1024]{3,2,1,0:T(8,128)(2,1)} %param.10, f32[1024]{0:T(1024)S(1)} %bitcast.71, s32[1024]{0:T(1024)S(1)} %get-tuple-element.19, s32[1024]{0:T(1024)S(1)} %get-tuple-element.20), kind=kOutput, calls=%fused_computation.3 | convolution fusion | flops 17193500672 | bytes 35663872 | tf_op jit(solution)/shard_map/ij,ie->je/dot_general | solution.py:52
  1303.7 25.5 %broadcast_in_dim_reshape.3 = bf16[1,1,256,32768]{3,2,1,0:T(8,128)(2,1)} reshape(bf16[8192,1024]{1,0:T(8,128)(2,1)} %convolution_convert_fusion) | data formatting | bytes 33554432 | tf_op jit(solution)/shard_map/broadcast_in_dim;reshape | solution.py:78
  1329.3 7.8 psum.7
  1338.7 16.3 %collective-permute-done.3 = bf16[256,32768]{0,1:T(8,128)(2,1)} collective-permute-done((bf16[256,32768]{0,1:T(8,128)(2,1)}, bf16[256,32768]{0,1:T(8,128)(2,1)}, u32[]{:S(2)}, u32[]{:S(2)}) %collective-permute-start.3) | collective-permute-done | bytes 16777248 | tf_op jit(solution)/shard_map/ppermute | solution.py:13
  1355.0 21.2 %copy.26 = bf16[1,1,256,32768]{3,2,1,0:T(8,128)(2,1)} copy(bf16[1,1,256,32768]{2,3,1,0:T(8,128)(2,1)} %bitcast.28) | data formatting | bytes 33554432
  (22 shorter events, 7.3 us)
Async XLA Ops:
  7.2 23.2 %copy-start = (bf16[1,1,1024,1024]{3,2,1,0:T(8,128)(2,1)S(1)}, bf16[1,1,1024,1024]{3,2,1,0:T(8,128)(2,1)}, u32[]{:S(2)}) copy-start(bf16[1,1,1024,1024]{3,2,1,0:T(8,128)(2,1)} %param.6) | copy-start | bytes 6291460
  7.2 27.0 %copy-start.2 = (s32[1,1,4,8]{3,2,1,0:T(4,128)S(1)}, s32[1,1,4,8]{3,2,1,0:T(4,128)}, u32[]{:S(2)}) copy-start(s32[1,1,4,8]{3,2,1,0:T(4,128)} %param.11) | copy-start | bytes 388
  29.7 183.1 %collective-permute-start = (bf16[256,32768]{0,1:T(8,128)(2,1)}, bf16[256,32768]{0,1:T(8,128)(2,1)}, u32[]{:S(2)}, u32[]{:S(2)}) collective-permute-start(bf16[256,32768]{0,1:T(8,128)(2,1)} %bitcast.65), channel_id=1, source_target_pairs={{0,24},{8,0},{16,8},{24,16},{1,25},{9,1},{17,9},{25,17},{2,26},{10... | collective-permute-start | bytes 50331656 | tf_op jit(solution)/shard_map/ppermute | solution.py:13
  32.9 202.9 %collective-permute-start.2 = (bf16[1024,1024]{0,1:T(8,128)(2,1)}, bf16[1024,1024]{0,1:T(8,128)(2,1)}, u32[]{:S(2)}, u32[]{:S(2)}) collective-permute-start(bf16[1024,1024]{0,1:T(8,128)(2,1)} %bitcast.67), channel_id=1, source_target_pairs={{0,4},{4,0},{1,5},{5,1},{2,6},{6,2},{3,7},{7,3},{8,12},{12,8},{9,1... | collective-permute-start | bytes 6291464 | tf_op jit(solution)/shard_map/ppermute | solution.py:13
  278.1 367.3 %all-to-all-start.1 = ((bf16[256,4,8192]{0,2,1:T(8,128)(2,1)}), bf16[256,4,8192]{0,2,1:T(8,128)(2,1)}, u32[]{:S(2)}, u32[]{:S(2)}) async-start(bf16[256,4,8192]{0,2,1:T(8,128)(2,1)} %bitcast.61), calls=%async_computation.2 | async-start | bytes 33554432 | tf_op jit(solution)/shard_map/all_to_all | solution.py:46
  285.2 25.9 %copy-start.1 = (f32[1,1,1024]{2,1,0:T(1,128)S(1)}, f32[1,1,1024]{2,1,0:T(1,128)}, u32[]{:S(2)}) copy-start(f32[1,1,1024]{2,1,0:T(1,128)} %param.9) | copy-start | bytes 12292
  285.2 990.0 %reduce-scatter.2.cloned.1.call-start = ((), (), s32[]{:S(2)}) async-start(), calls=%async_computation.3 | async-start | bytes 5242880 | tf_op jit(solution)/shard_map/reduce_scatter | solution.py:25
  1161.9 193.1 %collective-permute-start.3 = (bf16[256,32768]{0,1:T(8,128)(2,1)}, bf16[256,32768]{0,1:T(8,128)(2,1)}, u32[]{:S(2)}, u32[]{:S(2)}) collective-permute-start(bf16[256,32768]{0,1:T(8,128)(2,1)} %bitcast.63), channel_id=1, source_target_pairs={{0,8},{8,16},{16,24},{24,0},{1,9},{9,17},{17,25},{25,1},{2,10},{10... | collective-permute-start | bytes 50331656 | tf_op jit(solution)/shard_map/ppermute | solution.py:13
  1276.6 61.1 %collective-permute-start.1 = (bf16[256,1024]{0,1:T(8,128)(2,1)S(1)}, bf16[256,1024]{0,1:T(8,128)(2,1)S(1)}, u32[]{:S(2)}, u32[]{:S(2)}) collective-permute-start(bf16[256,1024]{0,1:T(8,128)(2,1)S(1)} %select_convert_fusion.1), channel_id=1, source_target_pairs={{0,4},{4,0},{1,5},{5,1},{2,6},{6,2},{3,7},{7,3},{8,12},{12,8},{9,1... | collective-permute-start | bytes 1572872 | tf_op jit(solution)/shard_map/ppermute | solution.py:13
Sparse Core Ops, SparseCore 0:
  1198.5 76.6 reduce-scatter.1
where the time goes:
time: 1390 us; the launch traced here: 1380 us
  waiting for transfers between devices  605 us (44%)
  blocking collectives  382 us (27%)
  local copies, waits for them, and re-layouts  229 us (16%)
  matrix products  126 us (9%)
  starting transfers between devices  23 us (2%)
  between operations  14.3 us (1%)
    all_to_all x1, blocking collectives, shards(): lax.all_to_all(grad_full.astype(jnp.bfloat16), 'env', split_axis=0, conca...  375 us
    all_to_all x1, waiting for transfers between devices, shards(): lax.all_to_all(absorbed, 'env', split_axis=1, concat_axis=0, tiled=True)  334 us
    ppermute x4, waiting for transfers between devices, passed_along(): return lax.ppermute(x, axis, [(i, (i + by) % size) for i in range(size)])  195 us
    reduce_scatter x1, waiting for transfers between devices, row_sums(): lax.psum_scatter(term_fn(jnp.int32(0), shard_rows * lax.axis_size('env'))...  76.2 us
    unnamed x10, local copies, waits for them, and re-layouts  47.3 us
  transfers between devices with their start and end apart: 6, of which 4 were waited for; matrix products, arithmetic and copies ran while one was open for 9% of the time, Pallas kernels for 0%

commit v1 on v0

v1 whole, which is shorter than its diff:
```python
import functools

import jax
import jax.numpy as jnp
from jax import lax
from jax.experimental import pallas as pl
from jax.experimental.pallas import tpu as pltpu
from jax.sharding import PartitionSpec as P

CHI = 1024
HALF = 32
BLK = 128

FULL_CHUNKS = (4, 12, 16)
EDGE_CHUNKS = (4, 6, 6, 6, 4, 3, 2, 1)

MIB = 1 << 20
F32 = jnp.float32
BF16 = jnp.bfloat16


def passed_along(x, axis, by):
    size = lax.axis_size(axis)
    return lax.ppermute(x, axis, [(i, (i + by) % size) for i in range(size)])


def swapped(x, d):
    return lax.ppermute(x, "env", [(i, i ^ d) for i in range(lax.axis_size("env"))])


def nn(a, b):
    return jnp.dot(a, b, preferred_element_type=F32)


def nt(a, b):
    return lax.dot_general(a, b, (((1,), (1,)), ((), ())), preferred_element_type=F32)


ANYWHERE = pl.BlockSpec(memory_space=pl.ANY)


def params(mib):
    return pltpu.CompilerParams(
        vmem_limit_bytes=mib * MIB, dimension_semantics=("arbitrary",)
    )


def cost(count, rows, moved):
    return pl.CostEstimate(
        flops=2 * count * rows * CHI * CHI, bytes_accessed=moved, transcendentals=0
    )


def full_chunk(me, top_edge, grad_new, first, count, after):
    rows = top_edge.shape[0]
    n = CHI // rows
    n_after = len(after)

    def kernel(me_ref, t_ref, *refs):
        g_refs, outs = refs[:n], refs[n + n_after:]
        t = t_ref[...]
        for g_ref, out in zip(g_refs, outs):
            out[0] = nt(t, g_ref[...]).astype(BF16)

    def grad_spec(d):
        return pl.BlockSpec((rows, CHI), lambda k, me: (me[0] ^ d, 0))

    return pl.pallas_call(
        kernel,
        grid_spec=pltpu.PrefetchScalarGridSpec(
            num_scalar_prefetch=1,
            grid=(count,),
            in_specs=[pl.BlockSpec((rows, CHI), lambda k, me: (0, first + k))]
            + [grad_spec(d) for d in range(n)] + [ANYWHERE] * n_after,
            out_specs=[pl.BlockSpec((1, rows, rows), lambda k, me: (k, 0, 0))] * n,
        ),
        out_shape=[jax.ShapeDtypeStruct((count, rows, rows), BF16)] * n,
        compiler_params=params(24),
        cost_estimate=cost(count, rows, 4 * count * rows * CHI),
        name="grad_full",
    )(me, top_edge, *[grad_new] * n, *after)


def absorbed_chunk(me, lower, corner_t, first, count, after):
    rows = lower.shape[2]
    n = CHI // rows
    n_after = len(after)

    def kernel(me_ref, l_ref, *refs):
        c_refs, outs = refs[:n], refs[n + n_after:]
        low = l_ref[0]
        for c_ref, out in zip(c_refs, outs):
            out[0] = nn(c_ref[...], low).astype(BF16)

    def corner_spec(d):
        return pl.BlockSpec((rows, CHI), lambda k, me: (me[0] ^ d, 0))

    return pl.pallas_call(
        kernel,
        grid_spec=pltpu.PrefetchScalarGridSpec(
            num_scalar_prefetch=1,
            grid=(count,),
            in_specs=[pl.BlockSpec((1, CHI, rows), lambda k, me: (first + k, 0, 0))]
            + [corner_spec(d) for d in range(n)] + [ANYWHERE] * n_after,
            out_specs=[pl.BlockSpec((1, rows, rows), lambda k, me: (k, 0, 0))] * n,
        ),
        out_shape=[jax.ShapeDtypeStruct((count, rows, rows), BF16)] * n,
        compiler_params=params(24),
        cost_estimate=cost(count, rows, 4 * count * rows * CHI),
        name="absorbed",
    )(me, lower, *[corner_t] * n, *after)


def half_chunk(me, blocks, lower, corner, held, first, count):
    rows = lower.shape[2]
    n = CHI // rows
    step = 2 if count % 2 == 0 and first % 2 == 0 else 1
    has_held = held is not None

    def kernel(me_ref, l_ref, *refs):
        f_refs, c_refs = refs[:n], refs[n:2 * n]
        half_ref, corner_ref, pair_ref = refs[-3:]

        @pl.when(pl.program_id(0) == 0)
        def _():
            corner_ref[...] = jnp.zeros_like(corner_ref)
            pair_ref[...] = jnp.zeros_like(pair_ref)

        for j in range(step):
            total = nn(c_refs[0][...], f_refs[0][j])
            for d in range(1, n):
                total += nn(c_refs[d][...], f_refs[d][j])
            half_ref[j] = total.astype(BF16)
            part = total * l_ref[j].astype(F32)
            pair_ref[...] += jnp.sum(part.reshape(CHI // 8, 8, rows), axis=0)
        low = jnp.concatenate([l_ref[j] for j in range(step)], axis=1)
        for d in range(n):
            full = jnp.concatenate([f_refs[d][j] for j in range(step)], axis=1)
            place = pl.ds(pl.multiple_of((me_ref[0] ^ d) * rows, rows), rows)
            corner_ref[:, place] += nt(low, full)

    def corner_spec(d):
        return pl.BlockSpec((CHI, rows), lambda k, me: (0, me[0] ^ d))

    operands = [me, lower, *blocks, *[corner] * n] + ([held] if has_held else [])
    return pl.pallas_call(
        kernel,
        grid_spec=pltpu.PrefetchScalarGridSpec(
            num_scalar_prefetch=1,
            grid=(count // step,),
            in_specs=[pl.BlockSpec((step, CHI, rows), lambda k, me: (first // step + k, 0, 0))]
            + [pl.BlockSpec((step, rows, rows), lambda k, me: (k, 0, 0))] * n
            + [corner_spec(d) for d in range(n)] + [ANYWHERE] * has_held,
            out_specs=[
                pl.BlockSpec((step, CHI, rows), lambda k, me: (first // step + k, 0, 0)),
                pl.BlockSpec((CHI, CHI), lambda k, me: (0, 0)),
                pl.BlockSpec((8, rows), lambda k, me: (0, 0)),
            ],
        ),
        out_shape=[
            jax.ShapeDtypeStruct(lower.shape, BF16),
            jax.ShapeDtypeStruct((CHI, CHI), F32),
            jax.ShapeDtypeStruct((8, rows), F32),
        ],
        input_output_aliases={len(operands) - 1: 0} if has_held else {},
        compiler_params=params(40),
        cost_estimate=cost(2 * count, rows, 6 * count * rows * CHI),
        name="grad_half",
    )(*operands)


def edge_chunk(me, blocks, grad_new, held, first, count):
    rows = blocks[0].shape[1]
    n = CHI // rows
    has_held = held is not None

    def kernel(me_ref, *refs):
        a_refs, g_refs, out = refs[:n], refs[n:2 * n], refs[-1]
        total = nn(a_refs[0][0], g_refs[0][...])
        for d in range(1, n):
            total += nn(a_refs[d][0], g_refs[d][...])
        out[...] = total.astype(BF16)

    def grad_spec(d):
        return pl.BlockSpec((rows, CHI), lambda k, me: (me[0] ^ d, 0))

    operands = [me, *blocks, *[grad_new] * n] + ([held] if has_held else [])
    return pl.pallas_call(
        kernel,
        grid_spec=pltpu.PrefetchScalarGridSpec(
            num_scalar_prefetch=1,
            grid=(count,),
            in_specs=[pl.BlockSpec((1, rows, rows), lambda k, me: (k, 0, 0))] * n
            + [grad_spec(d) for d in range(n)] + [ANYWHERE] * has_held,
            out_specs=pl.BlockSpec((rows, CHI), lambda k, me: (0, first + k)),
        ),
        out_shape=jax.ShapeDtypeStruct((rows, HALF * CHI), BF16),
        input_output_aliases={len(operands) - 1: 0} if has_held else {},
        compiler_params=params(24),
        cost_estimate=cost(count, rows, 4 * count * rows * CHI),
        name="grad_edge",
    )(*operands)


def exchanged(blocks):
    return [blocks[0]] + [swapped(blocks[d], d) for d in range(1, len(blocks))]


def summed_rows(partial, me, rows):
    left = partial.reshape(CHI // rows, rows, CHI)
    bit = 1
    while left.shape[0] > 1:
        pairs = left.reshape(left.shape[0] // 2, 2, rows, CHI)
        own = lax.rem(lax.div(me, jnp.int32(bit)), jnp.int32(2))
        kept = lax.dynamic_index_in_dim(pairs, own, 1, keepdims=False)
        sent = lax.dynamic_index_in_dim(pairs, 1 - own, 1, keepdims=False).astype(BF16)
        left = kept + swapped(sent, bit).astype(F32)
        bit *= 2
    return left[0]


def charge_masks(parity):
    charges = jnp.repeat(parity, BLK, axis=1)
    corner_mask = charges[0][:, None] == charges[1][None, :]
    out_mask = charges[2][:, None] == charges[3][None, :]
    return corner_mask, out_mask


def chunked_shards(corner, top_edge, half_system, values, cotangent, parity):
    rows = top_edge.shape[2]
    me = lax.axis_index("env").astype(jnp.int32)
    me_arr = me.reshape(1)
    corner_mask, out_mask = charge_masks(parity[0, 0])

    grad_new = jnp.where(
        out_mask, values[0, 0][:, None] ** (-0.5) * cotangent[0, 0].astype(F32), 0.0
    ).astype(BF16)

    lower_half = passed_along(half_system[0, 0], "row", -1)
    near_corner = passed_along(corner[0, 0], "col", 1)
    near_corner = jnp.where(corner_mask, near_corner, jnp.zeros_like(near_corner))

    in_flight = []

    def waits():
        return in_flight[-2] if len(in_flight) > 1 else []

    full_parts, first = [], 0
    for count in FULL_CHUNKS:
        blocks = full_chunk(me_arr, top_edge[0, 0], grad_new, first, count, waits())
        blocks = exchanged(blocks)
        in_flight.append(blocks[1:])
        full_parts.append((first, count, blocks))
        first += count

    lower = lower_half.T.reshape(CHI, HALF, rows).transpose(1, 0, 2)
    corner_t = near_corner.T

    edge_parts, first = [], 0
    for count in EDGE_CHUNKS:
        blocks = absorbed_chunk(me_arr, lower, corner_t, first, count, waits())
        blocks = exchanged(blocks)
        in_flight.append(blocks[1:])
        edge_parts.append((first, count, blocks))
        first += count

    grad_half, corner_total, pair_total = None, 0.0, 0.0
    for first, count, blocks in full_parts:
        grad_half, corner_part, pair_part = half_chunk(
            me_arr, blocks, lower, near_corner, grad_half, first, count
        )
        corner_total = corner_total + corner_part
        pair_total = pair_total + pair_part

    own_values = lax.dynamic_slice_in_dim(values[0, 0], me * rows, rows, 0)
    grad_values = -0.5 * jnp.sum(pair_total, axis=0) / own_values

    grad_half = grad_half.transpose(1, 0, 2).reshape(CHI * HALF, rows).T
    grad_half = passed_along(grad_half, "row", 1)

    own_mask = lax.dynamic_slice_in_dim(corner_mask, me * rows, rows, 0)
    grad_corner = jnp.where(own_mask, summed_rows(corner_total, me, rows), 0.0)
    grad_corner = passed_along(grad_corner.astype(BF16), "col", -1)

    grad_edge = None
    for first, count, blocks in edge_parts:
        grad_edge = edge_chunk(me_arr, blocks, grad_new, grad_edge, first, count)

    return (
        grad_corner[None, None],
        grad_edge[None, None],
        grad_half[None, None],
        grad_values[None, None],
    )


def whole_shards(corner, top_edge, half_system, values, cotangent, parity):
    rows = top_edge.shape[2]
    row_start = lax.axis_index("env") * rows
    corner_mask, out_mask = charge_masks(parity[0, 0])
    near_corner = passed_along(corner[0, 0], "col", 1)
    near_corner = jnp.where(corner_mask, near_corner, jnp.zeros_like(near_corner))
    lower_half = passed_along(half_system[0, 0], "row", -1).reshape(rows, CHI, HALF)
    absorbed = jnp.einsum("ab,iak->ibk", near_corner, lower_half, preferred_element_type=F32)
    absorbed = absorbed.astype(BF16).reshape(rows, CHI * HALF)
    gathered = lax.all_to_all(absorbed, "env", split_axis=1, concat_axis=0, tiled=True)
    edge_mat = top_edge[0, 0].reshape(rows * HALF, CHI)
    grad_new = jnp.where(
        out_mask, values[0, 0][:, None] ** (-0.5) * cotangent[0, 0].astype(F32), 0.0
    ).astype(BF16)
    grad_edge = jnp.einsum("ij,ie->je", gathered, grad_new, preferred_element_type=F32)
    grad_edge = grad_edge.astype(BF16).reshape(rows, HALF * CHI)
    grad_full = jnp.einsum("ie,je->ij", grad_new, edge_mat, preferred_element_type=F32)
    totals = lax.psum(jnp.sum(gathered * grad_full, axis=1), "env")
    pair_sums = lax.dynamic_slice_in_dim(totals, row_start, rows, 0)
    own_values = lax.dynamic_slice_in_dim(values[0, 0], row_start, rows, 0)
    grad_values = -0.5 * pair_sums / own_values
    grad_back = lax.all_to_all(
        grad_full.astype(BF16), "env", split_axis=0, concat_axis=1, tiled=True
    ).reshape(rows, CHI, HALF)
    grad_half = jnp.einsum("ab,ibk->iak", near_corner, grad_back, preferred_element_type=F32)
    grad_half = grad_half.astype(BF16).reshape(rows, CHI * HALF)
    summed = jnp.einsum("iak,ibk->ab", lower_half, grad_back, preferred_element_type=F32)
    summed = lax.psum_scatter(summed, "env", scatter_dimension=0, tiled=True)
    own_mask = lax.dynamic_slice_in_dim(corner_mask, row_start, rows, 0)
    grad_corner = jnp.where(own_mask, summed, 0.0).astype(BF16)
    grad_corner = passed_along(grad_corner, "col", -1)
    grad_half = passed_along(grad_half, "row", 1)
    return (
        grad_corner[None, None],
        grad_edge[None, None],
        grad_half[None, None],
        grad_values[None, None],
    )


def solution(mesh):
    n = mesh.shape["env"]
    chunked = n & (n - 1) == 0 and CHI // n % BLK == 0
    return jax.shard_map(
        chunked_shards if chunked else whole_shards,
        mesh=mesh,
        in_specs=(
            P("row", "col", None, None),
            P("row", "col", "env", None),
            P("row", "col", "env", None),
            P("row", "col", None),
            P("row", "col", None, None),
            P("row", "col", None, None),
        ),
        out_specs=(
            P("row", "col", "env", None),
            P("row", "col", "env", None),
            P("row", "col", "env", None),
            P("row", "col", "env"),
        ),
        check_vma=False,
    )
```

time: 1390 us -> 912 us (0.66)
  blocking collectives: 382 us -> 0 us
  Pallas kernels: 0 us -> 143 us
  matrix products: 126 us -> 0 us
  waiting for transfers between devices: 605 us -> 532 us
  local copies, waits for them, and re-layouts: 229 us -> 159 us
  starting transfers between devices: 23 us -> 57.9 us
    ppermute x0 -> x35, waiting for transfers between devices: none -> 464 us  [swapped(): lax.ppermute(x, 'env', [(i, i ^ d) for i in range(lax.axis_size('env'))])]
    all_to_all x1 -> x0, blocking collectives: 375 us -> none  [shards(): lax.all_to_all(grad_full.astype(jnp.bfloat16), 'env', split_axis=0, conca...]
    all_to_all x1 -> x0, waiting for transfers between devices: 334 us -> none  [shards(): lax.all_to_all(absorbed, 'env', split_axis=1, concat_axis=0, tiled=True)]
    pallas_call x0 -> x22, Pallas kernels: none -> 143 us  [the longest x3 50.8 us: half_chunk(): pl.pallas_call(kernel, grid_spec=pltpu.PrefetchScalarGridSpec(num_scalar_...]
    ppermute x4, waiting for transfers between devices: 195 us -> 68.1 us  [passed_along(): return lax.ppermute(x, axis, [(i, (i + by) % size) for i in range(size)])]
    dot_general x5 -> x0, matrix products: 126 us -> none  [the longest x1 27.5 us: shards(): jnp.einsum('ab,ibk->iak', near_corner, grad_back, preferred_element_type=...]
    reduce_scatter x1 -> x0, waiting for transfers between devices: 76.2 us -> none  [row_sums(): lax.psum_scatter(term_fn(jnp.int32(0), shard_rows * lax.axis_size('env'))...]
    unnamed x10 -> x109, local copies, waits for them, and re-layouts: 47.3 us -> 115 us
  transfers between devices with their start and end apart: 6 -> 39, of which waited for: 4 -> 21; matrix products, arithmetic and copies ran while one was open for 9% -> 5% of each run, Pallas kernels for 0% -> 13%
where the time goes in v1:
time: 912 us; the launch traced here: 909 us
  waiting for transfers between devices  532 us (58%)
  local copies, waits for them, and re-layouts  159 us (17%)
  Pallas kernels  143 us (16%)
  starting transfers between devices  57.9 us (6%)
  other arithmetic  15.6 us (2%)
    ppermute x35, waiting for transfers between devices, swapped(): lax.ppermute(x, 'env', [(i, i ^ d) for i in range(lax.axis_size('env'))])  464 us
    unnamed x109, local copies, waits for them, and re-layouts  115 us
    ppermute x4, waiting for transfers between devices, passed_along(): return lax.ppermute(x, axis, [(i, (i + by) % size) for i in range(size)])  68.1 us
    ppermute x35, starting transfers between devices, swapped(): lax.ppermute(x, 'env', [(i, i ^ d) for i in range(lax.axis_size('env'))])  54 us
    pallas_call x3, Pallas kernels, half_chunk(): pl.pallas_call(kernel, grid_spec=pltpu.PrefetchScalarGridSpec(num_scalar_...  50.8 us
    pallas_call x8, Pallas kernels, edge_chunk(): pl.pallas_call(kernel, grid_spec=pltpu.PrefetchScalarGridSpec(num_scalar_...  37.5 us
    pallas_call x3, Pallas kernels, full_chunk(): pl.pallas_call(kernel, grid_spec=pltpu.PrefetchScalarGridSpec(num_scalar_...  27.7 us
    pallas_call x8, Pallas kernels, absorbed_chunk(): pl.pallas_call(kernel, grid_spec=pltpu.PrefetchScalarGridSpec(num_scalar_...  27 us
  transfers between devices with their start and end apart: 39, of which 21 were waited for; matrix products, arithmetic and copies ran while one was open for 5% of the time, Pallas kernels for 13%

profile of v1, /device:TPU:9, one launch (start us, length us, event | category | flops | bytes accessed | tf_op | source)
XLA Modules:
  0.0 908.5 jit_solution(4498409798920078982)
XLA Ops:
  0.7 22.4 %copy.33 = bf16[1,1,256,32768]{2,3,1,0:T(8,128)(2,1)} copy(bf16[1,1,256,32768]{3,2,1,0:T(8,128)(2,1)} %param.8) | data formatting | bytes 33554432 | tf_op args[2]
  48.2 10.4 %grad_full.4 = (bf16[12,256,256]{2,1,0:T(8,128)(2,1)S(1)}, bf16[12,256,256]{2,1,0:T(8,128)(2,1)S(1)}, bf16[12,256,256]{2,1,0:T(8,128)(2,1)}, bf16[12,256,256]{2,1,0:T(8,128)(2,1)}) custom-call(s32[1]{0:T(128)} %bitcast.4.me_ref, bf16[256,32768]{1,0:T(8,128)(2,1)S(1)} %bitcast.62, ...), custom_call_target="tpu_custom_call" | custom-call | flops 6442450944 | bytes 12582912 | tf_op jit(solution)/shard_map/grad_full/pallas_call | solution.py:68
  63.4 44.2 %collective-permute-done.2.refs_2_.refs_5_ = bf16[4,256,256]{2,1,0:T(8,128)(2,1)S(1)} collective-permute-done((bf16[4,256,256]{2,1,0:T(8,128)(2,1)S(1)}, bf16[4,256,256]{2,1,0:T(8,128)(2,1)S(1)}, u32[]{:S(2)}, u32[]{:S(2)}) %collective-permute-start.2) | collective-permute-done | bytes 524320 | tf_op jit(solution)/shard_map/ppermute | solution.py:28
  107.6 13.6 %grad_full.5 = (bf16[16,256,256]{2,1,0:T(8,128)(2,1)S(1)}, bf16[16,256,256]{2,1,0:T(8,128)(2,1)}, bf16[16,256,256]{2,1,0:T(8,128)(2,1)}, bf16[16,256,256]{2,1,0:T(8,128)(2,1)}) custom-call(s32[1]{0:T(128)} %bitcast.4.me_ref, bf16[256,32768]{1,0:T(8,128)(2,1)S(1)} %bitcast.63, ...), custom_call_target="tpu_custom_call" | custom-call | flops 8589934592 | bytes 16777216 | tf_op jit(solution)/shard_map/grad_full/pallas_call | solution.py:68
  123.8 12.4 %collective-permute-start.8 = (bf16[16,256,256]{2,1,0:T(8,128)(2,1)}, bf16[16,256,256]{2,1,0:T(8,128)(2,1)}, u32[]{:S(2)}, u32[]{:S(2)}) collective-permute-start(bf16[16,256,256]{2,1,0:T(8,128)(2,1)} %get-tuple-element.69), channel_id=1, source_target_pairs={{0,1},{1,0},{2,3},{3,2},{4,5},{5,4},{6,7},{7,6},{8,9},{9,8},{10,11... | collective-permute-start | bytes 6291464 | tf_op jit(solution)/shard_map/ppermute | solution.py:28
  138.3 68.1 %collective-permute-done = bf16[256,32768]{0,1:T(8,128)(2,1)} collective-permute-done((bf16[256,32768]{0,1:T(8,128)(2,1)}, bf16[256,32768]{0,1:T(8,128)(2,1)}, u32[]{:S(2)}, u32[]{:S(2)}) %collective-permute-start) | collective-permute-done | bytes 16777248 | tf_op jit(solution)/shard_map/ppermute | solution.py:24
  213.6 15.8 %copy.55 = bf16[1024,32,256]{2,0,1:T(8,128)(2,1)} copy(bf16[1024,32,256]{2,1,0:T(8,128)(2,1)} %bitcast.7) | data formatting | bytes 33554432 | tf_op jit(solution)/shard_map/reshape | solution.py:256
  229.4 7.6 grad_half.3
  239.0 106.5 %collective-permute-done.7.refs_3_.refs_6_ = bf16[12,256,256]{2,1,0:T(8,128)(2,1)} collective-permute-done((bf16[12,256,256]{2,1,0:T(8,128)(2,1)}, bf16[12,256,256]{2,1,0:T(8,128)(2,1)}, u32[]{:S(2)}, u32[]{:S(2)}) %collective-permute-start.7) | collective-permute-done | bytes 1572896 | tf_op jit(solution)/shard_map/ppermute | solution.py:28
  345.5 17.9 %grad_half.4 = (bf16[32,1024,256]{2,1,0:T(8,128)(2,1)}, f32[1024,1024]{1,0:T(8,128)S(1)}, f32[8,256]{1,0:T(8,128)S(1)}) custom-call(s32[1]{0:T(128)} %bitcast.4.me_ref, bf16[32,1024,256]{2,1,0:T(8,128)(2,1)} %bitcast.51, bf16[12,256,256]{2,1,0:T(8,128)(2,1)S(1)} %copy-done.23, ...), custom_call_target="tpu_custom_call", output_to_operand_aliasing={{0}: (10, {})} | custom-call | flops 12884901888 | bytes 18874368 | tf_op jit(solution)/shard_map/grad_half/pallas_call | solution.py:146
  365.4 21.9 %collective-permute-done.9.refs_2_.refs_5_ = bf16[16,256,256]{2,1,0:T(8,128)(2,1)} collective-permute-done((bf16[16,256,256]{2,1,0:T(8,128)(2,1)}, bf16[16,256,256]{2,1,0:T(8,128)(2,1)}, u32[]{:S(2)}, u32[]{:S(2)}) %collective-permute-start.9) | collective-permute-done | bytes 2097184 | tf_op jit(solution)/shard_map/ppermute | solution.py:28
  387.3 48.1 %collective-permute-done.10.refs_3_.refs_6_ = bf16[16,256,256]{2,1,0:T(8,128)(2,1)} collective-permute-done((bf16[16,256,256]{2,1,0:T(8,128)(2,1)}, bf16[16,256,256]{2,1,0:T(8,128)(2,1)}, u32[]{:S(2)}, u32[]{:S(2)}) %collective-permute-start.10) | collective-permute-done | bytes 2097184 | tf_op jit(solution)/shard_map/ppermute | solution.py:28
  435.4 25.2 %grad_half.5 = (bf16[32,1024,256]{2,1,0:T(8,128)(2,1)}, f32[1024,1024]{1,0:T(8,128)}, f32[8,256]{1,0:T(8,128)S(1)}) custom-call(s32[1]{0:T(128)} %bitcast.4.me_ref, bf16[32,1024,256]{2,1,0:T(8,128)(2,1)} %bitcast.52, bf16[16,256,256]{2,1,0:T(8,128)(2,1)S(1)} %copy-done.45, ...), custom_call_target="tpu_custom_call", output_to_operand_aliasing={{0}: (10, {})} | custom-call | flops 17179869184 | bytes 25165824 | tf_op jit(solution)/shard_map/grad_half/pallas_call | solution.py:146
  460.6 17.9 %copy.50 = bf16[1024,32,256]{2,1,0:T(8,128)(2,1)} copy(bf16[1024,32,256]{2,0,1:T(8,128)(2,1)} %bitcast.65) | data formatting | bytes 33554432 | tf_op jit(solution)/shard_map/transpose | solution.py:278
  507.0 27.9 %collective-permute-done.26.refs_4_.refs_1_ = bf16[4,256,256]{2,1,0:T(8,128)(2,1)S(1)} collective-permute-done((bf16[4,256,256]{2,1,0:T(8,128)(2,1)S(1)}, bf16[4,256,256]{2,1,0:T(8,128)(2,1)S(1)}, u32[]{:S(2)}, u32[]{:S(2)}) %collective-permute-start.26) | collective-permute-done | bytes 524320 | tf_op jit(solution)/shard_map/ppermute | solution.py:28
  541.9 40.1 %collective-permute-done.28.refs_6_.refs_3_ = bf16[4,256,256]{2,1,0:T(8,128)(2,1)} collective-permute-done((bf16[4,256,256]{2,1,0:T(8,128)(2,1)}, bf16[4,256,256]{2,1,0:T(8,128)(2,1)}, u32[]{:S(2)}, u32[]{:S(2)}) %collective-permute-start.28) | collective-permute-done | bytes 524320 | tf_op jit(solution)/shard_map/ppermute | solution.py:28
  601.3 14.4 %collective-permute-done.16.refs_6_.refs_3_ = bf16[6,256,256]{2,1,0:T(8,128)(2,1)} collective-permute-done((bf16[6,256,256]{2,1,0:T(8,128)(2,1)}, bf16[6,256,256]{2,1,0:T(8,128)(2,1)}, u32[]{:S(2)}, u32[]{:S(2)}) %collective-permute-start.16) | collective-permute-done | bytes 786464 | tf_op jit(solution)/shard_map/ppermute | solution.py:28
  634.0 36.5 %collective-permute-done.29.refs_4_.refs_1_ = bf16[6,256,256]{2,1,0:T(8,128)(2,1)} collective-permute-done((bf16[6,256,256]{2,1,0:T(8,128)(2,1)}, bf16[6,256,256]{2,1,0:T(8,128)(2,1)}, u32[]{:S(2)}, u32[]{:S(2)}) %collective-permute-start.29) | collective-permute-done | bytes 786464 | tf_op jit(solution)/shard_map/ppermute | solution.py:28
  674.0 42.6 %collective-permute-done.31.refs_6_.refs_3_ = bf16[6,256,256]{2,1,0:T(8,128)(2,1)} collective-permute-done((bf16[6,256,256]{2,1,0:T(8,128)(2,1)}, bf16[6,256,256]{2,1,0:T(8,128)(2,1)}, u32[]{:S(2)}, u32[]{:S(2)}) %collective-permute-start.31) | collective-permute-done | bytes 786464 | tf_op jit(solution)/shard_map/ppermute | solution.py:28
  747.4 36.6 %collective-permute-done.19.refs_6_.refs_3_ = bf16[6,256,256]{2,1,0:T(8,128)(2,1)S(1)} collective-permute-done((bf16[6,256,256]{2,1,0:T(8,128)(2,1)S(1)}, bf16[6,256,256]{2,1,0:T(8,128)(2,1)S(1)}, u32[]{:S(2)}, u32[]{:S(2)}) %collective-permute-start.19) | collective-permute-done | bytes 786464 | tf_op jit(solution)/shard_map/ppermute | solution.py:28
  798.0 7.2 grad_edge.10.refs_8_
  806.4 8.0 collective-permute-done.33.refs_5_.refs_2_
  814.7 19.9 %collective-permute-done.34.refs_6_.refs_3_ = bf16[4,256,256]{2,1,0:T(8,128)(2,1)S(1)} collective-permute-done((bf16[4,256,256]{2,1,0:T(8,128)(2,1)S(1)}, bf16[4,256,256]{2,1,0:T(8,128)(2,1)S(1)}, u32[]{:S(2)}, u32[]{:S(2)}) %collective-permute-start.34) | collective-permute-done | bytes 524320 | tf_op jit(solution)/shard_map/ppermute | solution.py:28
  887.3 21.2 %copy.52 = bf16[1,1,256,32768]{3,2,1,0:T(8,128)(2,1)} copy(bf16[1,1,256,32768]{2,3,1,0:T(8,128)(2,1)} %bitcast.27) | data formatting | bytes 33554432
  (206 shorter events, 221.1 us)
Async XLA Ops:
  23.0 183.4 %collective-permute-start = (bf16[256,32768]{0,1:T(8,128)(2,1)}, bf16[256,32768]{0,1:T(8,128)(2,1)}, u32[]{:S(2)}, u32[]{:S(2)}) collective-permute-start(bf16[256,32768]{0,1:T(8,128)(2,1)} %bitcast.66), channel_id=1, source_target_pairs={{0,24},{8,0},{16,8},{24,16},{1,25},{9,1},{17,9},{25,17},{2,26},{10... | collective-permute-start | bytes 50331656 | tf_op jit(solution)/shard_map/ppermute | solution.py:24
  41.0 95.2 %collective-permute-start.4 = (bf16[1024,1024]{0,1:T(8,128)(2,1)}, bf16[1024,1024]{0,1:T(8,128)(2,1)S(1)}, u32[]{:S(2)}, u32[]{:S(2)}) collective-permute-start(bf16[1024,1024]{0,1:T(8,128)(2,1)} %bitcast.69), channel_id=1, source_target_pairs={{0,4},{4,0},{1,5},{5,1},{2,6},{6,2},{3,7},{7,3},{8,12},{12,8},{9,1... | collective-permute-start | bytes 6291464 | tf_op jit(solution)/shard_map/ppermute | solution.py:24
  59.7 62.9 %collective-permute-start.5 = (bf16[12,256,256]{2,1,0:T(8,128)(2,1)S(1)}, bf16[12,256,256]{2,1,0:T(8,128)(2,1)S(1)}, u32[]{:S(2)}, u32[]{:S(2)}) collective-permute-start(bf16[12,256,256]{2,1,0:T(8,128)(2,1)S(1)} %get-tuple-element.63), channel_id=1, source_target_pairs={{0,1},{1,0},{2,3},{3,2},{4,5},{5,4},{6,7},{7,6},{8,9},{9,8},{10,11... | collective-permute-start | bytes 4718600 | tf_op jit(solution)/shard_map/ppermute | solution.py:28
  107.5 131.5 %collective-permute-start.6 = (bf16[12,256,256]{2,1,0:T(8,128)(2,1)}, bf16[12,256,256]{2,1,0:T(8,128)(2,1)}, u32[]{:S(2)}, u32[]{:S(2)}) collective-permute-start(bf16[12,256,256]{2,1,0:T(8,128)(2,1)} %get-tuple-element.64), channel_id=1, source_target_pairs={{0,2},{1,3},{2,0},{3,1},{4,6},{5,7},{6,4},{7,5},{8,10},{9,11},{10,... | collective-permute-start | bytes 4718600 | tf_op jit(solution)/shard_map/ppermute | solution.py:28
  107.5 238.0 %collective-permute-start.7 = (bf16[12,256,256]{2,1,0:T(8,128)(2,1)}, bf16[12,256,256]{2,1,0:T(8,128)(2,1)}, u32[]{:S(2)}, u32[]{:S(2)}) collective-permute-start(bf16[12,256,256]{2,1,0:T(8,128)(2,1)} %get-tuple-element.65), channel_id=1, source_target_pairs={{0,3},{1,2},{2,1},{3,0},{4,7},{5,6},{6,5},{7,4},{8,11},{9,10},{10,... | collective-permute-start | bytes 4718600 | tf_op jit(solution)/shard_map/ppermute | solution.py:28
  123.8 241.6 %collective-permute-start.8 = (bf16[16,256,256]{2,1,0:T(8,128)(2,1)}, bf16[16,256,256]{2,1,0:T(8,128)(2,1)}, u32[]{:S(2)}, u32[]{:S(2)}) collective-permute-start(bf16[16,256,256]{2,1,0:T(8,128)(2,1)} %get-tuple-element.69), channel_id=1, source_target_pairs={{0,1},{1,0},{2,3},{3,2},{4,5},{5,4},{6,7},{7,6},{8,9},{9,8},{10,11... | collective-permute-start | bytes 6291464 | tf_op jit(solution)/shard_map/ppermute | solution.py:28
  136.2 251.1 %collective-permute-start.9 = (bf16[16,256,256]{2,1,0:T(8,128)(2,1)}, bf16[16,256,256]{2,1,0:T(8,128)(2,1)}, u32[]{:S(2)}, u32[]{:S(2)}) collective-permute-start(bf16[16,256,256]{2,1,0:T(8,128)(2,1)} %get-tuple-element.70), channel_id=1, source_target_pairs={{0,2},{1,3},{2,0},{3,1},{4,6},{5,7},{6,4},{7,5},{8,10},{9,11},{10,... | collective-permute-start | bytes 6291464 | tf_op jit(solution)/shard_map/ppermute | solution.py:28
  206.4 229.0 %collective-permute-start.10 = (bf16[16,256,256]{2,1,0:T(8,128)(2,1)}, bf16[16,256,256]{2,1,0:T(8,128)(2,1)}, u32[]{:S(2)}, u32[]{:S(2)}) collective-permute-start(bf16[16,256,256]{2,1,0:T(8,128)(2,1)} %get-tuple-element.71), channel_id=1, source_target_pairs={{0,3},{1,2},{2,1},{3,0},{4,7},{5,6},{6,5},{7,4},{8,11},{9,10},{10,... | collective-permute-start | bytes 6291464 | tf_op jit(solution)/shard_map/ppermute | solution.py:28
  478.5 408.8 %collective-permute-start.38 = (bf16[256,32768]{0,1:T(8,128)(2,1)}, bf16[256,32768]{0,1:T(8,128)(2,1)}, u32[]{:S(2)}, u32[]{:S(2)}) collective-permute-start(bf16[256,32768]{0,1:T(8,128)(2,1)} %bitcast.26), channel_id=1, source_target_pairs={{0,8},{8,16},{16,24},{24,0},{1,9},{9,17},{17,25},{25,1},{2,10},{10... | collective-permute-start | bytes 50331656 | tf_op jit(solution)/shard_map/ppermute | solution.py:24
  495.6 101.3 %collective-permute-start.14 = (bf16[6,256,256]{2,1,0:T(8,128)(2,1)}, bf16[6,256,256]{2,1,0:T(8,128)(2,1)S(1)}, u32[]{:S(2)}, u32[]{:S(2)}) collective-permute-start(bf16[6,256,256]{2,1,0:T(8,128)(2,1)} %get-tuple-element.74), channel_id=1, source_target_pairs={{0,1},{1,0},{2,3},{3,2},{4,5},{5,4},{6,7},{7,6},{8,9},{9,8},{10,11... | collective-permute-start | bytes 2359304 | tf_op jit(solution)/shard_map/ppermute | solution.py:28
  500.7 81.3 %collective-permute-start.28 = (bf16[4,256,256]{2,1,0:T(8,128)(2,1)}, bf16[4,256,256]{2,1,0:T(8,128)(2,1)}, u32[]{:S(2)}, u32[]{:S(2)}) collective-permute-start(bf16[4,256,256]{2,1,0:T(8,128)(2,1)} %get-tuple-element.89), channel_id=1, source_target_pairs={{0,3},{1,2},{2,1},{3,0},{4,7},{5,6},{6,5},{7,4},{8,11},{9,10},{10,... | collective-permute-start | bytes 1572872 | tf_op jit(solution)/shard_map/ppermute | solution.py:28
  534.9 63.5 %collective-permute-start.15 = (bf16[6,256,256]{2,1,0:T(8,128)(2,1)}, bf16[6,256,256]{2,1,0:T(8,128)(2,1)}, u32[]{:S(2)}, u32[]{:S(2)}) collective-permute-start(bf16[6,256,256]{2,1,0:T(8,128)(2,1)} %get-tuple-element.75), channel_id=1, source_target_pairs={{0,2},{1,3},{2,0},{3,1},{4,6},{5,7},{6,4},{7,5},{8,10},{9,11},{10,... | collective-permute-start | bytes 2359304 | tf_op jit(solution)/shard_map/ppermute | solution.py:28
  537.3 78.4 %collective-permute-start.16 = (bf16[6,256,256]{2,1,0:T(8,128)(2,1)}, bf16[6,256,256]{2,1,0:T(8,128)(2,1)}, u32[]{:S(2)}, u32[]{:S(2)}) collective-permute-start(bf16[6,256,256]{2,1,0:T(8,128)(2,1)} %get-tuple-element.76), channel_id=1, source_target_pairs={{0,3},{1,2},{2,1},{3,0},{4,7},{5,6},{6,5},{7,4},{8,11},{9,10},{10,... | collective-permute-start | bytes 2359304 | tf_op jit(solution)/shard_map/ppermute | solution.py:28
  596.9 73.6 %collective-permute-start.29 = (bf16[6,256,256]{2,1,0:T(8,128)(2,1)}, bf16[6,256,256]{2,1,0:T(8,128)(2,1)}, u32[]{:S(2)}, u32[]{:S(2)}) collective-permute-start(bf16[6,256,256]{2,1,0:T(8,128)(2,1)} %get-tuple-element.90), channel_id=1, source_target_pairs={{0,1},{1,0},{2,3},{3,2},{4,5},{5,4},{6,7},{7,6},{8,9},{9,8},{10,11... | collective-permute-start | bytes 2359304 | tf_op jit(solution)/shard_map/ppermute | solution.py:28
  598.4 72.8 %collective-permute-start.30 = (bf16[6,256,256]{2,1,0:T(8,128)(2,1)}, bf16[6,256,256]{2,1,0:T(8,128)(2,1)}, u32[]{:S(2)}, u32[]{:S(2)}) collective-permute-start(bf16[6,256,256]{2,1,0:T(8,128)(2,1)} %get-tuple-element.91), channel_id=1, source_target_pairs={{0,2},{1,3},{2,0},{3,1},{4,6},{5,7},{6,4},{7,5},{8,10},{9,11},{10,... | collective-permute-start | bytes 2359304 | tf_op jit(solution)/shard_map/ppermute | solution.py:28
  615.7 100.9 %collective-permute-start.31 = (bf16[6,256,256]{2,1,0:T(8,128)(2,1)}, bf16[6,256,256]{2,1,0:T(8,128)(2,1)}, u32[]{:S(2)}, u32[]{:S(2)}) collective-permute-start(bf16[6,256,256]{2,1,0:T(8,128)(2,1)} %get-tuple-element.92), channel_id=1, source_target_pairs={{0,3},{1,2},{2,1},{3,0},{4,7},{5,6},{6,5},{7,4},{8,11},{9,10},{10,... | collective-permute-start | bytes 2359304 | tf_op jit(solution)/shard_map/ppermute | solution.py:28
  625.2 100.1 %collective-permute-start.17 = (bf16[6,256,256]{2,1,0:T(8,128)(2,1)}, bf16[6,256,256]{2,1,0:T(8,128)(2,1)}, u32[]{:S(2)}, u32[]{:S(2)}) collective-permute-start(bf16[6,256,256]{2,1,0:T(8,128)(2,1)} %get-tuple-element.77), channel_id=1, source_target_pairs={{0,1},{1,0},{2,3},{3,2},{4,5},{5,4},{6,7},{7,6},{8,9},{9,8},{10,11... | collective-permute-start | bytes 2359304 | tf_op jit(solution)/shard_map/ppermute | solution.py:28
  670.5 73.7 %collective-permute-start.18 = (bf16[6,256,256]{2,1,0:T(8,128)(2,1)S(1)}, bf16[6,256,256]{2,1,0:T(8,128)(2,1)S(1)}, u32[]{:S(2)}, u32[]{:S(2)}) collective-permute-start(bf16[6,256,256]{2,1,0:T(8,128)(2,1)S(1)} %copy-done.39), channel_id=1, source_target_pairs={{0,2},{1,3},{2,0},{3,1},{4,6},{5,7},{6,4},{7,5},{8,10},{9,11},{10,... | collective-permute-start | bytes 2359304 | tf_op jit(solution)/shard_map/ppermute | solution.py:28
  671.2 112.8 %collective-permute-start.19 = (bf16[6,256,256]{2,1,0:T(8,128)(2,1)S(1)}, bf16[6,256,256]{2,1,0:T(8,128)(2,1)S(1)}, u32[]{:S(2)}, u32[]{:S(2)}) collective-permute-start(bf16[6,256,256]{2,1,0:T(8,128)(2,1)S(1)} %copy-done.37), channel_id=1, source_target_pairs={{0,3},{1,2},{2,1},{3,0},{4,7},{5,6},{6,5},{7,4},{8,11},{9,10},{10,... | collective-permute-start | bytes 2359304 | tf_op jit(solution)/shard_map/ppermute | solution.py:28
  716.6 78.2 %collective-permute-start.12 = (bf16[1,256,1024]{1,2,0:T(8,128)(2,1)S(1)}, bf16[1,256,1024]{1,2,0:T(8,128)(2,1)S(1)}, u32[]{:S(2)}, u32[]{:S(2)}) collective-permute-start(bf16[1,256,1024]{1,2,0:T(8,128)(2,1)S(1)} %dynamic-slice_convert_fusion), channel_id=1, source_target_pairs={{0,2},{1,3},{2,0},{3,1},{4,6},{5,7},{6,4},{7,5},{8,10},{9,11},{10,... | collective-permute-start | bytes 1572872 | tf_op jit(solution)/shard_map/ppermute | solution.py:28
  725.3 71.4 %collective-permute-start.32 = (bf16[4,256,256]{2,1,0:T(8,128)(2,1)S(1)}, bf16[4,256,256]{2,1,0:T(8,128)(2,1)S(1)}, u32[]{:S(2)}, u32[]{:S(2)}) collective-permute-start(bf16[4,256,256]{2,1,0:T(8,128)(2,1)S(1)} %get-tuple-element.93), channel_id=1, source_target_pairs={{0,1},{1,0},{2,3},{3,2},{4,5},{5,4},{6,7},{7,6},{8,9},{9,8},{10,11... | collective-permute-start | bytes 1572872 | tf_op jit(solution)/shard_map/ppermute | solution.py:28
  744.3 70.1 %collective-permute-start.33 = (bf16[4,256,256]{2,1,0:T(8,128)(2,1)S(1)}, bf16[4,256,256]{2,1,0:T(8,128)(2,1)S(1)}, u32[]{:S(2)}, u32[]{:S(2)}) collective-permute-start(bf16[4,256,256]{2,1,0:T(8,128)(2,1)S(1)} %get-tuple-element.94), channel_id=1, source_target_pairs={{0,2},{1,3},{2,0},{3,1},{4,6},{5,7},{6,4},{7,5},{8,10},{9,11},{10,... | collective-permute-start | bytes 1572872 | tf_op jit(solution)/shard_map/ppermute | solution.py:28
  784.0 50.6 %collective-permute-start.34 = (bf16[4,256,256]{2,1,0:T(8,128)(2,1)S(1)}, bf16[4,256,256]{2,1,0:T(8,128)(2,1)S(1)}, u32[]{:S(2)}, u32[]{:S(2)}) collective-permute-start(bf16[4,256,256]{2,1,0:T(8,128)(2,1)S(1)} %get-tuple-element.95), channel_id=1, source_target_pairs={{0,3},{1,2},{2,1},{3,0},{4,7},{5,6},{6,5},{7,4},{8,11},{9,10},{10,... | collective-permute-start | bytes 1572872 | tf_op jit(solution)/shard_map/ppermute | solution.py:28
  814.4 50.4 %collective-permute-start.13 = (bf16[256,1024]{0,1:T(8,128)(2,1)S(1)}, bf16[256,1024]{0,1:T(8,128)(2,1)S(1)}, u32[]{:S(2)}, u32[]{:S(2)}) collective-permute-start(bf16[256,1024]{0,1:T(8,128)(2,1)S(1)} %fusion.2), channel_id=1, source_target_pairs={{0,4},{4,0},{1,5},{5,1},{2,6},{6,2},{3,7},{7,3},{8,12},{12,8},{9,1... | collective-permute-start | bytes 1572872 | tf_op jit(solution)/shard_map/ppermute | solution.py:24
  (67 other events, 1441.6 us)

commit v2 on v1

v2 whole, which is shorter than its diff:
```python
import functools

import jax
import jax.numpy as jnp
from jax import lax
from jax.experimental import pallas as pl
from jax.experimental.layout import Layout, with_layout_constraint
from jax.experimental.pallas import tpu as pltpu
from jax.sharding import PartitionSpec as P

CHI = 1024
HALF = 32
BLK = 128

FULL_CHUNKS = (4, 28)
EDGE_CHUNKS = (9, 9, 6, 4, 3, 1)
ENV = 4

MIB = 1 << 20
VMEM_MIB = 56
COST_BITS = 20
HELD_BACK = {1: 0}
ORDER = "F0 F1 f C T A0 A1 a H0 H1 R1 A2 E0 A3 M E1 R2 A4 E2 R3 A5 E3 R4 E4 E5"
F32 = jnp.float32
BF16 = jnp.bfloat16


def passed_along(x, axis, by):
    size = lax.axis_size(axis)
    return lax.ppermute(x, axis, [(i, (i + by) % size) for i in range(size)])


def swapped(x, d, rows_on=0):
    n_row, n_env = lax.axis_size("row"), lax.axis_size("env")
    if not rows_on:
        return lax.ppermute(x, "env", [(i, i ^ d) for i in range(n_env)])
    pairs = [
        (r * n_env + i, (r + rows_on) % n_row * n_env + (i ^ d))
        for r in range(n_row) for i in range(n_env)
    ]
    return lax.ppermute(x, ("row", "env"), pairs)


def corner_moved(x, by):
    n_row, n_col = lax.axis_size("row"), lax.axis_size("col")
    pairs = [
        (r * n_col + c, (r + by) % n_row * n_col + (c + by) % n_col)
        for r in range(n_row) for c in range(n_col)
    ]
    return lax.ppermute(x, ("row", "col"), pairs)


def nn(a, b):
    return jnp.dot(a, b, preferred_element_type=F32)


def nt(a, b):
    return lax.dot_general(a, b, (((1,), (1,)), ((), ())), preferred_element_type=F32)


ANYWHERE = pl.BlockSpec(memory_space=pl.ANY)


def params(dims=1):
    return pltpu.CompilerParams(
        vmem_limit_bytes=VMEM_MIB * MIB, dimension_semantics=("arbitrary",) * dims
    )


def cost(count):
    return pl.CostEstimate(
        flops=count << COST_BITS, bytes_accessed=count << (COST_BITS - 8), transcendentals=0
    )


def row_major(x):
    return with_layout_constraint(x, Layout(tuple(range(x.ndim))))


def full_chunk(me, top_edge, grad_new, ds, first, count, after):
    rows = top_edge.shape[0]
    n_out = len(ds)

    def kernel(me_ref, t_ref, *refs):
        g_refs, outs = refs[:n_out], refs[-n_out:]
        t = t_ref[...]
        for g_ref, out in zip(g_refs, outs):
            out[0] = nt(t, g_ref[...]).astype(BF16)

    def grad_spec(d):
        return pl.BlockSpec((rows, CHI), lambda k, me: (me[0] ^ d, 0))

    return pl.pallas_call(
        kernel,
        grid_spec=pltpu.PrefetchScalarGridSpec(
            num_scalar_prefetch=1,
            grid=(count,),
            in_specs=[pl.BlockSpec((rows, CHI), lambda k, me: (0, first + k))]
            + [grad_spec(d) for d in ds] + [ANYWHERE] * len(after),
            out_specs=[pl.BlockSpec((1, rows, rows), lambda k, me: (k, 0, 0))] * n_out,
        ),
        out_shape=[jax.ShapeDtypeStruct((count, rows, rows), BF16)] * n_out,
        compiler_params=params(),
        cost_estimate=cost(count),
        name="grad_full",
    )(me, top_edge, *[grad_new] * n_out, *after)


GROUP = 64


def k_major(x, after):
    rows = x.shape[0]

    def kernel(x_ref, *refs):
        turned = x_ref[...].T.reshape(GROUP, HALF, rows)
        refs[-1][...] = jnp.transpose(turned, (1, 0, 2))

    return pl.pallas_call(
        kernel,
        grid=(CHI // GROUP,),
        in_specs=[pl.BlockSpec((rows, GROUP * HALF), lambda j: (0, j))] + [ANYWHERE] * len(after),
        out_specs=pl.BlockSpec((HALF, GROUP, rows), lambda j: (0, j, 0)),
        out_shape=jax.ShapeDtypeStruct((HALF, CHI, rows), BF16),
        compiler_params=params(),
        cost_estimate=cost(1),
        name="k_major",
    )(x, *after)


def k_minor(parts, after):
    rows = parts[0].shape[2]
    n_parts = len(parts)

    def kernel(*refs):
        whole = jnp.concatenate([ref[...] for ref in refs[:n_parts]], axis=0)
        refs[-1][...] = jnp.transpose(whole, (1, 0, 2)).reshape(GROUP * HALF, rows).T

    return pl.pallas_call(
        kernel,
        grid=(CHI // GROUP,),
        in_specs=[pl.BlockSpec((x.shape[0], GROUP, rows), lambda j: (0, j, 0)) for x in parts]
        + [ANYWHERE] * len(after),
        out_specs=pl.BlockSpec((rows, GROUP * HALF), lambda j: (0, j)),
        out_shape=jax.ShapeDtypeStruct((rows, CHI * HALF), BF16),
        compiler_params=params(),
        cost_estimate=cost(1),
        name="k_minor",
    )(*parts, *after)


def held_back(arrays, after):
    n_arrays = len(arrays)
    return pl.pallas_call(
        lambda *refs: None,
        in_specs=[ANYWHERE] * (n_arrays + len(after)),
        out_specs=[ANYWHERE] * n_arrays,
        out_shape=[jax.ShapeDtypeStruct(x.shape, x.dtype) for x in arrays],
        input_output_aliases={j: j for j in range(n_arrays)},
        compiler_params=pltpu.CompilerParams(vmem_limit_bytes=VMEM_MIB * MIB),
        cost_estimate=cost(1),
        name="held_back",
    )(*arrays, *after)


def absorbed_chunk(me, lower, corner_t, ds, first, count, after):
    rows = lower.shape[2]
    n_out = len(ds)

    def kernel(me_ref, l_ref, *refs):
        c_refs, outs = refs[:n_out], refs[-n_out:]
        low = l_ref[0]
        for c_ref, out in zip(c_refs, outs):
            out[0] = nn(c_ref[...], low).astype(BF16)

    def corner_spec(d):
        return pl.BlockSpec((rows, CHI), lambda k, me: (me[0] ^ d, 0))

    return pl.pallas_call(
        kernel,
        grid_spec=pltpu.PrefetchScalarGridSpec(
            num_scalar_prefetch=1,
            grid=(count,),
            in_specs=[pl.BlockSpec((1, CHI, rows), lambda k, me: (first + k, 0, 0))]
            + [corner_spec(d) for d in ds] + [ANYWHERE] * len(after),
            out_specs=[pl.BlockSpec((1, rows, rows), lambda k, me: (k, 0, 0))] * n_out,
        ),
        out_shape=[jax.ShapeDtypeStruct((count, rows, rows), BF16)] * n_out,
        compiler_params=params(),
        cost_estimate=cost(count),
        name="absorbed",
    )(me, lower, *[corner_t] * n_out, *after)


def half_chunk(me, blocks, lower, corner, held, first, count, after):
    rows = lower.shape[2]
    n = CHI // rows
    step = 2
    n_held = 0 if held is None else 2

    def kernel(me_ref, l_ref, *refs):
        f_refs, c_refs = refs[:n], refs[n:2 * n]
        half_ref, corner_ref, pair_ref = refs[-3:]

        @pl.when(pl.program_id(0) == 0)
        def _():
            if n_held:
                corner_ref[...] = refs[-5][...]
                pair_ref[...] = refs[-4][...]
            else:
                corner_ref[...] = jnp.zeros_like(corner_ref)
                pair_ref[...] = jnp.zeros_like(pair_ref)

        for j in range(step):
            total = nn(c_refs[0][...], f_refs[0][j])
            for d in range(1, n):
                total += nn(c_refs[d][...], f_refs[d][j])
            half_ref[j] = total.astype(BF16)
            part = total * l_ref[j].astype(F32)
            pair_ref[...] += jnp.sum(part.reshape(CHI // 8, 8, rows), axis=0)
        low = jnp.concatenate([l_ref[j] for j in range(step)], axis=1)
        for d in range(n):
            full = jnp.concatenate([f_refs[d][j] for j in range(step)], axis=1)
            place = pl.ds(pl.multiple_of((me_ref[0] ^ d) * rows, rows), rows)
            corner_ref[:, place] += nt(low, full)

    def corner_spec(d):
        return pl.BlockSpec((CHI, rows), lambda k, me: (0, me[0] ^ d))

    def block_spec(offset):
        return pl.BlockSpec((step, rows, rows), lambda k, me: (offset // step + k, 0, 0))

    corner_sum = pl.BlockSpec((CHI, CHI), lambda k, me: (0, 0))
    pair_sum = pl.BlockSpec((8, rows), lambda k, me: (0, 0))
    operands = [me, lower, *[x for x, _ in blocks], *[corner] * n, *after]
    operands += held if n_held else []
    return pl.pallas_call(
        kernel,
        grid_spec=pltpu.PrefetchScalarGridSpec(
            num_scalar_prefetch=1,
            grid=(count // step,),
            in_specs=[pl.BlockSpec((step, CHI, rows), lambda k, me: (first // step + k, 0, 0))]
            + [block_spec(offset) for _, offset in blocks]
            + [corner_spec(d) for d in range(n)] + [ANYWHERE] * len(after)
            + [corner_sum, pair_sum][:n_held],
            out_specs=[
                pl.BlockSpec((step, CHI, rows), lambda k, me: (k, 0, 0)),
                corner_sum,
                pair_sum,
            ],
        ),
        out_shape=[
            jax.ShapeDtypeStruct((count, CHI, rows), BF16),
            jax.ShapeDtypeStruct((CHI, CHI), F32),
            jax.ShapeDtypeStruct((8, rows), F32),
        ],
        compiler_params=params(),
        cost_estimate=cost(2 * count),
        name="grad_half",
    )(*operands)


def edge_chunk(me, blocks, grad_new, held, first, count, after):
    rows = blocks[0][0].shape[1]
    n = CHI // rows
    has_held = held is not None

    def kernel(me_ref, *refs):
        a_refs, g_refs, out = refs[:n], refs[n:2 * n], refs[-1]
        total = nn(a_refs[0][0], g_refs[0][...])
        for d in range(1, n):
            total += nn(a_refs[d][0], g_refs[d][...])
        out[...] = total.astype(BF16)

    def grad_spec(d):
        return pl.BlockSpec((rows, CHI), lambda k, me: (me[0] ^ d, 0))

    def block_spec(offset):
        return pl.BlockSpec((1, rows, rows), lambda k, me: (offset + k, 0, 0))

    operands = [me, *[x for x, _ in blocks], *[grad_new] * n, *after]
    operands += [held] if has_held else []
    return pl.pallas_call(
        kernel,
        grid_spec=pltpu.PrefetchScalarGridSpec(
            num_scalar_prefetch=1,
            grid=(count,),
            in_specs=[block_spec(offset) for _, offset in blocks]
            + [grad_spec(d) for d in range(n)] + [ANYWHERE] * (len(after) + has_held),
            out_specs=pl.BlockSpec((rows, CHI), lambda k, me: (0, first + k)),
        ),
        out_shape=jax.ShapeDtypeStruct((rows, HALF * CHI), BF16),
        input_output_aliases={len(operands) - 1: 0} if has_held else {},
        compiler_params=params(),
        cost_estimate=cost(count),
        name="grad_edge",
    )(*operands)


def exchanged(blocks):
    far_first = {d: swapped(blocks[d], d) for d in reversed(range(1, len(blocks)))}
    return [blocks[0]] + [far_first[d] for d in range(1, len(blocks))]


def same_charge(rows_ref, columns_ref, x):
    return jnp.where(rows_ref[...] == columns_ref[...], x, 0.0)


def masked_corner(corner, row_charge, column_charge, after):
    rows = CHI // ENV

    def kernel(x_ref, r_ref, c_ref, *refs):
        masked = same_charge(r_ref, c_ref, x_ref[...].astype(F32)).astype(BF16)
        refs[-2][...] = masked
        refs[-1][...] = masked.T

    return pl.pallas_call(
        kernel,
        grid=(ENV,),
        in_specs=[
            pl.BlockSpec((rows, CHI), lambda j: (j, 0)),
            pl.BlockSpec((rows, 1), lambda j: (j, 0)),
            pl.BlockSpec((1, CHI), lambda j: (0, 0)),
        ] + [ANYWHERE] * len(after),
        out_specs=[
            pl.BlockSpec((rows, CHI), lambda j: (j, 0)),
            pl.BlockSpec((CHI, rows), lambda j: (0, j)),
        ],
        out_shape=[jax.ShapeDtypeStruct((CHI, CHI), BF16)] * 2,
        compiler_params=params(),
        cost_estimate=cost(1),
        name="near_corner",
    )(corner, row_charge, column_charge, *after)


def corner_halves(me, total, after):
    rows = CHI // ENV

    def kernel(me_ref, total_ref, *refs):
        refs[-1][0] = total_ref[...].astype(BF16)

    return pl.pallas_call(
        kernel,
        grid_spec=pltpu.PrefetchScalarGridSpec(
            num_scalar_prefetch=1,
            grid=(2,),
            in_specs=[pl.BlockSpec((rows, CHI), lambda h, me: (2 * h + 1 - me[0] % 2, 0))]
            + [ANYWHERE] * len(after),
            out_specs=pl.BlockSpec((1, rows, CHI), lambda h, me: (h, 0, 0)),
        ),
        out_shape=jax.ShapeDtypeStruct((2, rows, CHI), BF16),
        compiler_params=params(),
        cost_estimate=cost(1),
        name="corner_halves",
    )(me, total, *after)


def corner_quarter(me, total, halves, after):
    rows = CHI // ENV

    def kernel(me_ref, total_ref, half_ref, *refs):
        refs[-1][...] = (total_ref[...] + half_ref[0].astype(F32)).astype(BF16)

    return pl.pallas_call(
        kernel,
        grid_spec=pltpu.PrefetchScalarGridSpec(
            num_scalar_prefetch=1,
            grid=(1,),
            in_specs=[
                pl.BlockSpec((rows, CHI), lambda q, me: (me[0] ^ 2, 0)),
                pl.BlockSpec((1, rows, CHI), lambda q, me: ((me[0] ^ 2) // 2, 0, 0)),
            ] + [ANYWHERE] * len(after),
            out_specs=pl.BlockSpec((rows, CHI), lambda q, me: (0, 0)),
        ),
        out_shape=jax.ShapeDtypeStruct((rows, CHI), BF16),
        compiler_params=params(),
        cost_estimate=cost(1),
        name="corner_quarter",
    )(me, total, halves, *after)


def corner_rows(me, total, halves, quarter, charges, after):
    rows = CHI // ENV

    def kernel(me_ref, total_ref, half_ref, quarter_ref, r_ref, c_ref, *refs):
        whole = total_ref[...] + half_ref[0].astype(F32) + quarter_ref[...].astype(F32)
        refs[-1][...] = same_charge(r_ref, c_ref, whole).astype(BF16)

    return pl.pallas_call(
        kernel,
        grid_spec=pltpu.PrefetchScalarGridSpec(
            num_scalar_prefetch=1,
            grid=(1,),
            in_specs=[
                pl.BlockSpec((rows, CHI), lambda q, me: (me[0], 0)),
                pl.BlockSpec((1, rows, CHI), lambda q, me: (me[0] // 2, 0, 0)),
                pl.BlockSpec((rows, CHI), lambda q, me: (0, 0)),
                pl.BlockSpec((rows, 1), lambda q, me: (me[0], 0)),
                pl.BlockSpec((1, CHI), lambda q, me: (0, 0)),
            ] + [ANYWHERE] * len(after),
            out_specs=pl.BlockSpec((rows, CHI), lambda q, me: (0, 0)),
        ),
        out_shape=jax.ShapeDtypeStruct((rows, CHI), BF16),
        compiler_params=params(),
        cost_estimate=cost(1),
        name="grad_corner",
    )(me, total, halves, quarter, *charges, *after)


def charge_masks(parity):
    charges = jnp.repeat(parity, BLK, axis=1)
    corner_mask = charges[0][:, None] == charges[1][None, :]
    out_mask = charges[2][:, None] == charges[3][None, :]
    return corner_mask, out_mask


def spans(counts):
    return [(sum(counts[:j]), count) for j, count in enumerate(counts)]


def chunked_shards(corner, top_edge, half_system, values, cotangent, parity):
    rows = CHI // ENV
    me = lax.axis_index("env").astype(jnp.int32)
    me_arr = me.reshape(1)
    near_corner = row_major(corner_moved(row_major(corner[0, 0]), 1))
    above = jnp.repeat(passed_along(parity[0, 0], "row", 1), BLK, axis=1)
    row_charge, column_charge = above[0][:, None], above[1][None, :]
    _, out_mask = charge_masks(parity[0, 0])
    grad_new = jnp.where(
        out_mask, values[0, 0][:, None] ** (-0.5) * cotangent[0, 0].astype(F32), 0.0
    ).astype(BF16)
    top, half = top_edge[0, 0], half_system[0, 0]
    full_spans, edge_spans = spans(FULL_CHUNKS), spans(EDGE_CHUNKS)

    full_far, full_near, edge_far, edge_near, half_parts = {}, [], {}, [], []
    totals = halves = quarter = grad_corner = grad_edge = grad_half = None
    last = []
    for step in ORDER.split():
        what, j = step[0], int(step[1:] or 0)
        if what == "F":
            blocks = full_chunk(me_arr, top, grad_new, (3, 2), *full_spans[j], last)
            last = [blocks[0]]
            if j in HELD_BACK:
                blocks = held_back(blocks, full_far[HELD_BACK[j]])
                last = [blocks[0]]
            full_far[j] = [swapped(blocks[0], 3, 1), swapped(blocks[1], 2, 1)]
        elif what == "f":
            blocks = full_chunk(me_arr, top, grad_new, (0, 1), 0, HALF, last)
            last = [blocks[0]]
            full_near = [swapped(blocks[0], 0, 1), swapped(blocks[1], 1, 1)]
        elif what == "C":
            near_corner, corner_t = masked_corner(near_corner, row_charge, column_charge, last)
            last = [corner_t]
        elif what == "T":
            lower = k_major(half, last)
            last = [lower]
        elif what == "A":
            blocks = absorbed_chunk(me_arr, lower, corner_t, (3, 2), *edge_spans[j], last)
            last = [blocks[0]]
            edge_far[j] = [swapped(blocks[0], 3, -1), swapped(blocks[1], 2, -1)]
        elif what == "a":
            blocks = absorbed_chunk(me_arr, lower, corner_t, (0, 1), 0, HALF, last)
            last = [blocks[0]]
            edge_near = [swapped(blocks[0], 0, -1), swapped(blocks[1], 1, -1)]
        elif what == "H":
            first, count = full_spans[j]
            blocks = [(x, first) for x in full_near] + [(x, 0) for x in reversed(full_far[j])]
            part, *totals = half_chunk(
                me_arr, blocks, lower, near_corner, totals, first, count, last
            )
            last = [totals[1]]
            half_parts.append(part)
        elif what == "M":
            grad_half = k_minor(half_parts, last)
            last = [grad_half]
        elif what == "R" and j == 1:
            halves = corner_halves(me_arr, totals[0], last)
            last = [halves]
            halves = swapped(halves, 1)
        elif what == "R" and j == 2:
            quarter = corner_quarter(me_arr, totals[0], halves, last)
            last = [quarter]
            quarter = swapped(quarter, 2)
        elif what == "R" and j == 3:
            charged = (row_charge, column_charge)
            grad_corner = corner_rows(me_arr, totals[0], halves, quarter, charged, last)
            last = [grad_corner]
            grad_corner = corner_moved(grad_corner, -1)
        elif what == "R":
            last = last + [grad_corner]
        elif what == "W":
            last = last + full_far[j]
        elif what == "w":
            last = last + full_near
        elif what == "E":
            first, count = edge_spans[j]
            blocks = [(x, first) for x in edge_near] + [(x, 0) for x in reversed(edge_far[j])]
            grad_edge = edge_chunk(
                me_arr, blocks, grad_new, grad_edge, first, count,
                [x for x in last if x is not grad_edge],
            )
            last = [grad_edge]
    own_values = lax.dynamic_slice_in_dim(values[0, 0], me * rows, rows, 0)
    pair_sums = passed_along(jnp.sum(totals[1], axis=0), "row", -1)
    grad_values = -0.5 * pair_sums / own_values

    return (
        grad_corner[None, None],
        grad_edge[None, None],
        grad_half[None, None],
        grad_values[None, None],
    )


def whole_shards(corner, top_edge, half_system, values, cotangent, parity):
    rows = top_edge.shape[2]
    row_start = lax.axis_index("env") * rows
    corner_mask, out_mask = charge_masks(parity[0, 0])
    near_corner = passed_along(corner[0, 0], "col", 1)
    near_corner = jnp.where(corner_mask, near_corner, jnp.zeros_like(near_corner))
    lower_half = passed_along(half_system[0, 0], "row", -1).reshape(rows, CHI, HALF)
    absorbed = jnp.einsum("ab,iak->ibk", near_corner, lower_half, preferred_element_type=F32)
    absorbed = absorbed.astype(BF16).reshape(rows, CHI * HALF)
    gathered = lax.all_to_all(absorbed, "env", split_axis=1, concat_axis=0, tiled=True)
    edge_mat = top_edge[0, 0].reshape(rows * HALF, CHI)
    grad_new = jnp.where(
        out_mask, values[0, 0][:, None] ** (-0.5) * cotangent[0, 0].astype(F32), 0.0
    ).astype(BF16)
    grad_edge = jnp.einsum("ij,ie->je", gathered, grad_new, preferred_element_type=F32)
    grad_edge = grad_edge.astype(BF16).reshape(rows, HALF * CHI)
    grad_full = jnp.einsum("ie,je->ij", grad_new, edge_mat, preferred_element_type=F32)
    totals = lax.psum(jnp.sum(gathered * grad_full, axis=1), "env")
    pair_sums = lax.dynamic_slice_in_dim(totals, row_start, rows, 0)
    own_values = lax.dynamic_slice_in_dim(values[0, 0], row_start, rows, 0)
    grad_values = -0.5 * pair_sums / own_values
    grad_back = lax.all_to_all(
        grad_full.astype(BF16), "env", split_axis=0, concat_axis=1, tiled=True
    ).reshape(rows, CHI, HALF)
    grad_half = jnp.einsum("ab,ibk->iak", near_corner, grad_back, preferred_element_type=F32)
    grad_half = grad_half.astype(BF16).reshape(rows, CHI * HALF)
    summed = jnp.einsum("iak,ibk->ab", lower_half, grad_back, preferred_element_type=F32)
    summed = lax.psum_scatter(summed, "env", scatter_dimension=0, tiled=True)
    own_mask = lax.dynamic_slice_in_dim(corner_mask, row_start, rows, 0)
    grad_corner = jnp.where(own_mask, summed, 0.0).astype(BF16)
    grad_corner = passed_along(grad_corner, "col", -1)
    grad_half = passed_along(grad_half, "row", 1)
    return (
        grad_corner[None, None],
        grad_edge[None, None],
        grad_half[None, None],
        grad_values[None, None],
    )


def solution(mesh):
    chunked = mesh.shape["env"] == ENV
    return jax.shard_map(
        chunked_shards if chunked else whole_shards,
        mesh=mesh,
        in_specs=(
            P("row", "col", None, None),
            P("row", "col", "env", None),
            P("row", "col", "env", None),
            P("row", "col", None),
            P("row", "col", None, None),
            P("row", "col", None, None),
        ),
        out_specs=(
            P("row", "col", "env", None),
            P("row", "col", "env", None),
            P("row", "col", "env", None),
            P("row", "col", "env"),
        ),
        check_vma=False,
    )
```

time: 912 us -> 795 us (0.87)
  waiting for transfers between devices: 532 us -> 359 us
  local copies, waits for them, and re-layouts: 159 us -> 11.1 us
  Pallas kernels: 143 us -> 272 us
  starting transfers between devices: 57.9 us -> 143 us
  other arithmetic: 15.6 us -> 3.78 us
    ppermute x35 -> x24, waiting for transfers between devices: 464 us -> 315 us  [the longest x20 315 us: swapped(): return lax.ppermute(x, ('row', 'env'), pairs)]
    unnamed x109 -> x47, local copies, waits for them, and re-layouts: 115 us -> 6.99 us
    ppermute x35 -> x24, starting transfers between devices: 54 us -> 142 us  [the longest x20 76.7 us: swapped(): return lax.ppermute(x, ('row', 'env'), pairs)]
    pallas_call x0 -> x7, Pallas kernels: none -> 51.7 us  [the longest x1 20 us: k_minor(): pl.pallas_call(kernel, grid=(CHI // GROUP,), in_specs=[pl.BlockSpec((x.sh...]
    pallas_call x8 -> x7, Pallas kernels: 27 us -> 63.3 us  [absorbed_chunk(): pl.pallas_call(kernel, grid_spec=pltpu.PrefetchScalarGridSpec(num_scalar_...]
    pallas_call x3, Pallas kernels: 27.7 us -> 57.5 us  [full_chunk(): pl.pallas_call(kernel, grid_spec=pltpu.PrefetchScalarGridSpec(num_scalar_...]
    ppermute x4 -> x2, waiting for transfers between devices: 68.1 us -> 44.4 us  [passed_along(): return lax.ppermute(x, axis, [(i, (i + by) % size) for i in range(size)])]
    transpose x1 -> x0, local copies, waits for them, and re-layouts: 17.9 us -> none  [chunked_shards(): grad_half = grad_half.transpose(1, 0, 2).reshape(CHI * HALF, rows).T]
  transfers between devices with their start and end apart: 39 -> 26, of which waited for: 21 -> 9; matrix products, arithmetic and copies ran while one was open for 5% -> 0% of each run, Pallas kernels for 13% -> 33%
where the time goes in v2:
time: 795 us; the launch traced here: 789 us
  waiting for transfers between devices  359 us (45%)
  Pallas kernels  272 us (34%)
  starting transfers between devices  143 us (18%)
  local copies, waits for them, and re-layouts  11.1 us (1%)
    ppermute x20, waiting for transfers between devices, swapped(): return lax.ppermute(x, ('row', 'env'), pairs)  315 us
    ppermute x20, starting transfers between devices, swapped(): return lax.ppermute(x, ('row', 'env'), pairs)  76.7 us
    pallas_call x7, Pallas kernels, absorbed_chunk(): pl.pallas_call(kernel, grid_spec=pltpu.PrefetchScalarGridSpec(num_scalar_...  63.3 us
    ppermute x2, starting transfers between devices, swapped(): return lax.ppermute(x, 'env', [(i, i ^ d) for i in range(n_env)])  57.5 us
    pallas_call x3, Pallas kernels, full_chunk(): pl.pallas_call(kernel, grid_spec=pltpu.PrefetchScalarGridSpec(num_scalar_...  57.5 us
    pallas_call x2, Pallas kernels, half_chunk(): pl.pallas_call(kernel, grid_spec=pltpu.PrefetchScalarGridSpec(num_scalar_...  53.4 us
    pallas_call x6, Pallas kernels, edge_chunk(): pl.pallas_call(kernel, grid_spec=pltpu.PrefetchScalarGridSpec(num_scalar_...  45.7 us
    ppermute x2, waiting for transfers between devices, passed_along(): return lax.ppermute(x, axis, [(i, (i + by) % size) for i in range(size)])  44.4 us
  transfers between devices with their start and end apart: 26, of which 9 were waited for; matrix products, arithmetic and copies ran while one was open for 0% of the time, Pallas kernels for 33%

profile of v2, /device:TPU:9, one launch (start us, length us, event | category | flops | bytes accessed | tf_op | source)
XLA Modules:
  0.0 789.5 jit_solution(10771306975132603324)
XLA Ops:
  13.9 24.7 %grad_full.4 = (bf16[28,256,256]{2,1,0:T(8,128)(2,1)}, bf16[28,256,256]{2,1,0:T(8,128)(2,1)}) custom-call(s32[1]{0:T(128)} %bitcast.me_ref, bf16[256,32768]{1,0:T(8,128)(2,1)} %bitcast.30, bf16[1024,1024]{1,0:T(8,128)(2,1)} %fusion.1.refs_0_.refs_1_.refs_4_.refs_5_.refs_6_.refs_7_, bf16[1024,1024]{1,0:T(8,128)(2,1)} %fusion.1.refs_0_.refs_1_.refs_4_.refs_5_.refs_6_.refs_7_, ...), custom_call_target="tpu_custom_call" | custom-call | flops 29360128 | bytes 114688 | tf_op jit(solution)/shard_map/grad_full/pallas_call | solution.py:93
  38.6 8.9 %collective-permute-done.3.refs_3_.refs_2_ = bf16[4,256,256]{2,1,0:T(8,128)(2,1)S(1)} collective-permute-done((bf16[4,256,256]{2,1,0:T(8,128)(2,1)}, bf16[4,256,256]{2,1,0:T(8,128)(2,1)S(1)}, u32[]{:S(2)}, u32[]{:S(2)}) %collective-permute-start.3) | collective-permute-done | bytes 524320 | tf_op jit(solution)/shard_map/ppermute | solution.py:41
  47.5 11.2 %collective-permute-done.2.refs_2_.refs_3_ = bf16[4,256,256]{2,1,0:T(8,128)(2,1)S(1)} collective-permute-done((bf16[4,256,256]{2,1,0:T(8,128)(2,1)}, bf16[4,256,256]{2,1,0:T(8,128)(2,1)S(1)}, u32[]{:S(2)}, u32[]{:S(2)}) %collective-permute-start.2) | collective-permute-done | bytes 524320 | tf_op jit(solution)/shard_map/ppermute | solution.py:41
  65.5 41.2 %collective-permute-done.1 = s32[4,8]{1,0:T(4,128)S(1)} collective-permute-done((s32[4,8]{1,0:T(4,128)S(1)}, s32[4,8]{1,0:T(4,128)S(1)}, u32[]{:S(2)}, u32[]{:S(2)}) %collective-permute-start.1) | collective-permute-done | bytes 160 | tf_op jit(solution)/shard_map/ppermute | solution.py:30
  107.8 28.0 %grad_full.5 = (bf16[32,256,256]{2,1,0:T(8,128)(2,1)}, bf16[32,256,256]{2,1,0:T(8,128)(2,1)}) custom-call(s32[1]{0:T(128)} %bitcast.me_ref, bf16[256,32768]{1,0:T(8,128)(2,1)} %bitcast.31, bf16[1024,1024]{1,0:T(8,128)(2,1)} %fusion.1.refs_0_.refs_1_.refs_4_.refs_5_.refs_6_.refs_7_, bf16[1024,1024]{1,0:T(8,128)(2,1)} %fusion.1.refs_0_.refs_1_.refs_4_.refs_5_.refs_6_.refs_7_, ...), custom_call_target="tpu_custom_call" | custom-call | flops 33554432 | bytes 131072 | tf_op jit(solution)/shard_map/grad_full/pallas_call | solution.py:93
  141.8 19.8 %k_major.1.l_ref.refs_2_ = bf16[32,1024,256]{2,1,0:T(8,128)(2,1)} custom-call(bf16[256,32768]{1,0:T(8,128)(2,1)} %bitcast.33, bf16[1024,1024]{1,0:T(8,128)(2,1)} %get-tuple-element.40.refs_0_.refs_1_), custom_call_target="tpu_custom_call" | custom-call | flops 1048576 | bytes 4096 | tf_op jit(solution)/shard_map/k_major/pallas_call | solution.py:119
  161.6 9.0 %absorbed.7 = (bf16[9,256,256]{2,1,0:T(8,128)(2,1)}, bf16[9,256,256]{2,1,0:T(8,128)(2,1)}) custom-call(s32[1]{0:T(128)} %bitcast.me_ref, bf16[32,1024,256]{2,1,0:T(8,128)(2,1)} %k_major.1.l_ref.refs_2_, bf16[1024,1024]{1,0:T(8,128)(2,1)} %get-tuple-element.40.refs_0_.refs_1_, bf16[1024,1024]{1,0:T(8,128)(2,1)} %get-tuple-element.40.refs_0_.refs_1_, ...), custom_call_target="tpu_custom_call" | custom-call | flops 9437184 | bytes 36864 | tf_op jit(solution)/shard_map/absorbed/pallas_call | solution.py:179
  176.6 9.0 %absorbed.8 = (bf16[9,256,256]{2,1,0:T(8,128)(2,1)}, bf16[9,256,256]{2,1,0:T(8,128)(2,1)}) custom-call(s32[1]{0:T(128)} %bitcast.me_ref, bf16[32,1024,256]{2,1,0:T(8,128)(2,1)} %k_major.1.l_ref.refs_2_, bf16[1024,1024]{1,0:T(8,128)(2,1)} %get-tuple-element.40.refs_0_.refs_1_, bf16[1024,1024]{1,0:T(8,128)(2,1)} %get-tuple-element.40.refs_0_.refs_1_, ...), custom_call_target="tpu_custom_call" | custom-call | flops 9437184 | bytes 36864 | tf_op jit(solution)/shard_map/absorbed/pallas_call | solution.py:179
  185.6 27.6 %absorbed.9 = (bf16[32,256,256]{2,1,0:T(8,128)(2,1)}, bf16[32,256,256]{2,1,0:T(8,128)(2,1)}) custom-call(s32[1]{0:T(128)} %bitcast.me_ref, bf16[32,1024,256]{2,1,0:T(8,128)(2,1)} %k_major.1.l_ref.refs_2_, bf16[1024,1024]{1,0:T(8,128)(2,1)} %get-tuple-element.40.refs_0_.refs_1_, bf16[1024,1024]{1,0:T(8,128)(2,1)} %get-tuple-element.40.refs_0_.refs_1_, ...), custom_call_target="tpu_custom_call" | custom-call | flops 33554432 | bytes 131072 | tf_op jit(solution)/shard_map/absorbed/pallas_call | solution.py:179
  213.2 211.9 %collective-permute-done.13.refs_2_ = bf16[9,256,256]{2,1,0:T(8,128)(2,1)S(1)} collective-permute-done((bf16[9,256,256]{2,1,0:T(8,128)(2,1)}, bf16[9,256,256]{2,1,0:T(8,128)(2,1)S(1)}, u32[]{:S(2)}, u32[]{:S(2)}) %collective-permute-start.13) | collective-permute-done | bytes 1179680 | tf_op jit(solution)/shard_map/ppermute | solution.py:41
  433.3 9.9 %grad_half.2 = (bf16[4,1024,256]{2,1,0:T(8,128)(2,1)}, f32[1024,1024]{1,0:T(8,128)}, f32[8,256]{1,0:T(8,128)}) custom-call(s32[1]{0:T(128)} %bitcast.me_ref, bf16[32,1024,256]{2,1,0:T(8,128)(2,1)} %k_major.1.l_ref.refs_2_, bf16[32,256,256]{2,1,0:T(8,128)(2,1)} %collective-permute-done.4.refs_0_, bf16[32,256,256]{2,1,0:T(8,128)(2,1)} %collective-permute-done.5.refs_1_, ...), custom_call_target="tpu_custom_call" | custom-call | flops 8388608 | bytes 32768 | tf_op jit(solution)/shard_map/grad_half/pallas_call | solution.py:237
  443.2 43.5 %grad_half.3 = (bf16[28,1024,256]{2,1,0:T(8,128)(2,1)}, f32[1024,1024]{1,0:T(8,128)}, f32[8,256]{1,0:T(8,128)}) custom-call(s32[1]{0:T(128)} %bitcast.me_ref, bf16[32,1024,256]{2,1,0:T(8,128)(2,1)} %k_major.1.l_ref.refs_2_, bf16[32,256,256]{2,1,0:T(8,128)(2,1)} %collective-permute-done.4.refs_0_, bf16[32,256,256]{2,1,0:T(8,128)(2,1)} %collective-permute-done.5.refs_1_, ...), custom_call_target="tpu_custom_call" | custom-call | flops 58720256 | bytes 229376 | tf_op jit(solution)/shard_map/grad_half/pallas_call | solution.py:237
  489.2 57.5 %collective-permute-start.8 = (bf16[2,256,1024]{2,1,0:T(8,128)(2,1)}, bf16[2,256,1024]{2,1,0:T(8,128)(2,1)S(1)}, u32[]{:S(2)}, u32[]{:S(2)}) collective-permute-start(bf16[2,256,1024]{2,1,0:T(8,128)(2,1)} %corner_halves.1.refs_2_), channel_id=1, source_target_pairs={{0,1},{1,0},{2,3},{3,2},{4,5},{5,4},{6,7},{7,6},{8,9},{9,8},{10,11... | collective-permute-start | bytes 3145736 | tf_op jit(solution)/shard_map/ppermute | solution.py:36
  546.7 6.4 absorbed.10
  553.1 14.6 %collective-permute-done.10.refs_1_ = bf16[32,256,256]{2,1,0:T(8,128)(2,1)S(1)} collective-permute-done((bf16[32,256,256]{2,1,0:T(8,128)(2,1)}, bf16[32,256,256]{2,1,0:T(8,128)(2,1)S(1)}, u32[]{:S(2)}, u32[]{:S(2)}) %collective-permute-start.10) | collective-permute-done | bytes 4194336 | tf_op jit(solution)/shard_map/ppermute | solution.py:41
  570.8 39.0 %collective-permute-start.17 = (bf16[6,256,256]{2,1,0:T(8,128)(2,1)}, bf16[6,256,256]{2,1,0:T(8,128)(2,1)S(1)}, u32[]{:S(2)}, u32[]{:S(2)}) collective-permute-start(bf16[6,256,256]{2,1,0:T(8,128)(2,1)} %get-tuple-element.56.refs_8_), channel_id=1, source_target_pairs={{0,27},{1,26},{2,25},{3,24},{8,3},{9,2},{10,1},{11,0},{16,11},{17,... | collective-permute-start | bytes 2359304 | tf_op jit(solution)/shard_map/ppermute | solution.py:41
  609.8 11.4 %grad_edge.6.refs_2_.refs_9_ = bf16[256,32768]{1,0:T(8,128)(2,1)} custom-call(s32[1]{0:T(128)} %bitcast.me_ref, bf16[32,256,256]{2,1,0:T(8,128)(2,1)} %collective-permute-done.9.refs_0_, bf16[32,256,256]{2,1,0:T(8,128)(2,1)} %copy-done, bf16[9,256,256]{2,1,0:T(8,128)(2,1)} %copy-done.8, bf16[9,256,256]{2,1,0:T(8,128)(2,1)} %collective-permute-done.14.refs_3_, ...), custom_call_target="tpu_custom_call" | custom-call | flops 9437184 | bytes 36864 | tf_op jit(solution)/shard_map/grad_edge/pallas_call | solution.py:283
  625.9 20.0 %k_minor.1.refs_8_ = bf16[256,32768]{1,0:T(8,128)(2,1)} custom-call(bf16[4,1024,256]{2,1,0:T(8,128)(2,1)} %get-tuple-element.53.refs_0_, bf16[28,1024,256]{2,1,0:T(8,128)(2,1)} %get-tuple-element.54.refs_1_, bf16[4,256,256]{2,1,0:T(8,128)(2,1)} %get-tuple-element.57.refs_2_), custom_call_target="tpu_custom_call" | custom-call | flops 1048576 | bytes 4096 | tf_op jit(solution)/shard_map/k_minor/pallas_call | solution.py:139
  645.9 11.4 %grad_edge.7.refs_0_.refs_9_ = bf16[256,32768]{1,0:T(8,128)(2,1)} custom-call(s32[1]{0:T(128)} %bitcast.me_ref, bf16[32,256,256]{2,1,0:T(8,128)(2,1)} %collective-permute-done.9.refs_0_, bf16[32,256,256]{2,1,0:T(8,128)(2,1)} %copy-done, bf16[9,256,256]{2,1,0:T(8,128)(2,1)} %collective-permute-done.11.refs_2_, ...), custom_call_target="tpu_custom_call", output_to_operand_aliasing={{}: (10, {})} | custom-call | flops 9437184 | bytes 36864 | tf_op jit(solution)/shard_map/grad_edge/pallas_call | solution.py:283
  667.1 40.2 %collective-permute-done.17.refs_3_ = bf16[6,256,256]{2,1,0:T(8,128)(2,1)S(1)} collective-permute-done((bf16[6,256,256]{2,1,0:T(8,128)(2,1)}, bf16[6,256,256]{2,1,0:T(8,128)(2,1)S(1)}, u32[]{:S(2)}, u32[]{:S(2)}) %collective-permute-start.17) | collective-permute-done | bytes 786464 | tf_op jit(solution)/shard_map/ppermute | solution.py:41
  708.1 8.1 %grad_edge.8.refs_0_.refs_9_ = bf16[256,32768]{1,0:T(8,128)(2,1)} custom-call(s32[1]{0:T(128)} %bitcast.me_ref, bf16[32,256,256]{2,1,0:T(8,128)(2,1)} %collective-permute-done.9.refs_0_, bf16[32,256,256]{2,1,0:T(8,128)(2,1)} %copy-done, bf16[6,256,256]{2,1,0:T(8,128)(2,1)} %copy-done.10, ...), custom_call_target="tpu_custom_call", output_to_operand_aliasing={{}: (10, {})} | custom-call | flops 6291456 | bytes 24576 | tf_op jit(solution)/shard_map/grad_edge/pallas_call | solution.py:283
  729.8 6.8 collective-permute-start.22
  741.0 22.4 %collective-permute-done.24.refs_3_ = bf16[4,256,256]{2,1,0:T(8,128)(2,1)S(1)} collective-permute-done((bf16[4,256,256]{2,1,0:T(8,128)(2,1)}, bf16[4,256,256]{2,1,0:T(8,128)(2,1)S(1)}, u32[]{:S(2)}, u32[]{:S(2)}) %collective-permute-start.24) | collective-permute-done | bytes 524320 | tf_op jit(solution)/shard_map/ppermute | solution.py:41
  766.5 6.1 grad_edge.9.refs_9_
  (111 shorter events, 100.0 us)
Async XLA Ops:
  10.1 37.4 %collective-permute-start.3 = (bf16[4,256,256]{2,1,0:T(8,128)(2,1)}, bf16[4,256,256]{2,1,0:T(8,128)(2,1)S(1)}, u32[]{:S(2)}, u32[]{:S(2)}) collective-permute-start(bf16[4,256,256]{2,1,0:T(8,128)(2,1)} %get-tuple-element.37), channel_id=1, source_target_pairs={{0,10},{1,11},{2,8},{3,9},{8,18},{9,19},{10,16},{11,17},{16,26},{1... | collective-permute-start | bytes 1572872 | tf_op jit(solution)/shard_map/ppermute | solution.py:41
  13.9 44.8 %collective-permute-start.2 = (bf16[4,256,256]{2,1,0:T(8,128)(2,1)}, bf16[4,256,256]{2,1,0:T(8,128)(2,1)S(1)}, u32[]{:S(2)}, u32[]{:S(2)}) collective-permute-start(bf16[4,256,256]{2,1,0:T(8,128)(2,1)} %get-tuple-element.34.refs_2_), channel_id=1, source_target_pairs={{0,11},{1,10},{2,9},{3,8},{8,19},{9,18},{10,17},{11,16},{16,27},{1... | collective-permute-start | bytes 1572872 | tf_op jit(solution)/shard_map/ppermute | solution.py:41
  59.5 369.0 %collective-permute-start.6 = (bf16[28,256,256]{2,1,0:T(8,128)(2,1)}, bf16[28,256,256]{2,1,0:T(8,128)(2,1)}, u32[]{:S(2)}, u32[]{:S(2)}) collective-permute-start(bf16[28,256,256]{2,1,0:T(8,128)(2,1)} %get-tuple-element.42), channel_id=1, source_target_pairs={{0,10},{1,11},{2,8},{3,9},{8,18},{9,19},{10,16},{11,17},{16,26},{1... | collective-permute-start | bytes 11010056 | tf_op jit(solution)/shard_map/ppermute | solution.py:41
  59.5 76.3 %collective-permute-start = (bf16[1024,1024]{1,0:T(8,128)(2,1)}, bf16[1024,1024]{1,0:T(8,128)(2,1)S(1)}, u32[]{:S(2)}, u32[]{:S(2)}) collective-permute-start(bf16[1024,1024]{1,0:T(8,128)(2,1)} %bitcast.2), channel_id=1, source_target_pairs={{0,12},{4,8},{8,20},{12,16},{16,28},{20,24},{24,4},{28,0},{1,13},{... | collective-permute-start | bytes 6291464 | tf_op jit(solution)/shard_map/ppermute | solution.py:50
  61.9 368.5 %collective-permute-start.7 = (bf16[28,256,256]{2,1,0:T(8,128)(2,1)}, bf16[28,256,256]{2,1,0:T(8,128)(2,1)}, u32[]{:S(2)}, u32[]{:S(2)}) collective-permute-start(bf16[28,256,256]{2,1,0:T(8,128)(2,1)} %get-tuple-element.38.refs_2_), channel_id=1, source_target_pairs={{0,11},{1,10},{2,9},{3,8},{8,19},{9,18},{10,17},{11,16},{16,27},{1... | collective-permute-start | bytes 11010056 | tf_op jit(solution)/shard_map/ppermute | solution.py:41
  64.0 42.7 %collective-permute-start.1 = (s32[4,8]{1,0:T(4,128)S(1)}, s32[4,8]{1,0:T(4,128)S(1)}, u32[]{:S(2)}, u32[]{:S(2)}) collective-permute-start(s32[4,8]{1,0:T(4,128)S(1)} %bitcast.41), channel_id=1, source_target_pairs={{0,8},{8,16},{16,24},{24,0},{1,9},{9,17},{17,25},{25,1},{2,10},{10... | collective-permute-start | bytes 392 | tf_op jit(solution)/shard_map/ppermute | solution.py:30
  170.5 254.6 %collective-permute-start.13 = (bf16[9,256,256]{2,1,0:T(8,128)(2,1)}, bf16[9,256,256]{2,1,0:T(8,128)(2,1)S(1)}, u32[]{:S(2)}, u32[]{:S(2)}) collective-permute-start(bf16[9,256,256]{2,1,0:T(8,128)(2,1)} %get-tuple-element.55), channel_id=1, source_target_pairs={{0,26},{1,27},{2,24},{3,25},{8,2},{9,3},{10,0},{11,1},{16,10},{17,... | collective-permute-start | bytes 3538952 | tf_op jit(solution)/shard_map/ppermute | solution.py:41
  170.5 259.9 %collective-permute-start.5 = (bf16[32,256,256]{2,1,0:T(8,128)(2,1)}, bf16[32,256,256]{2,1,0:T(8,128)(2,1)}, u32[]{:S(2)}, u32[]{:S(2)}) collective-permute-start(bf16[32,256,256]{2,1,0:T(8,128)(2,1)} %get-tuple-element.41), channel_id=1, source_target_pairs={{0,9},{1,8},{2,11},{3,10},{8,17},{9,16},{10,19},{11,18},{16,25},{1... | collective-permute-start | bytes 12582920 | tf_op jit(solution)/shard_map/ppermute | solution.py:41
  175.0 257.7 %collective-permute-start.4 = (bf16[32,256,256]{2,1,0:T(8,128)(2,1)}, bf16[32,256,256]{2,1,0:T(8,128)(2,1)}, u32[]{:S(2)}, u32[]{:S(2)}) collective-permute-start(bf16[32,256,256]{2,1,0:T(8,128)(2,1)} %get-tuple-element.39.refs_0_), channel_id=1, source_target_pairs={{0,8},{1,9},{2,10},{3,11},{8,16},{9,17},{10,18},{11,19},{16,24},{1... | collective-permute-start | bytes 12582920 | tf_op jit(solution)/shard_map/ppermute | solution.py:41
  425.2 142.6 %collective-permute-start.10 = (bf16[32,256,256]{2,1,0:T(8,128)(2,1)}, bf16[32,256,256]{2,1,0:T(8,128)(2,1)S(1)}, u32[]{:S(2)}, u32[]{:S(2)}) collective-permute-start(bf16[32,256,256]{2,1,0:T(8,128)(2,1)} %get-tuple-element.51), channel_id=1, source_target_pairs={{0,25},{1,24},{2,27},{3,26},{8,1},{9,0},{10,3},{11,2},{16,9},{17,8... | collective-permute-start | bytes 12582920 | tf_op jit(solution)/shard_map/ppermute | solution.py:41
  428.6 142.2 %collective-permute-start.9 = (bf16[32,256,256]{2,1,0:T(8,128)(2,1)}, bf16[32,256,256]{2,1,0:T(8,128)(2,1)}, u32[]{:S(2)}, u32[]{:S(2)}) collective-permute-start(bf16[32,256,256]{2,1,0:T(8,128)(2,1)} %get-tuple-element.46.refs_8_), channel_id=1, source_target_pairs={{0,24},{1,25},{2,26},{3,27},{8,0},{9,1},{10,2},{11,3},{16,8},{17,9... | collective-permute-start | bytes 12582920 | tf_op jit(solution)/shard_map/ppermute | solution.py:41
  430.4 58.8 %collective-permute-start.14 = (bf16[9,256,256]{2,1,0:T(8,128)(2,1)S(1)}, bf16[9,256,256]{2,1,0:T(8,128)(2,1)}, u32[]{:S(2)}, u32[]{:S(2)}) collective-permute-start(bf16[9,256,256]{2,1,0:T(8,128)(2,1)S(1)} %copy-done.9), channel_id=1, source_target_pairs={{0,27},{1,26},{2,25},{3,24},{8,3},{9,2},{10,1},{11,0},{16,11},{17,... | collective-permute-start | bytes 3538952 | tf_op jit(solution)/shard_map/ppermute | solution.py:41
  430.4 215.5 %collective-permute-start.11 = (bf16[9,256,256]{2,1,0:T(8,128)(2,1)}, bf16[9,256,256]{2,1,0:T(8,128)(2,1)}, u32[]{:S(2)}, u32[]{:S(2)}) collective-permute-start(bf16[9,256,256]{2,1,0:T(8,128)(2,1)} %get-tuple-element.52), channel_id=1, source_target_pairs={{0,26},{1,27},{2,24},{3,25},{8,2},{9,3},{10,0},{11,1},{16,10},{17,... | collective-permute-start | bytes 3538952 | tf_op jit(solution)/shard_map/ppermute | solution.py:41
  432.7 213.2 %collective-permute-start.12 = (bf16[9,256,256]{2,1,0:T(8,128)(2,1)S(1)}, bf16[9,256,256]{2,1,0:T(8,128)(2,1)}, u32[]{:S(2)}, u32[]{:S(2)}) collective-permute-start(bf16[9,256,256]{2,1,0:T(8,128)(2,1)S(1)} %copy-done.7), channel_id=1, source_target_pairs={{0,27},{1,26},{2,25},{3,24},{8,3},{9,2},{10,1},{11,0},{16,11},{17,... | collective-permute-start | bytes 3538952 | tf_op jit(solution)/shard_map/ppermute | solution.py:41
  489.2 168.1 %collective-permute-start.8 = (bf16[2,256,1024]{2,1,0:T(8,128)(2,1)}, bf16[2,256,1024]{2,1,0:T(8,128)(2,1)S(1)}, u32[]{:S(2)}, u32[]{:S(2)}) collective-permute-start(bf16[2,256,1024]{2,1,0:T(8,128)(2,1)} %corner_halves.1.refs_2_), channel_id=1, source_target_pairs={{0,1},{1,0},{2,3},{3,2},{4,5},{5,4},{6,7},{7,6},{8,9},{9,8},{10,11... | collective-permute-start | bytes 3145736 | tf_op jit(solution)/shard_map/ppermute | solution.py:36
  567.7 99.3 %collective-permute-start.16 = (bf16[6,256,256]{2,1,0:T(8,128)(2,1)}, bf16[6,256,256]{2,1,0:T(8,128)(2,1)S(1)}, u32[]{:S(2)}, u32[]{:S(2)}) collective-permute-start(bf16[6,256,256]{2,1,0:T(8,128)(2,1)} %get-tuple-element.58), channel_id=1, source_target_pairs={{0,26},{1,27},{2,24},{3,25},{8,2},{9,3},{10,0},{11,1},{16,10},{17,... | collective-permute-start | bytes 2359304 | tf_op jit(solution)/shard_map/ppermute | solution.py:41
  570.8 136.4 %collective-permute-start.17 = (bf16[6,256,256]{2,1,0:T(8,128)(2,1)}, bf16[6,256,256]{2,1,0:T(8,128)(2,1)S(1)}, u32[]{:S(2)}, u32[]{:S(2)}) collective-permute-start(bf16[6,256,256]{2,1,0:T(8,128)(2,1)} %get-tuple-element.56.refs_8_), channel_id=1, source_target_pairs={{0,27},{1,26},{2,25},{3,24},{8,3},{9,2},{10,1},{11,0},{16,11},{17,... | collective-permute-start | bytes 2359304 | tf_op jit(solution)/shard_map/ppermute | solution.py:41
  660.6 55.7 %collective-permute-start.15 = (bf16[256,1024]{1,0:T(8,128)(2,1)}, bf16[256,1024]{1,0:T(8,128)(2,1)S(1)}, u32[]{:S(2)}, u32[]{:S(2)}) collective-permute-start(bf16[256,1024]{1,0:T(8,128)(2,1)} %corner_quarter.1.refs_2_), channel_id=1, source_target_pairs={{0,2},{1,3},{2,0},{3,1},{4,6},{5,7},{6,4},{7,5},{8,10},{9,11},{10,... | collective-permute-start | bytes 1572872 | tf_op jit(solution)/shard_map/ppermute | solution.py:36
  660.6 79.2 %collective-permute-start.23 = (bf16[4,256,256]{2,1,0:T(8,128)(2,1)}, bf16[4,256,256]{2,1,0:T(8,128)(2,1)S(1)}, u32[]{:S(2)}, u32[]{:S(2)}) collective-permute-start(bf16[4,256,256]{2,1,0:T(8,128)(2,1)} %get-tuple-element.63), channel_id=1, source_target_pairs={{0,26},{1,27},{2,24},{3,25},{8,2},{9,3},{10,0},{11,1},{16,10},{17,... | collective-permute-start | bytes 1572872 | tf_op jit(solution)/shard_map/ppermute | solution.py:41
  661.6 101.8 %collective-permute-start.24 = (bf16[4,256,256]{2,1,0:T(8,128)(2,1)}, bf16[4,256,256]{2,1,0:T(8,128)(2,1)S(1)}, u32[]{:S(2)}, u32[]{:S(2)}) collective-permute-start(bf16[4,256,256]{2,1,0:T(8,128)(2,1)} %get-tuple-element.57.refs_2_), channel_id=1, source_target_pairs={{0,27},{1,26},{2,25},{3,24},{8,3},{9,2},{10,1},{11,0},{16,11},{17,... | collective-permute-start | bytes 1572872 | tf_op jit(solution)/shard_map/ppermute | solution.py:41
  719.7 53.0 %collective-permute-start.18 = (bf16[256,1024]{1,0:T(8,128)(2,1)}, bf16[256,1024]{1,0:T(8,128)(2,1)S(1)}, u32[]{:S(2)}, u32[]{:S(2)}) collective-permute-start(bf16[256,1024]{1,0:T(8,128)(2,1)} %grad_corner.1.refs_2_), channel_id=1, source_target_pairs={{0,28},{4,24},{8,4},{12,0},{16,12},{20,8},{24,20},{28,16},{1,29},{... | collective-permute-start | bytes 1572872 | tf_op jit(solution)/shard_map/ppermute | solution.py:50
  724.9 47.8 %collective-permute-start.21 = (bf16[3,256,256]{2,1,0:T(8,128)(2,1)S(1)}, bf16[3,256,256]{2,1,0:T(8,128)(2,1)S(1)}, u32[]{:S(2)}, u32[]{:S(2)}) collective-permute-start(bf16[3,256,256]{2,1,0:T(8,128)(2,1)S(1)} %copy-done.22), channel_id=1, source_target_pairs={{0,26},{1,27},{2,24},{3,25},{8,2},{9,3},{10,0},{11,1},{16,10},{17,... | collective-permute-start | bytes 1179656 | tf_op jit(solution)/shard_map/ppermute | solution.py:41
  729.8 48.2 %collective-permute-start.22 = (bf16[3,256,256]{2,1,0:T(8,128)(2,1)S(1)}, bf16[3,256,256]{2,1,0:T(8,128)(2,1)S(1)}, u32[]{:S(2)}, u32[]{:S(2)}) collective-permute-start(bf16[3,256,256]{2,1,0:T(8,128)(2,1)S(1)} %copy-done.15), channel_id=1, source_target_pairs={{0,27},{1,26},{2,25},{3,24},{8,3},{9,2},{10,1},{11,0},{16,11},{17,... | collective-permute-start | bytes 1179656 | tf_op jit(solution)/shard_map/ppermute | solution.py:41
  739.8 44.3 %collective-permute-start.19 = (bf16[1,256,256]{2,1,0:T(8,128)(2,1)}, bf16[1,256,256]{2,1,0:T(8,128)(2,1)S(1)}, u32[]{:S(2)}, u32[]{:S(2)}) collective-permute-start(bf16[1,256,256]{2,1,0:T(8,128)(2,1)} %get-tuple-element.60), channel_id=1, source_target_pairs={{0,26},{1,27},{2,24},{3,25},{8,2},{9,3},{10,0},{11,1},{16,10},{17,... | collective-permute-start | bytes 393224 | tf_op jit(solution)/shard_map/ppermute | solution.py:41
  (25 other events, 716.3 us)

commit v3 on v2

--- a/solution.py
+++ b/solution.py
@@ -19,8 +19,9 @@
 MIB = 1 << 20
 VMEM_MIB = 56
 COST_BITS = 20
-HELD_BACK = {1: 0}
-ORDER = "F0 F1 f C T A0 A1 a H0 H1 R1 A2 E0 A3 M E1 R2 A4 E2 R3 A5 E3 R4 E4 E5"
+CORNER_FIRST = 1
+HELD_BACK = {1: (2, 3)}
+ORDER = "F0 F1 C T A0 a A1 H0 H1 R1 A2 E0 A3 R2 M E1 A4 R3 E2 A5 E3 R4 E4 E5"
 F32 = jnp.float32
 BF16 = jnp.bfloat16
 
@@ -432,22 +433,18 @@
     top, half = top_edge[0, 0], half_system[0, 0]
     full_spans, edge_spans = spans(FULL_CHUNKS), spans(EDGE_CHUNKS)
 
-    full_far, full_near, edge_far, edge_near, half_parts = {}, [], {}, [], []
+    full, edge_far, edge_near, half_parts = {}, {}, [], []
     totals = halves = quarter = grad_corner = grad_edge = grad_half = None
     last = []
     for step in ORDER.split():
         what, j = step[0], int(step[1:] or 0)
         if what == "F":
-            blocks = full_chunk(me_arr, top, grad_new, (3, 2), *full_spans[j], last)
+            blocks = full_chunk(me_arr, top, grad_new, (3, 2, 1, 0), *full_spans[j], last)
             last = [blocks[0]]
             if j in HELD_BACK:
-                blocks = held_back(blocks, full_far[HELD_BACK[j]])
+                blocks = held_back(blocks, [full[j - 1][d] for d in HELD_BACK[j]] + [near_corner] * CORNER_FIRST)
                 last = [blocks[0]]
-            full_far[j] = [swapped(blocks[0], 3, 1), swapped(blocks[1], 2, 1)]
-        elif what == "f":
-            blocks = full_chunk(me_arr, top, grad_new, (0, 1), 0, HALF, last)
-            last = [blocks[0]]
-            full_near = [swapped(blocks[0], 0, 1), swapped(blocks[1], 1, 1)]
+            full[j] = [swapped(x, 3 - d, 1) for d, x in enumerate(blocks)][::-1]
         elif what == "C":
             near_corner, corner_t = masked_corner(near_corner, row_charge, column_charge, last)
             last = [corner_t]
@@ -464,7 +461,7 @@
             edge_near = [swapped(blocks[0], 0, -1), swapped(blocks[1], 1, -1)]
         elif what == "H":
             first, count = full_spans[j]
-            blocks = [(x, first) for x in full_near] + [(x, 0) for x in reversed(full_far[j])]
+            blocks = [(x, 0) for x in full[j]]
             part, *totals = half_chunk(
                 me_arr, blocks, lower, near_corner, totals, first, count, last
             )
@@ -489,9 +486,9 @@
         elif what == "R":
             last = last + [grad_corner]
         elif what == "W":
-            last = last + full_far[j]
+            last = last + full[j]
         elif what == "w":
-            last = last + full_near
+            last = last + full[j][:2]
         elif what == "E":
             first, count = edge_spans[j]
             blocks = [(x, first) for x in edge_near] + [(x, 0) for x in reversed(edge_far[j])]

time: 795 us -> 777 us (0.977)
  waiting for transfers between devices: 359 us -> 462 us
  starting transfers between devices: 143 us -> 45.4 us
  Pallas kernels: 272 us -> 249 us
    ppermute x2, starting transfers between devices: 57.5 us -> 2.18 us  [swapped(): return lax.ppermute(x, 'env', [(i, i ^ d) for i in range(n_env)])]
    ppermute x20 -> x22, waiting for transfers between devices: 315 us -> 357 us  [swapped(): return lax.ppermute(x, ('row', 'env'), pairs)]
    ppermute x20 -> x22, starting transfers between devices: 76.7 us -> 37.1 us  [swapped(): return lax.ppermute(x, ('row', 'env'), pairs)]
    ppermute x2, waiting for transfers between devices: 44.4 us -> 82.4 us  [passed_along(): return lax.ppermute(x, axis, [(i, (i + by) % size) for i in range(size)])]
    ppermute x2, waiting for transfers between devices: 0.01 us -> 22.5 us  [swapped(): return lax.ppermute(x, 'env', [(i, i ^ d) for i in range(n_env)])]
    pallas_call x3 -> x2, Pallas kernels: 57.5 us -> 35 us  [full_chunk(): pl.pallas_call(kernel, grid_spec=pltpu.PrefetchScalarGridSpec(num_scalar_...]
  transfers between devices with their start and end apart: 26 -> 28, of which waited for: 9 -> 12; matrix products, arithmetic and copies ran while one was open for 0% -> 1% of each run, Pallas kernels for 33% -> 32%
where the time goes in v3:
time: 777 us; the launch traced here: 773 us
  waiting for transfers between devices  462 us (59%)
  Pallas kernels  249 us (32%)
  starting transfers between devices  45.4 us (6%)
  local copies, waits for them, and re-layouts  11.7 us (2%)
    ppermute x22, waiting for transfers between devices, swapped(): return lax.ppermute(x, ('row', 'env'), pairs)  357 us
    ppermute x2, waiting for transfers between devices, passed_along(): return lax.ppermute(x, axis, [(i, (i + by) % size) for i in range(size)])  82.4 us
    pallas_call x7, Pallas kernels, absorbed_chunk(): pl.pallas_call(kernel, grid_spec=pltpu.PrefetchScalarGridSpec(num_scalar_...  63.4 us
    pallas_call x2, Pallas kernels, half_chunk(): pl.pallas_call(kernel, grid_spec=pltpu.PrefetchScalarGridSpec(num_scalar_...  53.4 us
    pallas_call x6, Pallas kernels, edge_chunk(): pl.pallas_call(kernel, grid_spec=pltpu.PrefetchScalarGridSpec(num_scalar_...  45.6 us
    ppermute x22, starting transfers between devices, swapped(): return lax.ppermute(x, ('row', 'env'), pairs)  37.1 us
    pallas_call x2, Pallas kernels, full_chunk(): pl.pallas_call(kernel, grid_spec=pltpu.PrefetchScalarGridSpec(num_scalar_...  35 us
    ppermute x2, waiting for transfers between devices, swapped(): return lax.ppermute(x, 'env', [(i, i ^ d) for i in range(n_env)])  22.5 us
  transfers between devices with their start and end apart: 28, of which 12 were waited for; matrix products, arithmetic and copies ran while one was open for 1% of the time, Pallas kernels for 32%

profile of v3, /device:TPU:9, one launch (start us, length us, event | category | flops | bytes accessed | tf_op | source)
XLA Modules:
  0.0 773.0 jit_solution(17572528068790245169)
XLA Ops:
  16.0 29.1 %grad_full.3 = (bf16[28,256,256]{2,1,0:T(8,128)(2,1)}, bf16[28,256,256]{2,1,0:T(8,128)(2,1)}, bf16[28,256,256]{2,1,0:T(8,128)(2,1)}, bf16[28,256,256]{2,1,0:T(8,128)(2,1)}) custom-call(s32[1]{0:T(128)} %bitcast.me_ref, bf16[256,32768]{1,0:T(8,128)(2,1)} %bitcast.30, bf16[1024,1024]{1,0:T(8,128)(2,1)} %fusion.1.refs_0_.refs_1_.refs_2_.refs_3_.refs_4_.refs_5_.refs_6_.refs_7_, ...), custom_call_target="tpu_custom_call" | custom-call | flops 29360128 | bytes 114688 | tf_op jit(solution)/shard_map/grad_full/pallas_call | solution.py:94
  50.4 11.2 %collective-permute-done.3.refs_5_.refs_3_ = bf16[4,256,256]{2,1,0:T(8,128)(2,1)S(1)} collective-permute-done((bf16[4,256,256]{2,1,0:T(8,128)(2,1)}, bf16[4,256,256]{2,1,0:T(8,128)(2,1)S(1)}, u32[]{:S(2)}, u32[]{:S(2)}) %collective-permute-start.3) | collective-permute-done | bytes 524320 | tf_op jit(solution)/shard_map/ppermute | solution.py:42
  69.7 82.4 %collective-permute-done.1 = s32[4,8]{1,0:T(4,128)S(1)} collective-permute-done((s32[4,8]{1,0:T(4,128)S(1)}, s32[4,8]{1,0:T(4,128)S(1)}, u32[]{:S(2)}, u32[]{:S(2)}) %collective-permute-start.1) | collective-permute-done | bytes 160 | tf_op jit(solution)/shard_map/ppermute | solution.py:31
  152.1 8.6 %collective-permute-start.7 = (bf16[28,256,256]{2,1,0:T(8,128)(2,1)}, bf16[28,256,256]{2,1,0:T(8,128)(2,1)}, u32[]{:S(2)}, u32[]{:S(2)}) collective-permute-start(bf16[28,256,256]{2,1,0:T(8,128)(2,1)} %get-tuple-element.44.refs_0_), channel_id=1, source_target_pairs={{0,11},{1,10},{2,9},{3,8},{8,19},{9,18},{10,17},{11,16},{16,27},{1... | collective-permute-start | bytes 11010056 | tf_op jit(solution)/shard_map/ppermute | solution.py:42
  167.1 19.8 %k_major.1.l_ref.refs_2_ = bf16[32,1024,256]{2,1,0:T(8,128)(2,1)} custom-call(bf16[256,32768]{1,0:T(8,128)(2,1)} %bitcast.32, bf16[1024,1024]{1,0:T(8,128)(2,1)} %get-tuple-element.45.refs_0_.refs_1_), custom_call_target="tpu_custom_call" | custom-call | flops 1048576 | bytes 4096 | tf_op jit(solution)/shard_map/k_major/pallas_call | solution.py:120
  186.9 9.0 %absorbed.7 = (bf16[9,256,256]{2,1,0:T(8,128)(2,1)}, bf16[9,256,256]{2,1,0:T(8,128)(2,1)}) custom-call(s32[1]{0:T(128)} %bitcast.me_ref, bf16[32,1024,256]{2,1,0:T(8,128)(2,1)} %k_major.1.l_ref.refs_2_, bf16[1024,1024]{1,0:T(8,128)(2,1)} %get-tuple-element.45.refs_0_.refs_1_, bf16[1024,1024]{1,0:T(8,128)(2,1)} %get-tuple-element.45.refs_0_.refs_1_, ...), custom_call_target="tpu_custom_call" | custom-call | flops 9437184 | bytes 36864 | tf_op jit(solution)/shard_map/absorbed/pallas_call | solution.py:180
  195.9 27.6 %absorbed.8 = (bf16[32,256,256]{2,1,0:T(8,128)(2,1)}, bf16[32,256,256]{2,1,0:T(8,128)(2,1)}) custom-call(s32[1]{0:T(128)} %bitcast.me_ref, bf16[32,1024,256]{2,1,0:T(8,128)(2,1)} %k_major.1.l_ref.refs_2_, bf16[1024,1024]{1,0:T(8,128)(2,1)} %get-tuple-element.45.refs_0_.refs_1_, bf16[1024,1024]{1,0:T(8,128)(2,1)} %get-tuple-element.45.refs_0_.refs_1_, ...), custom_call_target="tpu_custom_call" | custom-call | flops 33554432 | bytes 131072 | tf_op jit(solution)/shard_map/absorbed/pallas_call | solution.py:180
  223.5 12.7 %collective-permute-done.9.refs_1_ = bf16[4,256,256]{2,1,0:T(8,128)(2,1)S(1)} collective-permute-done((bf16[4,256,256]{2,1,0:T(8,128)(2,1)}, bf16[4,256,256]{2,1,0:T(8,128)(2,1)S(1)}, u32[]{:S(2)}, u32[]{:S(2)}) %collective-permute-start.9) | collective-permute-done | bytes 524320 | tf_op jit(solution)/shard_map/ppermute | solution.py:42
  240.5 9.0 %absorbed.9 = (bf16[9,256,256]{2,1,0:T(8,128)(2,1)}, bf16[9,256,256]{2,1,0:T(8,128)(2,1)}) custom-call(s32[1]{0:T(128)} %bitcast.me_ref, bf16[32,1024,256]{2,1,0:T(8,128)(2,1)} %k_major.1.l_ref.refs_2_, bf16[1024,1024]{1,0:T(8,128)(2,1)} %get-tuple-element.45.refs_0_.refs_1_, bf16[1024,1024]{1,0:T(8,128)(2,1)} %get-tuple-element.45.refs_0_.refs_1_, ...), custom_call_target="tpu_custom_call" | custom-call | flops 9437184 | bytes 36864 | tf_op jit(solution)/shard_map/absorbed/pallas_call | solution.py:180
  249.5 9.9 %grad_half.2 = (bf16[4,1024,256]{2,1,0:T(8,128)(2,1)}, f32[1024,1024]{1,0:T(8,128)}, f32[8,256]{1,0:T(8,128)}) custom-call(s32[1]{0:T(128)} %bitcast.me_ref, bf16[32,1024,256]{2,1,0:T(8,128)(2,1)} %k_major.1.l_ref.refs_2_, bf16[4,256,256]{2,1,0:T(8,128)(2,1)} %copy-done.12, bf16[4,256,256]{2,1,0:T(8,128)(2,1)} %copy-done.13, bf16[4,256,256]{2,1,0:T(8,128)(2,1)} %copy-done.3, ...), custom_call_target="tpu_custom_call" | custom-call | flops 8388608 | bytes 32768 | tf_op jit(solution)/shard_map/grad_half/pallas_call | solution.py:238
  259.4 124.4 %collective-permute-done.7.refs_3_ = bf16[28,256,256]{2,1,0:T(8,128)(2,1)} collective-permute-done((bf16[28,256,256]{2,1,0:T(8,128)(2,1)}, bf16[28,256,256]{2,1,0:T(8,128)(2,1)}, u32[]{:S(2)}, u32[]{:S(2)}) %collective-permute-start.7) | collective-permute-done | bytes 3670048 | tf_op jit(solution)/shard_map/ppermute | solution.py:42
  383.8 43.5 %grad_half.3 = (bf16[28,1024,256]{2,1,0:T(8,128)(2,1)}, f32[1024,1024]{1,0:T(8,128)}, f32[8,256]{1,0:T(8,128)}) custom-call(s32[1]{0:T(128)} %bitcast.me_ref, bf16[32,1024,256]{2,1,0:T(8,128)(2,1)} %k_major.1.l_ref.refs_2_, bf16[28,256,256]{2,1,0:T(8,128)(2,1)} %collective-permute-done.4.refs_0_, bf16[28,256,256]{2,1,0:T(8,128)(2,1)} %collective-permute-done.5.refs_1_, ...), custom_call_target="tpu_custom_call" | custom-call | flops 58720256 | bytes 229376 | tf_op jit(solution)/shard_map/grad_half/pallas_call | solution.py:238
  429.7 29.7 %collective-permute-done.13.refs_2_ = bf16[9,256,256]{2,1,0:T(8,128)(2,1)S(1)} collective-permute-done((bf16[9,256,256]{2,1,0:T(8,128)(2,1)}, bf16[9,256,256]{2,1,0:T(8,128)(2,1)S(1)}, u32[]{:S(2)}, u32[]{:S(2)}) %collective-permute-start.13) | collective-permute-done | bytes 1179680 | tf_op jit(solution)/shard_map/ppermute | solution.py:42
  462.7 72.6 %collective-permute-done.14.refs_3_ = bf16[9,256,256]{2,1,0:T(8,128)(2,1)} collective-permute-done((bf16[9,256,256]{2,1,0:T(8,128)(2,1)S(1)}, bf16[9,256,256]{2,1,0:T(8,128)(2,1)}, u32[]{:S(2)}, u32[]{:S(2)}) %collective-permute-start.14) | collective-permute-done | bytes 1179680 | tf_op jit(solution)/shard_map/ppermute | solution.py:42
  537.7 6.4 absorbed.10
  546.1 11.4 %grad_edge.6.refs_2_.refs_9_ = bf16[256,32768]{1,0:T(8,128)(2,1)} custom-call(s32[1]{0:T(128)} %bitcast.me_ref, bf16[32,256,256]{2,1,0:T(8,128)(2,1)} %collective-permute-done.11.refs_0_, bf16[32,256,256]{2,1,0:T(8,128)(2,1)} %copy-done, bf16[9,256,256]{2,1,0:T(8,128)(2,1)} %copy-done.8, bf16[9,256,256]{2,1,0:T(8,128)(2,1)} %collective-permute-done.14.refs_3_, ...), custom_call_target="tpu_custom_call" | custom-call | flops 9437184 | bytes 36864 | tf_op jit(solution)/shard_map/grad_edge/pallas_call | solution.py:284
  567.7 37.8 %collective-permute-done.16.refs_2_ = bf16[9,256,256]{2,1,0:T(8,128)(2,1)} collective-permute-done((bf16[9,256,256]{2,1,0:T(8,128)(2,1)}, bf16[9,256,256]{2,1,0:T(8,128)(2,1)}, u32[]{:S(2)}, u32[]{:S(2)}) %collective-permute-start.16) | collective-permute-done | bytes 1179680 | tf_op jit(solution)/shard_map/ppermute | solution.py:42
  608.8 44.4 %collective-permute-done.17.refs_3_ = bf16[9,256,256]{2,1,0:T(8,128)(2,1)S(1)} collective-permute-done((bf16[9,256,256]{2,1,0:T(8,128)(2,1)}, bf16[9,256,256]{2,1,0:T(8,128)(2,1)S(1)}, u32[]{:S(2)}, u32[]{:S(2)}) %collective-permute-start.17) | collective-permute-done | bytes 1179680 | tf_op jit(solution)/shard_map/ppermute | solution.py:42
  655.6 20.0 %k_minor.1.refs_8_ = bf16[256,32768]{1,0:T(8,128)(2,1)} custom-call(bf16[4,1024,256]{2,1,0:T(8,128)(2,1)} %get-tuple-element.64.refs_0_, bf16[28,1024,256]{2,1,0:T(8,128)(2,1)} %get-tuple-element.65.refs_1_, bf16[256,1024]{1,0:T(8,128)(2,1)} %corner_quarter.1.refs_2_), custom_call_target="tpu_custom_call" | custom-call | flops 1048576 | bytes 4096 | tf_op jit(solution)/shard_map/k_minor/pallas_call | solution.py:140
  675.6 22.5 %collective-permute-done.15.quarter_ref = bf16[256,1024]{1,0:T(8,128)(2,1)} collective-permute-done((bf16[256,1024]{1,0:T(8,128)(2,1)}, bf16[256,1024]{1,0:T(8,128)(2,1)}, u32[]{:S(2)}, u32[]{:S(2)}) %collective-permute-start.15) | collective-permute-done | bytes 524320 | tf_op jit(solution)/shard_map/ppermute | solution.py:37
  698.7 11.4 %grad_edge.7.refs_2_.refs_9_ = bf16[256,32768]{1,0:T(8,128)(2,1)} custom-call(s32[1]{0:T(128)} %bitcast.me_ref, bf16[32,256,256]{2,1,0:T(8,128)(2,1)} %collective-permute-done.11.refs_0_, bf16[32,256,256]{2,1,0:T(8,128)(2,1)} %copy-done, bf16[9,256,256]{2,1,0:T(8,128)(2,1)} %collective-permute-done.16.refs_2_, ...), custom_call_target="tpu_custom_call", output_to_operand_aliasing={{}: (10, {})} | custom-call | flops 9437184 | bytes 36864 | tf_op jit(solution)/shard_map/grad_edge/pallas_call | solution.py:284
  721.6 8.1 %grad_edge.8.refs_2_.refs_9_ = bf16[256,32768]{1,0:T(8,128)(2,1)} custom-call(s32[1]{0:T(128)} %bitcast.me_ref, bf16[32,256,256]{2,1,0:T(8,128)(2,1)} %collective-permute-done.11.refs_0_, bf16[32,256,256]{2,1,0:T(8,128)(2,1)} %copy-done, bf16[6,256,256]{2,1,0:T(8,128)(2,1)} %copy-done.10, ...), custom_call_target="tpu_custom_call", output_to_operand_aliasing={{}: (10, {})} | custom-call | flops 6291456 | bytes 24576 | tf_op jit(solution)/shard_map/grad_edge/pallas_call | solution.py:284
  733.2 9.9 %collective-permute-done.26.refs_3_ = bf16[4,256,256]{2,1,0:T(8,128)(2,1)} collective-permute-done((bf16[4,256,256]{2,1,0:T(8,128)(2,1)}, bf16[4,256,256]{2,1,0:T(8,128)(2,1)}, u32[]{:S(2)}, u32[]{:S(2)}) %collective-permute-start.26) | collective-permute-done | bytes 524320 | tf_op jit(solution)/shard_map/ppermute | solution.py:42
  752.3 9.3 %collective-permute-done.24.refs_3_ = bf16[3,256,256]{2,1,0:T(8,128)(2,1)S(1)} collective-permute-done((bf16[3,256,256]{2,1,0:T(8,128)(2,1)}, bf16[3,256,256]{2,1,0:T(8,128)(2,1)S(1)}, u32[]{:S(2)}, u32[]{:S(2)}) %collective-permute-start.24) | collective-permute-done | bytes 393248 | tf_op jit(solution)/shard_map/ppermute | solution.py:42
  (110 shorter events, 101.4 us)
Async XLA Ops:
  0.6 61.0 %collective-permute-start = (bf16[1024,1024]{1,0:T(8,128)(2,1)}, bf16[1024,1024]{1,0:T(8,128)(2,1)S(1)}, u32[]{:S(2)}, u32[]{:S(2)}) collective-permute-start(bf16[1024,1024]{1,0:T(8,128)(2,1)} %bitcast.41), channel_id=1, source_target_pairs={{0,12},{4,8},{8,20},{12,16},{16,28},{20,24},{24,4},{28,0},{1,13},{... | collective-permute-start | bytes 6291464 | tf_op jit(solution)/shard_map/ppermute | solution.py:51
  14.0 36.4 %collective-permute-start.2 = (bf16[4,256,256]{2,1,0:T(8,128)(2,1)}, bf16[4,256,256]{2,1,0:T(8,128)(2,1)S(1)}, u32[]{:S(2)}, u32[]{:S(2)}) collective-permute-start(bf16[4,256,256]{2,1,0:T(8,128)(2,1)} %get-tuple-element.43), channel_id=1, source_target_pairs={{0,10},{1,11},{2,8},{3,9},{8,18},{9,19},{10,16},{11,17},{16,26},{1... | collective-permute-start | bytes 1572872 | tf_op jit(solution)/shard_map/ppermute | solution.py:42
  16.0 45.6 %collective-permute-start.3 = (bf16[4,256,256]{2,1,0:T(8,128)(2,1)}, bf16[4,256,256]{2,1,0:T(8,128)(2,1)S(1)}, u32[]{:S(2)}, u32[]{:S(2)}) collective-permute-start(bf16[4,256,256]{2,1,0:T(8,128)(2,1)} %get-tuple-element.38.refs_4_), channel_id=1, source_target_pairs={{0,11},{1,10},{2,9},{3,8},{8,19},{9,18},{10,17},{11,16},{16,27},{1... | collective-permute-start | bytes 1572872 | tf_op jit(solution)/shard_map/ppermute | solution.py:42
  63.1 173.1 %collective-permute-start.4 = (bf16[28,256,256]{2,1,0:T(8,128)(2,1)}, bf16[28,256,256]{2,1,0:T(8,128)(2,1)}, u32[]{:S(2)}, u32[]{:S(2)}) collective-permute-start(bf16[28,256,256]{2,1,0:T(8,128)(2,1)} %get-tuple-element.46), channel_id=1, source_target_pairs={{0,8},{1,9},{2,10},{3,11},{8,16},{9,17},{10,18},{11,19},{16,24},{1... | collective-permute-start | bytes 11010056 | tf_op jit(solution)/shard_map/ppermute | solution.py:42
  64.1 172.2 %collective-permute-start.5 = (bf16[28,256,256]{2,1,0:T(8,128)(2,1)}, bf16[28,256,256]{2,1,0:T(8,128)(2,1)}, u32[]{:S(2)}, u32[]{:S(2)}) collective-permute-start(bf16[28,256,256]{2,1,0:T(8,128)(2,1)} %get-tuple-element.47), channel_id=1, source_target_pairs={{0,9},{1,8},{2,11},{3,10},{8,17},{9,16},{10,19},{11,18},{16,25},{1... | collective-permute-start | bytes 11010056 | tf_op jit(solution)/shard_map/ppermute | solution.py:42
  64.1 176.2 %collective-permute-start.6 = (bf16[28,256,256]{2,1,0:T(8,128)(2,1)}, bf16[28,256,256]{2,1,0:T(8,128)(2,1)}, u32[]{:S(2)}, u32[]{:S(2)}) collective-permute-start(bf16[28,256,256]{2,1,0:T(8,128)(2,1)} %get-tuple-element.48), channel_id=1, source_target_pairs={{0,10},{1,11},{2,8},{3,9},{8,18},{9,19},{10,16},{11,17},{16,26},{1... | collective-permute-start | bytes 11010056 | tf_op jit(solution)/shard_map/ppermute | solution.py:42
  68.1 84.0 %collective-permute-start.8 = (bf16[4,256,256]{2,1,0:T(8,128)(2,1)S(1)}, bf16[4,256,256]{2,1,0:T(8,128)(2,1)S(1)}, u32[]{:S(2)}, u32[]{:S(2)}) collective-permute-start(bf16[4,256,256]{2,1,0:T(8,128)(2,1)S(1)} %copy-done.20), channel_id=1, source_target_pairs={{0,8},{1,9},{2,10},{3,11},{8,16},{9,17},{10,18},{11,19},{16,24},{1... | collective-permute-start | bytes 1572872 | tf_op jit(solution)/shard_map/ppermute | solution.py:42
  68.2 83.9 %collective-permute-start.1 = (s32[4,8]{1,0:T(4,128)S(1)}, s32[4,8]{1,0:T(4,128)S(1)}, u32[]{:S(2)}, u32[]{:S(2)}) collective-permute-start(s32[4,8]{1,0:T(4,128)S(1)} %bitcast.40), channel_id=1, source_target_pairs={{0,8},{8,16},{16,24},{24,0},{1,9},{9,17},{17,25},{25,1},{2,10},{10... | collective-permute-start | bytes 392 | tf_op jit(solution)/shard_map/ppermute | solution.py:31
  152.1 84.1 %collective-permute-start.9 = (bf16[4,256,256]{2,1,0:T(8,128)(2,1)}, bf16[4,256,256]{2,1,0:T(8,128)(2,1)S(1)}, u32[]{:S(2)}, u32[]{:S(2)}) collective-permute-start(bf16[4,256,256]{2,1,0:T(8,128)(2,1)} %get-tuple-element.51), channel_id=1, source_target_pairs={{0,9},{1,8},{2,11},{3,10},{8,17},{9,16},{10,19},{11,18},{16,25},{1... | collective-permute-start | bytes 1572872 | tf_op jit(solution)/shard_map/ppermute | solution.py:42
  152.1 231.7 %collective-permute-start.7 = (bf16[28,256,256]{2,1,0:T(8,128)(2,1)}, bf16[28,256,256]{2,1,0:T(8,128)(2,1)}, u32[]{:S(2)}, u32[]{:S(2)}) collective-permute-start(bf16[28,256,256]{2,1,0:T(8,128)(2,1)} %get-tuple-element.44.refs_0_), channel_id=1, source_target_pairs={{0,11},{1,10},{2,9},{3,8},{8,19},{9,18},{10,17},{11,16},{16,27},{1... | collective-permute-start | bytes 11010056 | tf_op jit(solution)/shard_map/ppermute | solution.py:42
  236.2 307.9 %collective-permute-start.12 = (bf16[32,256,256]{2,1,0:T(8,128)(2,1)}, bf16[32,256,256]{2,1,0:T(8,128)(2,1)S(1)}, u32[]{:S(2)}, u32[]{:S(2)}) collective-permute-start(bf16[32,256,256]{2,1,0:T(8,128)(2,1)} %get-tuple-element.59), channel_id=1, source_target_pairs={{0,25},{1,24},{2,27},{3,26},{8,1},{9,0},{10,3},{11,2},{16,9},{17,8... | collective-permute-start | bytes 12582920 | tf_op jit(solution)/shard_map/ppermute | solution.py:42
  236.2 307.9 %collective-permute-start.11 = (bf16[32,256,256]{2,1,0:T(8,128)(2,1)}, bf16[32,256,256]{2,1,0:T(8,128)(2,1)}, u32[]{:S(2)}, u32[]{:S(2)}) collective-permute-start(bf16[32,256,256]{2,1,0:T(8,128)(2,1)} %get-tuple-element.53.refs_2_), channel_id=1, source_target_pairs={{0,24},{1,25},{2,26},{3,27},{8,0},{9,1},{10,2},{11,3},{16,8},{17,9... | collective-permute-start | bytes 12582920 | tf_op jit(solution)/shard_map/ppermute | solution.py:42
  237.0 222.4 %collective-permute-start.13 = (bf16[9,256,256]{2,1,0:T(8,128)(2,1)}, bf16[9,256,256]{2,1,0:T(8,128)(2,1)S(1)}, u32[]{:S(2)}, u32[]{:S(2)}) collective-permute-start(bf16[9,256,256]{2,1,0:T(8,128)(2,1)} %get-tuple-element.60), channel_id=1, source_target_pairs={{0,26},{1,27},{2,24},{3,25},{8,2},{9,3},{10,0},{11,1},{16,10},{17,... | collective-permute-start | bytes 3538952 | tf_op jit(solution)/shard_map/ppermute | solution.py:42
  240.3 295.1 %collective-permute-start.14 = (bf16[9,256,256]{2,1,0:T(8,128)(2,1)S(1)}, bf16[9,256,256]{2,1,0:T(8,128)(2,1)}, u32[]{:S(2)}, u32[]{:S(2)}) collective-permute-start(bf16[9,256,256]{2,1,0:T(8,128)(2,1)S(1)} %copy-done.7), channel_id=1, source_target_pairs={{0,27},{1,26},{2,25},{3,24},{8,3},{9,2},{10,1},{11,0},{16,11},{17,... | collective-permute-start | bytes 3538952 | tf_op jit(solution)/shard_map/ppermute | solution.py:42
  429.7 132.6 %collective-permute-start.10 = (bf16[2,256,1024]{2,1,0:T(8,128)(2,1)}, bf16[2,256,1024]{2,1,0:T(8,128)(2,1)S(1)}, u32[]{:S(2)}, u32[]{:S(2)}) collective-permute-start(bf16[2,256,1024]{2,1,0:T(8,128)(2,1)} %corner_halves.1.refs_2_), channel_id=1, source_target_pairs={{0,1},{1,0},{2,3},{3,2},{4,5},{5,4},{6,7},{7,6},{8,9},{9,8},{10,11... | collective-permute-start | bytes 3145736 | tf_op jit(solution)/shard_map/ppermute | solution.py:37
  459.4 146.1 %collective-permute-start.16 = (bf16[9,256,256]{2,1,0:T(8,128)(2,1)}, bf16[9,256,256]{2,1,0:T(8,128)(2,1)}, u32[]{:S(2)}, u32[]{:S(2)}) collective-permute-start(bf16[9,256,256]{2,1,0:T(8,128)(2,1)} %get-tuple-element.63), channel_id=1, source_target_pairs={{0,26},{1,27},{2,24},{3,25},{8,2},{9,3},{10,0},{11,1},{16,10},{17,... | collective-permute-start | bytes 3538952 | tf_op jit(solution)/shard_map/ppermute | solution.py:42
  535.3 117.9 %collective-permute-start.17 = (bf16[9,256,256]{2,1,0:T(8,128)(2,1)}, bf16[9,256,256]{2,1,0:T(8,128)(2,1)S(1)}, u32[]{:S(2)}, u32[]{:S(2)}) collective-permute-start(bf16[9,256,256]{2,1,0:T(8,128)(2,1)} %get-tuple-element.54.refs_8_), channel_id=1, source_target_pairs={{0,27},{1,26},{2,25},{3,24},{8,3},{9,2},{10,1},{11,0},{16,11},{17,... | collective-permute-start | bytes 3538952 | tf_op jit(solution)/shard_map/ppermute | solution.py:42
  544.1 174.0 %collective-permute-start.19 = (bf16[6,256,256]{2,1,0:T(8,128)(2,1)}, bf16[6,256,256]{2,1,0:T(8,128)(2,1)S(1)}, u32[]{:S(2)}, u32[]{:S(2)}) collective-permute-start(bf16[6,256,256]{2,1,0:T(8,128)(2,1)} %get-tuple-element.67), channel_id=1, source_target_pairs={{0,26},{1,27},{2,24},{3,25},{8,2},{9,3},{10,0},{11,1},{16,10},{17,... | collective-permute-start | bytes 2359304 | tf_op jit(solution)/shard_map/ppermute | solution.py:42
  544.2 176.5 %collective-permute-start.20 = (bf16[6,256,256]{2,1,0:T(8,128)(2,1)}, bf16[6,256,256]{2,1,0:T(8,128)(2,1)S(1)}, u32[]{:S(2)}, u32[]{:S(2)}) collective-permute-start(bf16[6,256,256]{2,1,0:T(8,128)(2,1)} %get-tuple-element.61.refs_8_), channel_id=1, source_target_pairs={{0,27},{1,26},{2,25},{3,24},{8,3},{9,2},{10,1},{11,0},{16,11},{17,... | collective-permute-start | bytes 2359304 | tf_op jit(solution)/shard_map/ppermute | solution.py:42
  565.5 132.7 %collective-permute-start.15 = (bf16[256,1024]{1,0:T(8,128)(2,1)}, bf16[256,1024]{1,0:T(8,128)(2,1)}, u32[]{:S(2)}, u32[]{:S(2)}) collective-permute-start(bf16[256,1024]{1,0:T(8,128)(2,1)} %corner_quarter.1.refs_2_), channel_id=1, source_target_pairs={{0,2},{1,3},{2,0},{3,1},{4,6},{5,7},{6,4},{7,5},{8,10},{9,11},{10,... | collective-permute-start | bytes 1572872 | tf_op jit(solution)/shard_map/ppermute | solution.py:37
  605.5 126.8 %collective-permute-start.25 = (bf16[4,256,256]{2,1,0:T(8,128)(2,1)}, bf16[4,256,256]{2,1,0:T(8,128)(2,1)}, u32[]{:S(2)}, u32[]{:S(2)}) collective-permute-start(bf16[4,256,256]{2,1,0:T(8,128)(2,1)} %get-tuple-element.71), channel_id=1, source_target_pairs={{0,26},{1,27},{2,24},{3,25},{8,2},{9,3},{10,0},{11,1},{16,10},{17,... | collective-permute-start | bytes 1572872 | tf_op jit(solution)/shard_map/ppermute | solution.py:42
  653.2 89.9 %collective-permute-start.26 = (bf16[4,256,256]{2,1,0:T(8,128)(2,1)}, bf16[4,256,256]{2,1,0:T(8,128)(2,1)}, u32[]{:S(2)}, u32[]{:S(2)}) collective-permute-start(bf16[4,256,256]{2,1,0:T(8,128)(2,1)} %get-tuple-element.62.refs_0_), channel_id=1, source_target_pairs={{0,27},{1,26},{2,25},{3,24},{8,3},{9,2},{10,1},{11,0},{16,11},{17,... | collective-permute-start | bytes 1572872 | tf_op jit(solution)/shard_map/ppermute | solution.py:42
  720.7 40.9 %collective-permute-start.24 = (bf16[3,256,256]{2,1,0:T(8,128)(2,1)}, bf16[3,256,256]{2,1,0:T(8,128)(2,1)S(1)}, u32[]{:S(2)}, u32[]{:S(2)}) collective-permute-start(bf16[3,256,256]{2,1,0:T(8,128)(2,1)} %get-tuple-element.66.refs_0_), channel_id=1, source_target_pairs={{0,27},{1,26},{2,25},{3,24},{8,3},{9,2},{10,1},{11,0},{16,11},{17,... | collective-permute-start | bytes 1179656 | tf_op jit(solution)/shard_map/ppermute | solution.py:42
  732.2 35.5 %collective-permute-start.21 = (bf16[1,256,256]{2,1,0:T(8,128)(2,1)}, bf16[1,256,256]{2,1,0:T(8,128)(2,1)S(1)}, u32[]{:S(2)}, u32[]{:S(2)}) collective-permute-start(bf16[1,256,256]{2,1,0:T(8,128)(2,1)} %get-tuple-element.68), channel_id=1, source_target_pairs={{0,26},{1,27},{2,24},{3,25},{8,2},{9,3},{10,0},{11,1},{16,10},{17,... | collective-permute-start | bytes 393224 | tf_op jit(solution)/shard_map/ppermute | solution.py:42
  (25 other events, 449.6 us)

commit v4 on v3

--- a/solution.py
+++ b/solution.py
@@ -78,33 +78,78 @@
     return with_layout_constraint(x, Layout(tuple(range(x.ndim))))
 
 
-def full_chunk(me, top_edge, grad_new, ds, first, count, after):
+def full_chunk(top_edge, grad_blocks, ds, first, count, after):
     rows = top_edge.shape[0]
     n_out = len(ds)
-
-    def kernel(me_ref, t_ref, *refs):
+    step = 2 if first % 2 == 0 and count % 2 == 0 else 1
+
+    def kernel(t_ref, *refs):
         g_refs, outs = refs[:n_out], refs[-n_out:]
-        t = t_ref[...]
+        t = jnp.concatenate([t_ref[:, j * CHI:(j + 1) * CHI] for j in range(step)], axis=0)
         for g_ref, out in zip(g_refs, outs):
-            out[0] = nt(t, g_ref[...]).astype(BF16)
-
-    def grad_spec(d):
-        return pl.BlockSpec((rows, CHI), lambda k, me: (me[0] ^ d, 0))
-
-    return pl.pallas_call(
-        kernel,
-        grid_spec=pltpu.PrefetchScalarGridSpec(
-            num_scalar_prefetch=1,
-            grid=(count,),
-            in_specs=[pl.BlockSpec((rows, CHI), lambda k, me: (0, first + k))]
-            + [grad_spec(d) for d in ds] + [ANYWHERE] * len(after),
-            out_specs=[pl.BlockSpec((1, rows, rows), lambda k, me: (k, 0, 0))] * n_out,
-        ),
+            out[...] = nt(t, g_ref[...]).astype(BF16).reshape(step, rows, rows)
+
+    return pl.pallas_call(
+        kernel,
+        grid=(count // step,),
+        in_specs=[pl.BlockSpec((rows, step * CHI), lambda k: (0, first // step + k))]
+        + [pl.BlockSpec((rows, CHI), lambda k: (0, 0))] * n_out + [ANYWHERE] * len(after),
+        out_specs=[pl.BlockSpec((step, rows, rows), lambda k: (k, 0, 0))] * n_out,
         out_shape=[jax.ShapeDtypeStruct((count, rows, rows), BF16)] * n_out,
         compiler_params=params(),
         cost_estimate=cost(count),
         name="grad_full",
-    )(me, top_edge, *[grad_new] * n_out, *after)
+    )(top_edge, *[grad_blocks[d] for d in ds], *after)
+
+
+def first_full_chunk(me, parity, top_edge, values, cotangent, ds, count):
+    rows = top_edge.shape[0]
+    n = CHI // rows
+    step = 2 if count % 2 == 0 else 1
+
+    def kernel(me_ref, parity_ref, t_ref, *refs):
+        v_refs, cot_refs, g_refs, outs = refs[:n], refs[n:2 * n], refs[2 * n:3 * n], refs[3 * n:]
+
+        @pl.when(pl.program_id(0) == 0)
+        def _():
+            for d in range(n):
+                weight = jnp.broadcast_to(v_refs[d][...], (8, rows)).T[:, :1] ** (-0.5)
+                for i in range(rows // BLK):
+                    charge = parity_ref[2, (me_ref[0] ^ d) * (rows // BLK) + i]
+                    part = slice(i * BLK, (i + 1) * BLK)
+                    for e in range(CHI // BLK):
+                        across = slice(e * BLK, (e + 1) * BLK)
+                        scaled = weight[part] * cot_refs[d][part, across].astype(F32)
+                        kept = jnp.where(charge == parity_ref[3, e], scaled, 0.0)
+                        g_refs[d][part, across] = kept.astype(BF16)
+
+        t = jnp.concatenate([t_ref[:, j * CHI:(j + 1) * CHI] for j in range(step)], axis=0)
+        for d, out in zip(ds, outs):
+            out[...] = nt(t, g_refs[d][...]).astype(BF16).reshape(step, rows, rows)
+
+    def value_spec(d):
+        return pl.BlockSpec((1, rows), lambda k, me, parity: (0, me[0] ^ d))
+
+    def cotangent_spec(d):
+        return pl.BlockSpec((rows, CHI), lambda k, me, parity: (me[0] ^ d, 0))
+
+    made = pl.pallas_call(
+        kernel,
+        grid_spec=pltpu.PrefetchScalarGridSpec(
+            num_scalar_prefetch=2,
+            grid=(count // step,),
+            in_specs=[pl.BlockSpec((rows, step * CHI), lambda k, me, parity: (0, k))]
+            + [value_spec(d) for d in range(n)] + [cotangent_spec(d) for d in range(n)],
+            out_specs=[pl.BlockSpec((rows, CHI), lambda k, me, parity: (0, 0))] * n
+            + [pl.BlockSpec((step, rows, rows), lambda k, me, parity: (k, 0, 0))] * len(ds),
+        ),
+        out_shape=[jax.ShapeDtypeStruct((rows, CHI), BF16)] * n
+        + [jax.ShapeDtypeStruct((count, rows, rows), BF16)] * len(ds),
+        compiler_params=params(),
+        cost_estimate=cost(count),
+        name="grad_full",
+    )(me, parity, top_edge, *[values] * n, *[cotangent] * n)
+    return made[:n], made[n:]
 
 
 GROUP = 64
@@ -261,35 +306,30 @@
     )(*operands)
 
 
-def edge_chunk(me, blocks, grad_new, held, first, count, after):
+def edge_chunk(blocks, grad_blocks, held, first, count, after):
     rows = blocks[0][0].shape[1]
     n = CHI // rows
     has_held = held is not None
 
-    def kernel(me_ref, *refs):
+    def kernel(*refs):
         a_refs, g_refs, out = refs[:n], refs[n:2 * n], refs[-1]
         total = nn(a_refs[0][0], g_refs[0][...])
         for d in range(1, n):
             total += nn(a_refs[d][0], g_refs[d][...])
         out[...] = total.astype(BF16)
 
-    def grad_spec(d):
-        return pl.BlockSpec((rows, CHI), lambda k, me: (me[0] ^ d, 0))
-
     def block_spec(offset):
-        return pl.BlockSpec((1, rows, rows), lambda k, me: (offset + k, 0, 0))
-
-    operands = [me, *[x for x, _ in blocks], *[grad_new] * n, *after]
+        return pl.BlockSpec((1, rows, rows), lambda k: (offset + k, 0, 0))
+
+    operands = [*[x for x, _ in blocks], *grad_blocks, *after]
     operands += [held] if has_held else []
     return pl.pallas_call(
         kernel,
-        grid_spec=pltpu.PrefetchScalarGridSpec(
-            num_scalar_prefetch=1,
-            grid=(count,),
-            in_specs=[block_spec(offset) for _, offset in blocks]
-            + [grad_spec(d) for d in range(n)] + [ANYWHERE] * (len(after) + has_held),
-            out_specs=pl.BlockSpec((rows, CHI), lambda k, me: (0, first + k)),
-        ),
+        grid=(count,),
+        in_specs=[block_spec(offset) for _, offset in blocks]
+        + [pl.BlockSpec((rows, CHI), lambda k: (0, 0))] * n
+        + [ANYWHERE] * (len(after) + has_held),
+        out_specs=pl.BlockSpec((rows, CHI), lambda k: (0, first + k)),
         out_shape=jax.ShapeDtypeStruct((rows, HALF * CHI), BF16),
         input_output_aliases={len(operands) - 1: 0} if has_held else {},
         compiler_params=params(),
@@ -426,10 +466,6 @@
     near_corner = row_major(corner_moved(row_major(corner[0, 0]), 1))
     above = jnp.repeat(passed_along(parity[0, 0], "row", 1), BLK, axis=1)
     row_charge, column_charge = above[0][:, None], above[1][None, :]
-    _, out_mask = charge_masks(parity[0, 0])
-    grad_new = jnp.where(
-        out_mask, values[0, 0][:, None] ** (-0.5) * cotangent[0, 0].astype(F32), 0.0
-    ).astype(BF16)
     top, half = top_edge[0, 0], half_system[0, 0]
     full_spans, edge_spans = spans(FULL_CHUNKS), spans(EDGE_CHUNKS)
 
@@ -439,7 +475,13 @@
     for step in ORDER.split():
         what, j = step[0], int(step[1:] or 0)
         if what == "F":
-            blocks = full_chunk(me_arr, top, grad_new, (3, 2, 1, 0), *full_spans[j], last)
+            if j == 0:
+                grad_blocks, blocks = first_full_chunk(
+                    me_arr, parity[0, 0], top, values[0], cotangent[0, 0],
+                    (3, 2, 1, 0), full_spans[0][1],
+                )
+            else:
+                blocks = full_chunk(top, grad_blocks, (3, 2, 1, 0), *full_spans[j], last)
             last = [blocks[0]]
             if j in HELD_BACK:
                 blocks = held_back(blocks, [full[j - 1][d] for d in HELD_BACK[j]] + [near_corner] * CORNER_FIRST)
@@ -493,7 +535,7 @@
             first, count = edge_spans[j]
             blocks = [(x, first) for x in edge_near] + [(x, 0) for x in reversed(edge_far[j])]
             grad_edge = edge_chunk(
-                me_arr, blocks, grad_new, grad_edge, first, count,
+                blocks, grad_blocks, grad_edge, first, count,
                 [x for x in last if x is not grad_edge],
             )
             last = [grad_edge]

time: 777 us -> 773 us (level)
  waiting for transfers between devices: 462 us -> 470 us
  transfers between devices with their start and end apart: 28 -> 28, of which waited for: 12 -> 12; matrix products, arithmetic and copies ran while one was open for 1% -> 0% of each run, Pallas kernels for 32% -> 31%
where the time goes in v4:
time: 773 us; the launch traced here: 770 us
  waiting for transfers between devices  470 us (61%)
  Pallas kernels  243 us (31%)
  starting transfers between devices  46.5 us (6%)
  local copies, waits for them, and re-layouts  9.21 us (1%)
    ppermute x22, waiting for transfers between devices, swapped(): return lax.ppermute(x, ('row', 'env'), pairs)  365 us
    ppermute x2, waiting for transfers between devices, passed_along(): return lax.ppermute(x, axis, [(i, (i + by) % size) for i in range(size)])  82.4 us
    pallas_call x7, Pallas kernels, absorbed_chunk(): pl.pallas_call(kernel, grid_spec=pltpu.PrefetchScalarGridSpec(num_scalar_...  63.2 us
    pallas_call x2, Pallas kernels, half_chunk(): pl.pallas_call(kernel, grid_spec=pltpu.PrefetchScalarGridSpec(num_scalar_...  53.3 us
    pallas_call x6, Pallas kernels, edge_chunk(): pl.pallas_call(kernel, grid=(count,), in_specs=[block_spec(offset) for _,...  45.5 us
    ppermute x22, starting transfers between devices, swapped(): return lax.ppermute(x, ('row', 'env'), pairs)  38.1 us
    ppermute x2, waiting for transfers between devices, swapped(): return lax.ppermute(x, 'env', [(i, i ^ d) for i in range(n_env)])  22.5 us
    pallas_call x1, Pallas kernels, full_chunk(): pl.pallas_call(kernel, grid=(count // step,), in_specs=[pl.BlockSpec((row...  21.7 us
  transfers between devices with their start and end apart: 28, of which 12 were waited for; matrix products, arithmetic and copies ran while one was open for 0% of the time, Pallas kernels for 31%

profile of v4, /device:TPU:9, one launch (start us, length us, event | category | flops | bytes accessed | tf_op | source)
XLA Modules:
  0.0 769.7 jit_solution(17525686974052708672)
XLA Ops:
  12.6 21.7 %grad_full.3 = (bf16[28,256,256]{2,1,0:T(8,128)(2,1)}, bf16[28,256,256]{2,1,0:T(8,128)(2,1)}, bf16[28,256,256]{2,1,0:T(8,128)(2,1)}, bf16[28,256,256]{2,1,0:T(8,128)(2,1)}) custom-call(bf16[256,32768]{1,0:T(8,128)(2,1)} %bitcast.20, bf16[256,1024]{1,0:T(8,128)(2,1)} %get-tuple-element.42.refs_0_.refs_7_, ...), custom_call_target="tpu_custom_call" | custom-call | flops 29360128 | bytes 114688 | tf_op jit(solution)/shard_map/grad_full/pallas_call | solution.py:92
  34.3 12.7 %collective-permute-done.2.refs_4_.refs_2_ = bf16[4,256,256]{2,1,0:T(8,128)(2,1)S(1)} collective-permute-done((bf16[4,256,256]{2,1,0:T(8,128)(2,1)}, bf16[4,256,256]{2,1,0:T(8,128)(2,1)S(1)}, u32[]{:S(2)}, u32[]{:S(2)}) %collective-permute-start.2) | collective-permute-done | bytes 524320 | tf_op jit(solution)/shard_map/ppermute | solution.py:42
  47.0 11.2 %collective-permute-done.3.refs_5_.refs_3_ = bf16[4,256,256]{2,1,0:T(8,128)(2,1)S(1)} collective-permute-done((bf16[4,256,256]{2,1,0:T(8,128)(2,1)}, bf16[4,256,256]{2,1,0:T(8,128)(2,1)S(1)}, u32[]{:S(2)}, u32[]{:S(2)}) %collective-permute-start.3) | collective-permute-done | bytes 524320 | tf_op jit(solution)/shard_map/ppermute | solution.py:42
  66.3 82.4 %collective-permute-done.1 = s32[4,8]{1,0:T(4,128)S(1)} collective-permute-done((s32[4,8]{1,0:T(4,128)S(1)}, s32[4,8]{1,0:T(4,128)S(1)}, u32[]{:S(2)}, u32[]{:S(2)}) %collective-permute-start.1) | collective-permute-done | bytes 160 | tf_op jit(solution)/shard_map/ppermute | solution.py:31
  148.7 8.6 %collective-permute-start.7 = (bf16[28,256,256]{2,1,0:T(8,128)(2,1)}, bf16[28,256,256]{2,1,0:T(8,128)(2,1)}, u32[]{:S(2)}, u32[]{:S(2)}) collective-permute-start(bf16[28,256,256]{2,1,0:T(8,128)(2,1)} %get-tuple-element.52.refs_0_), channel_id=1, source_target_pairs={{0,11},{1,10},{2,9},{3,8},{8,19},{9,18},{10,17},{11,16},{16,27},{1... | collective-permute-start | bytes 11010056 | tf_op jit(solution)/shard_map/ppermute | solution.py:42
  163.6 19.8 %k_major.1.l_ref.refs_2_ = bf16[32,1024,256]{2,1,0:T(8,128)(2,1)} custom-call(bf16[256,32768]{1,0:T(8,128)(2,1)} %bitcast.26, bf16[1024,1024]{1,0:T(8,128)(2,1)} %get-tuple-element.53.refs_0_.refs_1_), custom_call_target="tpu_custom_call" | custom-call | flops 1048576 | bytes 4096 | tf_op jit(solution)/shard_map/k_major/pallas_call | solution.py:165
  183.4 9.0 %absorbed.7 = (bf16[9,256,256]{2,1,0:T(8,128)(2,1)}, bf16[9,256,256]{2,1,0:T(8,128)(2,1)}) custom-call(s32[1]{0:T(128)} %bitcast.me_ref, bf16[32,1024,256]{2,1,0:T(8,128)(2,1)} %k_major.1.l_ref.refs_2_, bf16[1024,1024]{1,0:T(8,128)(2,1)} %get-tuple-element.53.refs_0_.refs_1_, bf16[1024,1024]{1,0:T(8,128)(2,1)} %get-tuple-element.53.refs_0_.refs_1_, ...), custom_call_target="tpu_custom_call" | custom-call | flops 9437184 | bytes 36864 | tf_op jit(solution)/shard_map/absorbed/pallas_call | solution.py:225
  192.4 27.6 %absorbed.8 = (bf16[32,256,256]{2,1,0:T(8,128)(2,1)}, bf16[32,256,256]{2,1,0:T(8,128)(2,1)}) custom-call(s32[1]{0:T(128)} %bitcast.me_ref, bf16[32,1024,256]{2,1,0:T(8,128)(2,1)} %k_major.1.l_ref.refs_2_, bf16[1024,1024]{1,0:T(8,128)(2,1)} %get-tuple-element.53.refs_0_.refs_1_, bf16[1024,1024]{1,0:T(8,128)(2,1)} %get-tuple-element.53.refs_0_.refs_1_, ...), custom_call_target="tpu_custom_call" | custom-call | flops 33554432 | bytes 131072 | tf_op jit(solution)/shard_map/absorbed/pallas_call | solution.py:225
  220.0 12.9 %collective-permute-done.9.refs_1_ = bf16[4,256,256]{2,1,0:T(8,128)(2,1)S(1)} collective-permute-done((bf16[4,256,256]{2,1,0:T(8,128)(2,1)}, bf16[4,256,256]{2,1,0:T(8,128)(2,1)S(1)}, u32[]{:S(2)}, u32[]{:S(2)}) %collective-permute-start.9) | collective-permute-done | bytes 524320 | tf_op jit(solution)/shard_map/ppermute | solution.py:42
  237.1 9.0 %absorbed.9 = (bf16[9,256,256]{2,1,0:T(8,128)(2,1)}, bf16[9,256,256]{2,1,0:T(8,128)(2,1)}) custom-call(s32[1]{0:T(128)} %bitcast.me_ref, bf16[32,1024,256]{2,1,0:T(8,128)(2,1)} %k_major.1.l_ref.refs_2_, bf16[1024,1024]{1,0:T(8,128)(2,1)} %get-tuple-element.53.refs_0_.refs_1_, bf16[1024,1024]{1,0:T(8,128)(2,1)} %get-tuple-element.53.refs_0_.refs_1_, ...), custom_call_target="tpu_custom_call" | custom-call | flops 9437184 | bytes 36864 | tf_op jit(solution)/shard_map/absorbed/pallas_call | solution.py:225
  246.1 9.9 %grad_half.2 = (bf16[4,1024,256]{2,1,0:T(8,128)(2,1)}, f32[1024,1024]{1,0:T(8,128)}, f32[8,256]{1,0:T(8,128)}) custom-call(s32[1]{0:T(128)} %bitcast.me_ref, bf16[32,1024,256]{2,1,0:T(8,128)(2,1)} %k_major.1.l_ref.refs_2_, bf16[4,256,256]{2,1,0:T(8,128)(2,1)} %copy-done.12, bf16[4,256,256]{2,1,0:T(8,128)(2,1)} %copy-done.13, bf16[4,256,256]{2,1,0:T(8,128)(2,1)} %copy-done.5, ...), custom_call_target="tpu_custom_call" | custom-call | flops 8388608 | bytes 32768 | tf_op jit(solution)/shard_map/grad_half/pallas_call | solution.py:283
  256.0 124.4 %collective-permute-done.7.refs_3_ = bf16[28,256,256]{2,1,0:T(8,128)(2,1)} collective-permute-done((bf16[28,256,256]{2,1,0:T(8,128)(2,1)}, bf16[28,256,256]{2,1,0:T(8,128)(2,1)}, u32[]{:S(2)}, u32[]{:S(2)}) %collective-permute-start.7) | collective-permute-done | bytes 3670048 | tf_op jit(solution)/shard_map/ppermute | solution.py:42
  380.4 43.4 %grad_half.3 = (bf16[28,1024,256]{2,1,0:T(8,128)(2,1)}, f32[1024,1024]{1,0:T(8,128)}, f32[8,256]{1,0:T(8,128)}) custom-call(s32[1]{0:T(128)} %bitcast.me_ref, bf16[32,1024,256]{2,1,0:T(8,128)(2,1)} %k_major.1.l_ref.refs_2_, bf16[28,256,256]{2,1,0:T(8,128)(2,1)} %collective-permute-done.4.refs_0_, bf16[28,256,256]{2,1,0:T(8,128)(2,1)} %collective-permute-done.5.refs_1_, ...), custom_call_target="tpu_custom_call" | custom-call | flops 58720256 | bytes 229376 | tf_op jit(solution)/shard_map/grad_half/pallas_call | solution.py:283
  426.4 29.7 %collective-permute-done.13.refs_2_ = bf16[9,256,256]{2,1,0:T(8,128)(2,1)} collective-permute-done((bf16[9,256,256]{2,1,0:T(8,128)(2,1)}, bf16[9,256,256]{2,1,0:T(8,128)(2,1)}, u32[]{:S(2)}, u32[]{:S(2)}) %collective-permute-start.13) | collective-permute-done | bytes 1179680 | tf_op jit(solution)/shard_map/ppermute | solution.py:42
  459.5 72.5 %collective-permute-done.14.refs_3_ = bf16[9,256,256]{2,1,0:T(8,128)(2,1)} collective-permute-done((bf16[9,256,256]{2,1,0:T(8,128)(2,1)S(1)}, bf16[9,256,256]{2,1,0:T(8,128)(2,1)}, u32[]{:S(2)}, u32[]{:S(2)}) %collective-permute-start.14) | collective-permute-done | bytes 1179680 | tf_op jit(solution)/shard_map/ppermute | solution.py:42
  542.7 11.4 %grad_edge.6.refs_2_.refs_9_ = bf16[256,32768]{1,0:T(8,128)(2,1)} custom-call(bf16[32,256,256]{2,1,0:T(8,128)(2,1)} %collective-permute-done.11.refs_0_, bf16[32,256,256]{2,1,0:T(8,128)(2,1)} %copy-done, bf16[9,256,256]{2,1,0:T(8,128)(2,1)} %collective-permute-done.13.refs_2_, bf16[9,256,256]{2,1,0:T(8,128)(2,1)} %collective-permute-done.14.refs_3_, ...), custom_call_target="tpu_custom_call" | custom-call | flops 9437184 | bytes 36864 | tf_op jit(solution)/shard_map/grad_edge/pallas_call | solution.py:326
  564.2 37.9 %collective-permute-done.16.refs_2_ = bf16[9,256,256]{2,1,0:T(8,128)(2,1)} collective-permute-done((bf16[9,256,256]{2,1,0:T(8,128)(2,1)}, bf16[9,256,256]{2,1,0:T(8,128)(2,1)}, u32[]{:S(2)}, u32[]{:S(2)}) %collective-permute-start.16) | collective-permute-done | bytes 1179680 | tf_op jit(solution)/shard_map/ppermute | solution.py:42
  605.5 44.4 %collective-permute-done.17.refs_3_ = bf16[9,256,256]{2,1,0:T(8,128)(2,1)S(1)} collective-permute-done((bf16[9,256,256]{2,1,0:T(8,128)(2,1)S(1)}, bf16[9,256,256]{2,1,0:T(8,128)(2,1)S(1)}, u32[]{:S(2)}, u32[]{:S(2)}) %collective-permute-start.17) | collective-permute-done | bytes 1179680 | tf_op jit(solution)/shard_map/ppermute | solution.py:42
  652.2 20.0 %k_minor.1.refs_8_ = bf16[256,32768]{1,0:T(8,128)(2,1)} custom-call(bf16[4,1024,256]{2,1,0:T(8,128)(2,1)} %get-tuple-element.72.refs_0_, bf16[28,1024,256]{2,1,0:T(8,128)(2,1)} %get-tuple-element.73.refs_1_, bf16[256,1024]{1,0:T(8,128)(2,1)} %corner_quarter.1.refs_2_), custom_call_target="tpu_custom_call" | custom-call | flops 1048576 | bytes 4096 | tf_op jit(solution)/shard_map/k_minor/pallas_call | solution.py:185
  672.2 22.5 %collective-permute-done.15.quarter_ref = bf16[256,1024]{1,0:T(8,128)(2,1)} collective-permute-done((bf16[256,1024]{1,0:T(8,128)(2,1)}, bf16[256,1024]{1,0:T(8,128)(2,1)}, u32[]{:S(2)}, u32[]{:S(2)}) %collective-permute-start.15) | collective-permute-done | bytes 524320 | tf_op jit(solution)/shard_map/ppermute | solution.py:37
  695.4 11.4 %grad_edge.7.refs_2_.refs_9_ = bf16[256,32768]{1,0:T(8,128)(2,1)} custom-call(bf16[32,256,256]{2,1,0:T(8,128)(2,1)} %collective-permute-done.11.refs_0_, bf16[32,256,256]{2,1,0:T(8,128)(2,1)} %copy-done, bf16[9,256,256]{2,1,0:T(8,128)(2,1)} %collective-permute-done.16.refs_2_, bf16[9,256,256]{2,1,0:T(8,128)(2,1)} %copy-done.9, ...), custom_call_target="tpu_custom_call", output_to_operand_aliasing={{}: (9, {})} | custom-call | flops 9437184 | bytes 36864 | tf_op jit(solution)/shard_map/grad_edge/pallas_call | solution.py:326
  718.2 8.1 %grad_edge.8.refs_2_.refs_9_ = bf16[256,32768]{1,0:T(8,128)(2,1)} custom-call(bf16[32,256,256]{2,1,0:T(8,128)(2,1)} %collective-permute-done.11.refs_0_, bf16[32,256,256]{2,1,0:T(8,128)(2,1)} %copy-done, bf16[6,256,256]{2,1,0:T(8,128)(2,1)} %collective-permute-done.19.refs_2_, ...), custom_call_target="tpu_custom_call", output_to_operand_aliasing={{}: (9, {})} | custom-call | flops 6291456 | bytes 24576 | tf_op jit(solution)/shard_map/grad_edge/pallas_call | solution.py:326
  729.8 9.9 %collective-permute-done.26.refs_3_ = bf16[4,256,256]{2,1,0:T(8,128)(2,1)S(1)} collective-permute-done((bf16[4,256,256]{2,1,0:T(8,128)(2,1)}, bf16[4,256,256]{2,1,0:T(8,128)(2,1)S(1)}, u32[]{:S(2)}, u32[]{:S(2)}) %collective-permute-start.26) | collective-permute-done | bytes 524320 | tf_op jit(solution)/shard_map/ppermute | solution.py:42
  748.8 9.5 %collective-permute-done.24.refs_3_ = bf16[3,256,256]{2,1,0:T(8,128)(2,1)S(1)} collective-permute-done((bf16[3,256,256]{2,1,0:T(8,128)(2,1)S(1)}, bf16[3,256,256]{2,1,0:T(8,128)(2,1)S(1)}, u32[]{:S(2)}, u32[]{:S(2)}) %collective-permute-start.24) | collective-permute-done | bytes 393248 | tf_op jit(solution)/shard_map/ppermute | solution.py:42
  (108 shorter events, 99.2 us)
Async XLA Ops:
  0.6 57.6 %collective-permute-start = (bf16[1024,1024]{1,0:T(8,128)(2,1)}, bf16[1024,1024]{1,0:T(8,128)(2,1)S(1)}, u32[]{:S(2)}, u32[]{:S(2)}) collective-permute-start(bf16[1024,1024]{1,0:T(8,128)(2,1)} %bitcast.39), channel_id=1, source_target_pairs={{0,12},{4,8},{8,20},{12,16},{16,28},{20,24},{24,4},{28,0},{1,13},{... | collective-permute-start | bytes 6291464 | tf_op jit(solution)/shard_map/ppermute | solution.py:51
  10.6 36.4 %collective-permute-start.2 = (bf16[4,256,256]{2,1,0:T(8,128)(2,1)}, bf16[4,256,256]{2,1,0:T(8,128)(2,1)S(1)}, u32[]{:S(2)}, u32[]{:S(2)}) collective-permute-start(bf16[4,256,256]{2,1,0:T(8,128)(2,1)} %get-tuple-element.51), channel_id=1, source_target_pairs={{0,10},{1,11},{2,8},{3,9},{8,18},{9,19},{10,16},{11,17},{16,26},{1... | collective-permute-start | bytes 1572872 | tf_op jit(solution)/shard_map/ppermute | solution.py:42
  12.6 45.6 %collective-permute-start.3 = (bf16[4,256,256]{2,1,0:T(8,128)(2,1)}, bf16[4,256,256]{2,1,0:T(8,128)(2,1)S(1)}, u32[]{:S(2)}, u32[]{:S(2)}) collective-permute-start(bf16[4,256,256]{2,1,0:T(8,128)(2,1)} %get-tuple-element.46.refs_4_), channel_id=1, source_target_pairs={{0,11},{1,10},{2,9},{3,8},{8,19},{9,18},{10,17},{11,16},{16,27},{1... | collective-permute-start | bytes 1572872 | tf_op jit(solution)/shard_map/ppermute | solution.py:42
  59.7 173.1 %collective-permute-start.4 = (bf16[28,256,256]{2,1,0:T(8,128)(2,1)}, bf16[28,256,256]{2,1,0:T(8,128)(2,1)}, u32[]{:S(2)}, u32[]{:S(2)}) collective-permute-start(bf16[28,256,256]{2,1,0:T(8,128)(2,1)} %get-tuple-element.54), channel_id=1, source_target_pairs={{0,8},{1,9},{2,10},{3,11},{8,16},{9,17},{10,18},{11,19},{16,24},{1... | collective-permute-start | bytes 11010056 | tf_op jit(solution)/shard_map/ppermute | solution.py:42
  60.7 172.2 %collective-permute-start.5 = (bf16[28,256,256]{2,1,0:T(8,128)(2,1)}, bf16[28,256,256]{2,1,0:T(8,128)(2,1)}, u32[]{:S(2)}, u32[]{:S(2)}) collective-permute-start(bf16[28,256,256]{2,1,0:T(8,128)(2,1)} %get-tuple-element.55), channel_id=1, source_target_pairs={{0,9},{1,8},{2,11},{3,10},{8,17},{9,16},{10,19},{11,18},{16,25},{1... | collective-permute-start | bytes 11010056 | tf_op jit(solution)/shard_map/ppermute | solution.py:42
  60.7 176.2 %collective-permute-start.6 = (bf16[28,256,256]{2,1,0:T(8,128)(2,1)}, bf16[28,256,256]{2,1,0:T(8,128)(2,1)}, u32[]{:S(2)}, u32[]{:S(2)}) collective-permute-start(bf16[28,256,256]{2,1,0:T(8,128)(2,1)} %get-tuple-element.56), channel_id=1, source_target_pairs={{0,10},{1,11},{2,8},{3,9},{8,18},{9,19},{10,16},{11,17},{16,26},{1... | collective-permute-start | bytes 11010056 | tf_op jit(solution)/shard_map/ppermute | solution.py:42
  64.7 84.0 %collective-permute-start.8 = (bf16[4,256,256]{2,1,0:T(8,128)(2,1)S(1)}, bf16[4,256,256]{2,1,0:T(8,128)(2,1)S(1)}, u32[]{:S(2)}, u32[]{:S(2)}) collective-permute-start(bf16[4,256,256]{2,1,0:T(8,128)(2,1)S(1)} %copy-done.21), channel_id=1, source_target_pairs={{0,8},{1,9},{2,10},{3,11},{8,16},{9,17},{10,18},{11,19},{16,24},{1... | collective-permute-start | bytes 1572872 | tf_op jit(solution)/shard_map/ppermute | solution.py:42
  64.8 83.9 %collective-permute-start.1 = (s32[4,8]{1,0:T(4,128)S(1)}, s32[4,8]{1,0:T(4,128)S(1)}, u32[]{:S(2)}, u32[]{:S(2)}) collective-permute-start(s32[4,8]{1,0:T(4,128)S(1)} %bitcast.37), channel_id=1, source_target_pairs={{0,8},{8,16},{16,24},{24,0},{1,9},{9,17},{17,25},{25,1},{2,10},{10... | collective-permute-start | bytes 392 | tf_op jit(solution)/shard_map/ppermute | solution.py:31
  148.7 84.1 %collective-permute-start.9 = (bf16[4,256,256]{2,1,0:T(8,128)(2,1)}, bf16[4,256,256]{2,1,0:T(8,128)(2,1)S(1)}, u32[]{:S(2)}, u32[]{:S(2)}) collective-permute-start(bf16[4,256,256]{2,1,0:T(8,128)(2,1)} %get-tuple-element.59), channel_id=1, source_target_pairs={{0,9},{1,8},{2,11},{3,10},{8,17},{9,16},{10,19},{11,18},{16,25},{1... | collective-permute-start | bytes 1572872 | tf_op jit(solution)/shard_map/ppermute | solution.py:42
  148.7 231.7 %collective-permute-start.7 = (bf16[28,256,256]{2,1,0:T(8,128)(2,1)}, bf16[28,256,256]{2,1,0:T(8,128)(2,1)}, u32[]{:S(2)}, u32[]{:S(2)}) collective-permute-start(bf16[28,256,256]{2,1,0:T(8,128)(2,1)} %get-tuple-element.52.refs_0_), channel_id=1, source_target_pairs={{0,11},{1,10},{2,9},{3,8},{8,19},{9,18},{10,17},{11,16},{16,27},{1... | collective-permute-start | bytes 11010056 | tf_op jit(solution)/shard_map/ppermute | solution.py:42
  232.8 307.8 %collective-permute-start.12 = (bf16[32,256,256]{2,1,0:T(8,128)(2,1)}, bf16[32,256,256]{2,1,0:T(8,128)(2,1)S(1)}, u32[]{:S(2)}, u32[]{:S(2)}) collective-permute-start(bf16[32,256,256]{2,1,0:T(8,128)(2,1)} %get-tuple-element.67), channel_id=1, source_target_pairs={{0,25},{1,24},{2,27},{3,26},{8,1},{9,0},{10,3},{11,2},{16,9},{17,8... | collective-permute-start | bytes 12582920 | tf_op jit(solution)/shard_map/ppermute | solution.py:42
  232.8 307.9 %collective-permute-start.11 = (bf16[32,256,256]{2,1,0:T(8,128)(2,1)}, bf16[32,256,256]{2,1,0:T(8,128)(2,1)}, u32[]{:S(2)}, u32[]{:S(2)}) collective-permute-start(bf16[32,256,256]{2,1,0:T(8,128)(2,1)} %get-tuple-element.61.refs_2_), channel_id=1, source_target_pairs={{0,24},{1,25},{2,26},{3,27},{8,0},{9,1},{10,2},{11,3},{16,8},{17,9... | collective-permute-start | bytes 12582920 | tf_op jit(solution)/shard_map/ppermute | solution.py:42
  232.9 223.1 %collective-permute-start.13 = (bf16[9,256,256]{2,1,0:T(8,128)(2,1)}, bf16[9,256,256]{2,1,0:T(8,128)(2,1)}, u32[]{:S(2)}, u32[]{:S(2)}) collective-permute-start(bf16[9,256,256]{2,1,0:T(8,128)(2,1)} %get-tuple-element.68), channel_id=1, source_target_pairs={{0,26},{1,27},{2,24},{3,25},{8,2},{9,3},{10,0},{11,1},{16,10},{17,... | collective-permute-start | bytes 3538952 | tf_op jit(solution)/shard_map/ppermute | solution.py:42
  236.9 295.1 %collective-permute-start.14 = (bf16[9,256,256]{2,1,0:T(8,128)(2,1)S(1)}, bf16[9,256,256]{2,1,0:T(8,128)(2,1)}, u32[]{:S(2)}, u32[]{:S(2)}) collective-permute-start(bf16[9,256,256]{2,1,0:T(8,128)(2,1)S(1)} %copy-done.7), channel_id=1, source_target_pairs={{0,27},{1,26},{2,25},{3,24},{8,3},{9,2},{10,1},{11,0},{16,11},{17,... | collective-permute-start | bytes 3538952 | tf_op jit(solution)/shard_map/ppermute | solution.py:42
  426.3 132.4 %collective-permute-start.10 = (bf16[2,256,1024]{2,1,0:T(8,128)(2,1)}, bf16[2,256,1024]{2,1,0:T(8,128)(2,1)S(1)}, u32[]{:S(2)}, u32[]{:S(2)}) collective-permute-start(bf16[2,256,1024]{2,1,0:T(8,128)(2,1)} %corner_halves.1.refs_2_), channel_id=1, source_target_pairs={{0,1},{1,0},{2,3},{3,2},{4,5},{5,4},{6,7},{7,6},{8,9},{9,8},{10,11... | collective-permute-start | bytes 3145736 | tf_op jit(solution)/shard_map/ppermute | solution.py:37
  456.0 146.1 %collective-permute-start.16 = (bf16[9,256,256]{2,1,0:T(8,128)(2,1)}, bf16[9,256,256]{2,1,0:T(8,128)(2,1)}, u32[]{:S(2)}, u32[]{:S(2)}) collective-permute-start(bf16[9,256,256]{2,1,0:T(8,128)(2,1)} %get-tuple-element.71), channel_id=1, source_target_pairs={{0,26},{1,27},{2,24},{3,25},{8,2},{9,3},{10,0},{11,1},{16,10},{17,... | collective-permute-start | bytes 3538952 | tf_op jit(solution)/shard_map/ppermute | solution.py:42
  532.0 117.9 %collective-permute-start.17 = (bf16[9,256,256]{2,1,0:T(8,128)(2,1)S(1)}, bf16[9,256,256]{2,1,0:T(8,128)(2,1)S(1)}, u32[]{:S(2)}, u32[]{:S(2)}) collective-permute-start(bf16[9,256,256]{2,1,0:T(8,128)(2,1)S(1)} %copy-done.8), channel_id=1, source_target_pairs={{0,27},{1,26},{2,25},{3,24},{8,3},{9,2},{10,1},{11,0},{16,11},{17,... | collective-permute-start | bytes 3538952 | tf_op jit(solution)/shard_map/ppermute | solution.py:42
  540.7 174.1 %collective-permute-start.19 = (bf16[6,256,256]{2,1,0:T(8,128)(2,1)}, bf16[6,256,256]{2,1,0:T(8,128)(2,1)}, u32[]{:S(2)}, u32[]{:S(2)}) collective-permute-start(bf16[6,256,256]{2,1,0:T(8,128)(2,1)} %get-tuple-element.75), channel_id=1, source_target_pairs={{0,26},{1,27},{2,24},{3,25},{8,2},{9,3},{10,0},{11,1},{16,10},{17,... | collective-permute-start | bytes 2359304 | tf_op jit(solution)/shard_map/ppermute | solution.py:42
  540.8 176.6 %collective-permute-start.20 = (bf16[6,256,256]{2,1,0:T(8,128)(2,1)}, bf16[6,256,256]{2,1,0:T(8,128)(2,1)}, u32[]{:S(2)}, u32[]{:S(2)}) collective-permute-start(bf16[6,256,256]{2,1,0:T(8,128)(2,1)} %get-tuple-element.69.refs_8_), channel_id=1, source_target_pairs={{0,27},{1,26},{2,25},{3,24},{8,3},{9,2},{10,1},{11,0},{16,11},{17,... | collective-permute-start | bytes 2359304 | tf_op jit(solution)/shard_map/ppermute | solution.py:42
  562.0 132.8 %collective-permute-start.15 = (bf16[256,1024]{1,0:T(8,128)(2,1)}, bf16[256,1024]{1,0:T(8,128)(2,1)}, u32[]{:S(2)}, u32[]{:S(2)}) collective-permute-start(bf16[256,1024]{1,0:T(8,128)(2,1)} %corner_quarter.1.refs_2_), channel_id=1, source_target_pairs={{0,2},{1,3},{2,0},{3,1},{4,6},{5,7},{6,4},{7,5},{8,10},{9,11},{10,... | collective-permute-start | bytes 1572872 | tf_op jit(solution)/shard_map/ppermute | solution.py:37
  602.1 126.7 %collective-permute-start.25 = (bf16[4,256,256]{2,1,0:T(8,128)(2,1)}, bf16[4,256,256]{2,1,0:T(8,128)(2,1)S(1)}, u32[]{:S(2)}, u32[]{:S(2)}) collective-permute-start(bf16[4,256,256]{2,1,0:T(8,128)(2,1)} %get-tuple-element.79), channel_id=1, source_target_pairs={{0,26},{1,27},{2,24},{3,25},{8,2},{9,3},{10,0},{11,1},{16,10},{17,... | collective-permute-start | bytes 1572872 | tf_op jit(solution)/shard_map/ppermute | solution.py:42
  649.8 89.9 %collective-permute-start.26 = (bf16[4,256,256]{2,1,0:T(8,128)(2,1)}, bf16[4,256,256]{2,1,0:T(8,128)(2,1)S(1)}, u32[]{:S(2)}, u32[]{:S(2)}) collective-permute-start(bf16[4,256,256]{2,1,0:T(8,128)(2,1)} %get-tuple-element.70.refs_0_), channel_id=1, source_target_pairs={{0,27},{1,26},{2,25},{3,24},{8,3},{9,2},{10,1},{11,0},{16,11},{17,... | collective-permute-start | bytes 1572872 | tf_op jit(solution)/shard_map/ppermute | solution.py:42
  717.3 40.9 %collective-permute-start.24 = (bf16[3,256,256]{2,1,0:T(8,128)(2,1)S(1)}, bf16[3,256,256]{2,1,0:T(8,128)(2,1)S(1)}, u32[]{:S(2)}, u32[]{:S(2)}) collective-permute-start(bf16[3,256,256]{2,1,0:T(8,128)(2,1)S(1)} %copy-done.16), channel_id=1, source_target_pairs={{0,27},{1,26},{2,25},{3,24},{8,3},{9,2},{10,1},{11,0},{16,11},{17,... | collective-permute-start | bytes 1179656 | tf_op jit(solution)/shard_map/ppermute | solution.py:42
  728.8 35.6 %collective-permute-start.21 = (bf16[1,256,256]{2,1,0:T(8,128)(2,1)}, bf16[1,256,256]{2,1,0:T(8,128)(2,1)S(1)}, u32[]{:S(2)}, u32[]{:S(2)}) collective-permute-start(bf16[1,256,256]{2,1,0:T(8,128)(2,1)} %get-tuple-element.76), channel_id=1, source_target_pairs={{0,26},{1,27},{2,24},{3,25},{8,2},{9,3},{10,0},{11,1},{16,10},{17,... | collective-permute-start | bytes 393224 | tf_op jit(solution)/shard_map/ppermute | solution.py:42
  (26 other events, 504.6 us)

commit v5 on v4

--- a/solution.py
+++ b/solution.py
@@ -102,30 +102,31 @@
     )(top_edge, *[grad_blocks[d] for d in ds], *after)
 
 
-def first_full_chunk(me, parity, top_edge, values, cotangent, ds, count):
+def first_full_chunk(me, parity, top_edge, values, cotangent, ds, count, after):
     rows = top_edge.shape[0]
-    n = CHI // rows
+    n = len(ds)
     step = 2 if count % 2 == 0 else 1
 
     def kernel(me_ref, parity_ref, t_ref, *refs):
-        v_refs, cot_refs, g_refs, outs = refs[:n], refs[n:2 * n], refs[2 * n:3 * n], refs[3 * n:]
+        v_refs, cot_refs = refs[:n], refs[n:2 * n]
+        g_refs, outs = refs[-2 * n:-n], refs[-n:]
 
         @pl.when(pl.program_id(0) == 0)
         def _():
-            for d in range(n):
-                weight = jnp.broadcast_to(v_refs[d][...], (8, rows)).T[:, :1] ** (-0.5)
+            for d, v_ref, cot_ref, g_ref in zip(ds, v_refs, cot_refs, g_refs):
+                weight = jnp.broadcast_to(v_ref[...], (8, rows)).T[:, :1] ** (-0.5)
                 for i in range(rows // BLK):
                     charge = parity_ref[2, (me_ref[0] ^ d) * (rows // BLK) + i]
                     part = slice(i * BLK, (i + 1) * BLK)
                     for e in range(CHI // BLK):
                         across = slice(e * BLK, (e + 1) * BLK)
-                        scaled = weight[part] * cot_refs[d][part, across].astype(F32)
+                        scaled = weight[part] * cot_ref[part, across].astype(F32)
                         kept = jnp.where(charge == parity_ref[3, e], scaled, 0.0)
-                        g_refs[d][part, across] = kept.astype(BF16)
+                        g_ref[part, across] = kept.astype(BF16)
 
         t = jnp.concatenate([t_ref[:, j * CHI:(j + 1) * CHI] for j in range(step)], axis=0)
-        for d, out in zip(ds, outs):
-            out[...] = nt(t, g_refs[d][...]).astype(BF16).reshape(step, rows, rows)
+        for g_ref, out in zip(g_refs, outs):
+            out[...] = nt(t, g_ref[...]).astype(BF16).reshape(step, rows, rows)
 
     def value_spec(d):
         return pl.BlockSpec((1, rows), lambda k, me, parity: (0, me[0] ^ d))
@@ -139,16 +140,17 @@
             num_scalar_prefetch=2,
             grid=(count // step,),
             in_specs=[pl.BlockSpec((rows, step * CHI), lambda k, me, parity: (0, k))]
-            + [value_spec(d) for d in range(n)] + [cotangent_spec(d) for d in range(n)],
+            + [value_spec(d) for d in ds] + [cotangent_spec(d) for d in ds]
+            + [ANYWHERE] * len(after),
             out_specs=[pl.BlockSpec((rows, CHI), lambda k, me, parity: (0, 0))] * n
-            + [pl.BlockSpec((step, rows, rows), lambda k, me, parity: (k, 0, 0))] * len(ds),
+            + [pl.BlockSpec((step, rows, rows), lambda k, me, parity: (k, 0, 0))] * n,
         ),
         out_shape=[jax.ShapeDtypeStruct((rows, CHI), BF16)] * n
-        + [jax.ShapeDtypeStruct((count, rows, rows), BF16)] * len(ds),
+        + [jax.ShapeDtypeStruct((count, rows, rows), BF16)] * n,
         compiler_params=params(),
         cost_estimate=cost(count),
         name="grad_full",
-    )(me, parity, top_edge, *[values] * n, *[cotangent] * n)
+    )(me, parity, top_edge, *[values] * n, *[cotangent] * n, *after)
     return made[:n], made[n:]
 
 
@@ -476,13 +478,19 @@
         what, j = step[0], int(step[1:] or 0)
         if what == "F":
             if j == 0:
-                grad_blocks, blocks = first_full_chunk(
-                    me_arr, parity[0, 0], top, values[0], cotangent[0, 0],
-                    (3, 2, 1, 0), full_spans[0][1],
-                )
+                def first_blocks(ds, after):
+                    return first_full_chunk(
+                        me_arr, parity[0, 0], top, values[0], cotangent[0, 0],
+                        ds, full_spans[0][1], after,
+                    )
+
+                far_grad, far = first_blocks((3, 2), last)
+                near_grad, near = first_blocks((1, 0), [far[0]])
+                grad_blocks, blocks = [*far_grad, *near_grad][::-1], [*far, *near]
+                last = [near[0]]
             else:
                 blocks = full_chunk(top, grad_blocks, (3, 2, 1, 0), *full_spans[j], last)
-            last = [blocks[0]]
+                last = [blocks[0]]
             if j in HELD_BACK:
                 blocks = held_back(blocks, [full[j - 1][d] for d in HELD_BACK[j]] + [near_corner] * CORNER_FIRST)
                 last = [blocks[0]]

time: 773 us -> 771 us (level)
  transfers between devices with their start and end apart: 28 -> 28, of which waited for: 12 -> 12; matrix products, arithmetic and copies ran while one was open for 0% -> 0% of each run, Pallas kernels for 31% -> 32%
where the time goes in v5:
time: 771 us; the launch traced here: 768 us
  waiting for transfers between devices  465 us (60%)
  Pallas kernels  246 us (32%)
  starting transfers between devices  46.4 us (6%)
  local copies, waits for them, and re-layouts  9.23 us (1%)
    ppermute x22, waiting for transfers between devices, swapped(): return lax.ppermute(x, ('row', 'env'), pairs)  360 us
    ppermute x2, waiting for transfers between devices, passed_along(): return lax.ppermute(x, axis, [(i, (i + by) % size) for i in range(size)])  82.4 us
    pallas_call x7, Pallas kernels, absorbed_chunk(): pl.pallas_call(kernel, grid_spec=pltpu.PrefetchScalarGridSpec(num_scalar_...  63.3 us
    pallas_call x2, Pallas kernels, half_chunk(): pl.pallas_call(kernel, grid_spec=pltpu.PrefetchScalarGridSpec(num_scalar_...  53.3 us
    pallas_call x6, Pallas kernels, edge_chunk(): pl.pallas_call(kernel, grid=(count,), in_specs=[block_spec(offset) for _,...  45.5 us
    ppermute x22, starting transfers between devices, swapped(): return lax.ppermute(x, ('row', 'env'), pairs)  38.1 us
    ppermute x2, waiting for transfers between devices, swapped(): return lax.ppermute(x, 'env', [(i, i ^ d) for i in range(n_env)])  22.5 us
    pallas_call x1, Pallas kernels, full_chunk(): pl.pallas_call(kernel, grid=(count // step,), in_specs=[pl.BlockSpec((row...  21.7 us
  transfers between devices with their start and end apart: 28, of which 12 were waited for; matrix products, arithmetic and copies ran while one was open for 0% of the time, Pallas kernels for 32%

profile of v5, /device:TPU:9, one launch (start us, length us, event | category | flops | bytes accessed | tf_op | source)
XLA Modules:
  0.0 767.7 jit_solution(10398398452038896694)
XLA Ops:
  15.5 21.7 %grad_full.5 = (bf16[28,256,256]{2,1,0:T(8,128)(2,1)}, bf16[28,256,256]{2,1,0:T(8,128)(2,1)}, bf16[28,256,256]{2,1,0:T(8,128)(2,1)}, bf16[28,256,256]{2,1,0:T(8,128)(2,1)}) custom-call(bf16[256,32768]{1,0:T(8,128)(2,1)} %bitcast.21, bf16[256,1024]{1,0:T(8,128)(2,1)} %get-tuple-element.42.refs_0_.refs_7_, ...), custom_call_target="tpu_custom_call" | custom-call | flops 29360128 | bytes 114688 | tf_op jit(solution)/shard_map/grad_full/pallas_call | solution.py:92
  37.2 7.6 collective-permute-done.2.refs_4_.refs_2_
  44.8 11.2 %collective-permute-done.3.refs_5_.refs_3_ = bf16[4,256,256]{2,1,0:T(8,128)(2,1)S(1)} collective-permute-done((bf16[4,256,256]{2,1,0:T(8,128)(2,1)}, bf16[4,256,256]{2,1,0:T(8,128)(2,1)S(1)}, u32[]{:S(2)}, u32[]{:S(2)}) %collective-permute-start.3) | collective-permute-done | bytes 524320 | tf_op jit(solution)/shard_map/ppermute | solution.py:42
  64.2 82.4 %collective-permute-done.1 = s32[4,8]{1,0:T(4,128)S(1)} collective-permute-done((s32[4,8]{1,0:T(4,128)S(1)}, s32[4,8]{1,0:T(4,128)S(1)}, u32[]{:S(2)}, u32[]{:S(2)}) %collective-permute-start.1) | collective-permute-done | bytes 160 | tf_op jit(solution)/shard_map/ppermute | solution.py:31
  146.6 8.5 %collective-permute-start.7 = (bf16[28,256,256]{2,1,0:T(8,128)(2,1)}, bf16[28,256,256]{2,1,0:T(8,128)(2,1)}, u32[]{:S(2)}, u32[]{:S(2)}) collective-permute-start(bf16[28,256,256]{2,1,0:T(8,128)(2,1)} %get-tuple-element.53.refs_0_), channel_id=1, source_target_pairs={{0,11},{1,10},{2,9},{3,8},{8,19},{9,18},{10,17},{11,16},{16,27},{1... | collective-permute-start | bytes 11010056 | tf_op jit(solution)/shard_map/ppermute | solution.py:42
  161.4 19.8 %k_major.1.l_ref.refs_2_ = bf16[32,1024,256]{2,1,0:T(8,128)(2,1)} custom-call(bf16[256,32768]{1,0:T(8,128)(2,1)} %bitcast.27, bf16[1024,1024]{1,0:T(8,128)(2,1)} %get-tuple-element.54.refs_0_.refs_1_), custom_call_target="tpu_custom_call" | custom-call | flops 1048576 | bytes 4096 | tf_op jit(solution)/shard_map/k_major/pallas_call | solution.py:167
  181.3 9.0 %absorbed.7 = (bf16[9,256,256]{2,1,0:T(8,128)(2,1)}, bf16[9,256,256]{2,1,0:T(8,128)(2,1)}) custom-call(s32[1]{0:T(128)} %bitcast.me_ref, bf16[32,1024,256]{2,1,0:T(8,128)(2,1)} %k_major.1.l_ref.refs_2_, bf16[1024,1024]{1,0:T(8,128)(2,1)} %get-tuple-element.54.refs_0_.refs_1_, bf16[1024,1024]{1,0:T(8,128)(2,1)} %get-tuple-element.54.refs_0_.refs_1_, ...), custom_call_target="tpu_custom_call" | custom-call | flops 9437184 | bytes 36864 | tf_op jit(solution)/shard_map/absorbed/pallas_call | solution.py:227
  190.3 27.6 %absorbed.8 = (bf16[32,256,256]{2,1,0:T(8,128)(2,1)}, bf16[32,256,256]{2,1,0:T(8,128)(2,1)}) custom-call(s32[1]{0:T(128)} %bitcast.me_ref, bf16[32,1024,256]{2,1,0:T(8,128)(2,1)} %k_major.1.l_ref.refs_2_, bf16[1024,1024]{1,0:T(8,128)(2,1)} %get-tuple-element.54.refs_0_.refs_1_, bf16[1024,1024]{1,0:T(8,128)(2,1)} %get-tuple-element.54.refs_0_.refs_1_, ...), custom_call_target="tpu_custom_call" | custom-call | flops 33554432 | bytes 131072 | tf_op jit(solution)/shard_map/absorbed/pallas_call | solution.py:227
  217.9 12.8 %collective-permute-done.9.refs_1_ = bf16[4,256,256]{2,1,0:T(8,128)(2,1)S(1)} collective-permute-done((bf16[4,256,256]{2,1,0:T(8,128)(2,1)}, bf16[4,256,256]{2,1,0:T(8,128)(2,1)S(1)}, u32[]{:S(2)}, u32[]{:S(2)}) %collective-permute-start.9) | collective-permute-done | bytes 524320 | tf_op jit(solution)/shard_map/ppermute | solution.py:42
  234.9 9.0 %absorbed.9 = (bf16[9,256,256]{2,1,0:T(8,128)(2,1)}, bf16[9,256,256]{2,1,0:T(8,128)(2,1)}) custom-call(s32[1]{0:T(128)} %bitcast.me_ref, bf16[32,1024,256]{2,1,0:T(8,128)(2,1)} %k_major.1.l_ref.refs_2_, bf16[1024,1024]{1,0:T(8,128)(2,1)} %get-tuple-element.54.refs_0_.refs_1_, bf16[1024,1024]{1,0:T(8,128)(2,1)} %get-tuple-element.54.refs_0_.refs_1_, ...), custom_call_target="tpu_custom_call" | custom-call | flops 9437184 | bytes 36864 | tf_op jit(solution)/shard_map/absorbed/pallas_call | solution.py:227
  243.9 9.9 %grad_half.2 = (bf16[4,1024,256]{2,1,0:T(8,128)(2,1)}, f32[1024,1024]{1,0:T(8,128)}, f32[8,256]{1,0:T(8,128)}) custom-call(s32[1]{0:T(128)} %bitcast.me_ref, bf16[32,1024,256]{2,1,0:T(8,128)(2,1)} %k_major.1.l_ref.refs_2_, bf16[4,256,256]{2,1,0:T(8,128)(2,1)} %copy-done.12, bf16[4,256,256]{2,1,0:T(8,128)(2,1)} %copy-done.13, bf16[4,256,256]{2,1,0:T(8,128)(2,1)} %copy-done.5, ...), custom_call_target="tpu_custom_call" | custom-call | flops 8388608 | bytes 32768 | tf_op jit(solution)/shard_map/grad_half/pallas_call | solution.py:285
  253.8 124.4 %collective-permute-done.7.refs_3_ = bf16[28,256,256]{2,1,0:T(8,128)(2,1)} collective-permute-done((bf16[28,256,256]{2,1,0:T(8,128)(2,1)}, bf16[28,256,256]{2,1,0:T(8,128)(2,1)}, u32[]{:S(2)}, u32[]{:S(2)}) %collective-permute-start.7) | collective-permute-done | bytes 3670048 | tf_op jit(solution)/shard_map/ppermute | solution.py:42
  378.2 43.4 %grad_half.3 = (bf16[28,1024,256]{2,1,0:T(8,128)(2,1)}, f32[1024,1024]{1,0:T(8,128)}, f32[8,256]{1,0:T(8,128)}) custom-call(s32[1]{0:T(128)} %bitcast.me_ref, bf16[32,1024,256]{2,1,0:T(8,128)(2,1)} %k_major.1.l_ref.refs_2_, bf16[28,256,256]{2,1,0:T(8,128)(2,1)} %collective-permute-done.4.refs_0_, bf16[28,256,256]{2,1,0:T(8,128)(2,1)} %collective-permute-done.5.refs_1_, ...), custom_call_target="tpu_custom_call" | custom-call | flops 58720256 | bytes 229376 | tf_op jit(solution)/shard_map/grad_half/pallas_call | solution.py:285
  424.2 29.7 %collective-permute-done.13.refs_2_ = bf16[9,256,256]{2,1,0:T(8,128)(2,1)} collective-permute-done((bf16[9,256,256]{2,1,0:T(8,128)(2,1)}, bf16[9,256,256]{2,1,0:T(8,128)(2,1)}, u32[]{:S(2)}, u32[]{:S(2)}) %collective-permute-start.13) | collective-permute-done | bytes 1179680 | tf_op jit(solution)/shard_map/ppermute | solution.py:42
  457.3 72.5 %collective-permute-done.14.refs_3_ = bf16[9,256,256]{2,1,0:T(8,128)(2,1)} collective-permute-done((bf16[9,256,256]{2,1,0:T(8,128)(2,1)S(1)}, bf16[9,256,256]{2,1,0:T(8,128)(2,1)}, u32[]{:S(2)}, u32[]{:S(2)}) %collective-permute-start.14) | collective-permute-done | bytes 1179680 | tf_op jit(solution)/shard_map/ppermute | solution.py:42
  540.6 11.4 %grad_edge.6.refs_2_.refs_9_ = bf16[256,32768]{1,0:T(8,128)(2,1)} custom-call(bf16[32,256,256]{2,1,0:T(8,128)(2,1)} %collective-permute-done.11.refs_0_, bf16[32,256,256]{2,1,0:T(8,128)(2,1)} %copy-done, bf16[9,256,256]{2,1,0:T(8,128)(2,1)} %collective-permute-done.13.refs_2_, bf16[9,256,256]{2,1,0:T(8,128)(2,1)} %collective-permute-done.14.refs_3_, ...), custom_call_target="tpu_custom_call" | custom-call | flops 9437184 | bytes 36864 | tf_op jit(solution)/shard_map/grad_edge/pallas_call | solution.py:328
  562.1 37.9 %collective-permute-done.16.refs_2_ = bf16[9,256,256]{2,1,0:T(8,128)(2,1)} collective-permute-done((bf16[9,256,256]{2,1,0:T(8,128)(2,1)}, bf16[9,256,256]{2,1,0:T(8,128)(2,1)}, u32[]{:S(2)}, u32[]{:S(2)}) %collective-permute-start.16) | collective-permute-done | bytes 1179680 | tf_op jit(solution)/shard_map/ppermute | solution.py:42
  603.3 44.4 %collective-permute-done.17.refs_3_ = bf16[9,256,256]{2,1,0:T(8,128)(2,1)S(1)} collective-permute-done((bf16[9,256,256]{2,1,0:T(8,128)(2,1)S(1)}, bf16[9,256,256]{2,1,0:T(8,128)(2,1)S(1)}, u32[]{:S(2)}, u32[]{:S(2)}) %collective-permute-start.17) | collective-permute-done | bytes 1179680 | tf_op jit(solution)/shard_map/ppermute | solution.py:42
  650.1 20.0 %k_minor.1.refs_8_ = bf16[256,32768]{1,0:T(8,128)(2,1)} custom-call(bf16[4,1024,256]{2,1,0:T(8,128)(2,1)} %get-tuple-element.72.refs_0_, bf16[28,1024,256]{2,1,0:T(8,128)(2,1)} %get-tuple-element.73.refs_1_, bf16[256,1024]{1,0:T(8,128)(2,1)} %corner_quarter.1.refs_2_), custom_call_target="tpu_custom_call" | custom-call | flops 1048576 | bytes 4096 | tf_op jit(solution)/shard_map/k_minor/pallas_call | solution.py:187
  670.1 22.5 %collective-permute-done.15.quarter_ref = bf16[256,1024]{1,0:T(8,128)(2,1)} collective-permute-done((bf16[256,1024]{1,0:T(8,128)(2,1)}, bf16[256,1024]{1,0:T(8,128)(2,1)}, u32[]{:S(2)}, u32[]{:S(2)}) %collective-permute-start.15) | collective-permute-done | bytes 524320 | tf_op jit(solution)/shard_map/ppermute | solution.py:37
  693.2 11.4 %grad_edge.7.refs_2_.refs_9_ = bf16[256,32768]{1,0:T(8,128)(2,1)} custom-call(bf16[32,256,256]{2,1,0:T(8,128)(2,1)} %collective-permute-done.11.refs_0_, bf16[32,256,256]{2,1,0:T(8,128)(2,1)} %copy-done, bf16[9,256,256]{2,1,0:T(8,128)(2,1)} %collective-permute-done.16.refs_2_, bf16[9,256,256]{2,1,0:T(8,128)(2,1)} %copy-done.9, ...), custom_call_target="tpu_custom_call", output_to_operand_aliasing={{}: (9, {})} | custom-call | flops 9437184 | bytes 36864 | tf_op jit(solution)/shard_map/grad_edge/pallas_call | solution.py:328
  716.1 8.1 %grad_edge.8.refs_2_.refs_9_ = bf16[256,32768]{1,0:T(8,128)(2,1)} custom-call(bf16[32,256,256]{2,1,0:T(8,128)(2,1)} %collective-permute-done.11.refs_0_, bf16[32,256,256]{2,1,0:T(8,128)(2,1)} %copy-done, bf16[6,256,256]{2,1,0:T(8,128)(2,1)} %collective-permute-done.19.refs_2_, ...), custom_call_target="tpu_custom_call", output_to_operand_aliasing={{}: (9, {})} | custom-call | flops 6291456 | bytes 24576 | tf_op jit(solution)/shard_map/grad_edge/pallas_call | solution.py:328
  727.7 9.9 %collective-permute-done.26.refs_3_ = bf16[4,256,256]{2,1,0:T(8,128)(2,1)S(1)} collective-permute-done((bf16[4,256,256]{2,1,0:T(8,128)(2,1)}, bf16[4,256,256]{2,1,0:T(8,128)(2,1)S(1)}, u32[]{:S(2)}, u32[]{:S(2)}) %collective-permute-start.26) | collective-permute-done | bytes 524320 | tf_op jit(solution)/shard_map/ppermute | solution.py:42
  746.7 9.6 %collective-permute-done.24.refs_3_ = bf16[3,256,256]{2,1,0:T(8,128)(2,1)S(1)} collective-permute-done((bf16[3,256,256]{2,1,0:T(8,128)(2,1)S(1)}, bf16[3,256,256]{2,1,0:T(8,128)(2,1)S(1)}, u32[]{:S(2)}, u32[]{:S(2)}) %collective-permute-start.24) | collective-permute-done | bytes 393248 | tf_op jit(solution)/shard_map/ppermute | solution.py:42
  (109 shorter events, 102.2 us)
Async XLA Ops:
  0.6 55.4 %collective-permute-start = (bf16[1024,1024]{1,0:T(8,128)(2,1)}, bf16[1024,1024]{1,0:T(8,128)(2,1)S(1)}, u32[]{:S(2)}, u32[]{:S(2)}) collective-permute-start(bf16[1024,1024]{1,0:T(8,128)(2,1)} %bitcast.41), channel_id=1, source_target_pairs={{0,12},{4,8},{8,20},{12,16},{16,28},{20,24},{24,4},{28,0},{1,13},{... | collective-permute-start | bytes 6291464 | tf_op jit(solution)/shard_map/ppermute | solution.py:51
  8.5 36.4 %collective-permute-start.2 = (bf16[4,256,256]{2,1,0:T(8,128)(2,1)}, bf16[4,256,256]{2,1,0:T(8,128)(2,1)S(1)}, u32[]{:S(2)}, u32[]{:S(2)}) collective-permute-start(bf16[4,256,256]{2,1,0:T(8,128)(2,1)} %get-tuple-element.52), channel_id=1, source_target_pairs={{0,10},{1,11},{2,8},{3,9},{8,18},{9,19},{10,16},{11,17},{16,26},{1... | collective-permute-start | bytes 1572872 | tf_op jit(solution)/shard_map/ppermute | solution.py:42
  10.5 45.6 %collective-permute-start.3 = (bf16[4,256,256]{2,1,0:T(8,128)(2,1)}, bf16[4,256,256]{2,1,0:T(8,128)(2,1)S(1)}, u32[]{:S(2)}, u32[]{:S(2)}) collective-permute-start(bf16[4,256,256]{2,1,0:T(8,128)(2,1)} %get-tuple-element.44.refs_4_), channel_id=1, source_target_pairs={{0,11},{1,10},{2,9},{3,8},{8,19},{9,18},{10,17},{11,16},{16,27},{1... | collective-permute-start | bytes 1572872 | tf_op jit(solution)/shard_map/ppermute | solution.py:42
  57.6 173.1 %collective-permute-start.4 = (bf16[28,256,256]{2,1,0:T(8,128)(2,1)}, bf16[28,256,256]{2,1,0:T(8,128)(2,1)}, u32[]{:S(2)}, u32[]{:S(2)}) collective-permute-start(bf16[28,256,256]{2,1,0:T(8,128)(2,1)} %get-tuple-element.55), channel_id=1, source_target_pairs={{0,8},{1,9},{2,10},{3,11},{8,16},{9,17},{10,18},{11,19},{16,24},{1... | collective-permute-start | bytes 11010056 | tf_op jit(solution)/shard_map/ppermute | solution.py:42
  58.5 172.2 %collective-permute-start.5 = (bf16[28,256,256]{2,1,0:T(8,128)(2,1)}, bf16[28,256,256]{2,1,0:T(8,128)(2,1)}, u32[]{:S(2)}, u32[]{:S(2)}) collective-permute-start(bf16[28,256,256]{2,1,0:T(8,128)(2,1)} %get-tuple-element.56), channel_id=1, source_target_pairs={{0,9},{1,8},{2,11},{3,10},{8,17},{9,16},{10,19},{11,18},{16,25},{1... | collective-permute-start | bytes 11010056 | tf_op jit(solution)/shard_map/ppermute | solution.py:42
  58.5 176.2 %collective-permute-start.6 = (bf16[28,256,256]{2,1,0:T(8,128)(2,1)}, bf16[28,256,256]{2,1,0:T(8,128)(2,1)}, u32[]{:S(2)}, u32[]{:S(2)}) collective-permute-start(bf16[28,256,256]{2,1,0:T(8,128)(2,1)} %get-tuple-element.57), channel_id=1, source_target_pairs={{0,10},{1,11},{2,8},{3,9},{8,18},{9,19},{10,16},{11,17},{16,26},{1... | collective-permute-start | bytes 11010056 | tf_op jit(solution)/shard_map/ppermute | solution.py:42
  62.5 84.0 %collective-permute-start.8 = (bf16[4,256,256]{2,1,0:T(8,128)(2,1)S(1)}, bf16[4,256,256]{2,1,0:T(8,128)(2,1)S(1)}, u32[]{:S(2)}, u32[]{:S(2)}) collective-permute-start(bf16[4,256,256]{2,1,0:T(8,128)(2,1)S(1)} %copy-done.21), channel_id=1, source_target_pairs={{0,8},{1,9},{2,10},{3,11},{8,16},{9,17},{10,18},{11,19},{16,24},{1... | collective-permute-start | bytes 1572872 | tf_op jit(solution)/shard_map/ppermute | solution.py:42
  62.7 83.9 %collective-permute-start.1 = (s32[4,8]{1,0:T(4,128)S(1)}, s32[4,8]{1,0:T(4,128)S(1)}, u32[]{:S(2)}, u32[]{:S(2)}) collective-permute-start(s32[4,8]{1,0:T(4,128)S(1)} %bitcast.38), channel_id=1, source_target_pairs={{0,8},{8,16},{16,24},{24,0},{1,9},{9,17},{17,25},{25,1},{2,10},{10... | collective-permute-start | bytes 392 | tf_op jit(solution)/shard_map/ppermute | solution.py:31
  146.6 84.1 %collective-permute-start.9 = (bf16[4,256,256]{2,1,0:T(8,128)(2,1)}, bf16[4,256,256]{2,1,0:T(8,128)(2,1)S(1)}, u32[]{:S(2)}, u32[]{:S(2)}) collective-permute-start(bf16[4,256,256]{2,1,0:T(8,128)(2,1)} %get-tuple-element.47.refs_4_), channel_id=1, source_target_pairs={{0,9},{1,8},{2,11},{3,10},{8,17},{9,16},{10,19},{11,18},{16,25},{1... | collective-permute-start | bytes 1572872 | tf_op jit(solution)/shard_map/ppermute | solution.py:42
  146.6 231.7 %collective-permute-start.7 = (bf16[28,256,256]{2,1,0:T(8,128)(2,1)}, bf16[28,256,256]{2,1,0:T(8,128)(2,1)}, u32[]{:S(2)}, u32[]{:S(2)}) collective-permute-start(bf16[28,256,256]{2,1,0:T(8,128)(2,1)} %get-tuple-element.53.refs_0_), channel_id=1, source_target_pairs={{0,11},{1,10},{2,9},{3,8},{8,19},{9,18},{10,17},{11,16},{16,27},{1... | collective-permute-start | bytes 11010056 | tf_op jit(solution)/shard_map/ppermute | solution.py:42
  230.7 307.9 %collective-permute-start.12 = (bf16[32,256,256]{2,1,0:T(8,128)(2,1)}, bf16[32,256,256]{2,1,0:T(8,128)(2,1)S(1)}, u32[]{:S(2)}, u32[]{:S(2)}) collective-permute-start(bf16[32,256,256]{2,1,0:T(8,128)(2,1)} %get-tuple-element.67), channel_id=1, source_target_pairs={{0,25},{1,24},{2,27},{3,26},{8,1},{9,0},{10,3},{11,2},{16,9},{17,8... | collective-permute-start | bytes 12582920 | tf_op jit(solution)/shard_map/ppermute | solution.py:42
  230.7 307.9 %collective-permute-start.11 = (bf16[32,256,256]{2,1,0:T(8,128)(2,1)}, bf16[32,256,256]{2,1,0:T(8,128)(2,1)}, u32[]{:S(2)}, u32[]{:S(2)}) collective-permute-start(bf16[32,256,256]{2,1,0:T(8,128)(2,1)} %get-tuple-element.61.refs_2_), channel_id=1, source_target_pairs={{0,24},{1,25},{2,26},{3,27},{8,0},{9,1},{10,2},{11,3},{16,8},{17,9... | collective-permute-start | bytes 12582920 | tf_op jit(solution)/shard_map/ppermute | solution.py:42
  230.8 223.1 %collective-permute-start.13 = (bf16[9,256,256]{2,1,0:T(8,128)(2,1)}, bf16[9,256,256]{2,1,0:T(8,128)(2,1)}, u32[]{:S(2)}, u32[]{:S(2)}) collective-permute-start(bf16[9,256,256]{2,1,0:T(8,128)(2,1)} %get-tuple-element.68), channel_id=1, source_target_pairs={{0,26},{1,27},{2,24},{3,25},{8,2},{9,3},{10,0},{11,1},{16,10},{17,... | collective-permute-start | bytes 3538952 | tf_op jit(solution)/shard_map/ppermute | solution.py:42
  234.8 295.1 %collective-permute-start.14 = (bf16[9,256,256]{2,1,0:T(8,128)(2,1)S(1)}, bf16[9,256,256]{2,1,0:T(8,128)(2,1)}, u32[]{:S(2)}, u32[]{:S(2)}) collective-permute-start(bf16[9,256,256]{2,1,0:T(8,128)(2,1)S(1)} %copy-done.7), channel_id=1, source_target_pairs={{0,27},{1,26},{2,25},{3,24},{8,3},{9,2},{10,1},{11,0},{16,11},{17,... | collective-permute-start | bytes 3538952 | tf_op jit(solution)/shard_map/ppermute | solution.py:42
  424.2 132.5 %collective-permute-start.10 = (bf16[2,256,1024]{2,1,0:T(8,128)(2,1)}, bf16[2,256,1024]{2,1,0:T(8,128)(2,1)S(1)}, u32[]{:S(2)}, u32[]{:S(2)}) collective-permute-start(bf16[2,256,1024]{2,1,0:T(8,128)(2,1)} %corner_halves.1.refs_2_), channel_id=1, source_target_pairs={{0,1},{1,0},{2,3},{3,2},{4,5},{5,4},{6,7},{7,6},{8,9},{9,8},{10,11... | collective-permute-start | bytes 3145736 | tf_op jit(solution)/shard_map/ppermute | solution.py:37
  453.9 146.1 %collective-permute-start.16 = (bf16[9,256,256]{2,1,0:T(8,128)(2,1)}, bf16[9,256,256]{2,1,0:T(8,128)(2,1)}, u32[]{:S(2)}, u32[]{:S(2)}) collective-permute-start(bf16[9,256,256]{2,1,0:T(8,128)(2,1)} %get-tuple-element.71), channel_id=1, source_target_pairs={{0,26},{1,27},{2,24},{3,25},{8,2},{9,3},{10,0},{11,1},{16,10},{17,... | collective-permute-start | bytes 3538952 | tf_op jit(solution)/shard_map/ppermute | solution.py:42
  529.8 117.9 %collective-permute-start.17 = (bf16[9,256,256]{2,1,0:T(8,128)(2,1)S(1)}, bf16[9,256,256]{2,1,0:T(8,128)(2,1)S(1)}, u32[]{:S(2)}, u32[]{:S(2)}) collective-permute-start(bf16[9,256,256]{2,1,0:T(8,128)(2,1)S(1)} %copy-done.8), channel_id=1, source_target_pairs={{0,27},{1,26},{2,25},{3,24},{8,3},{9,2},{10,1},{11,0},{16,11},{17,... | collective-permute-start | bytes 3538952 | tf_op jit(solution)/shard_map/ppermute | solution.py:42
  538.6 174.1 %collective-permute-start.19 = (bf16[6,256,256]{2,1,0:T(8,128)(2,1)}, bf16[6,256,256]{2,1,0:T(8,128)(2,1)}, u32[]{:S(2)}, u32[]{:S(2)}) collective-permute-start(bf16[6,256,256]{2,1,0:T(8,128)(2,1)} %get-tuple-element.75), channel_id=1, source_target_pairs={{0,26},{1,27},{2,24},{3,25},{8,2},{9,3},{10,0},{11,1},{16,10},{17,... | collective-permute-start | bytes 2359304 | tf_op jit(solution)/shard_map/ppermute | solution.py:42
  538.6 176.6 %collective-permute-start.20 = (bf16[6,256,256]{2,1,0:T(8,128)(2,1)}, bf16[6,256,256]{2,1,0:T(8,128)(2,1)}, u32[]{:S(2)}, u32[]{:S(2)}) collective-permute-start(bf16[6,256,256]{2,1,0:T(8,128)(2,1)} %get-tuple-element.69.refs_8_), channel_id=1, source_target_pairs={{0,27},{1,26},{2,25},{3,24},{8,3},{9,2},{10,1},{11,0},{16,11},{17,... | collective-permute-start | bytes 2359304 | tf_op jit(solution)/shard_map/ppermute | solution.py:42
  559.9 132.7 %collective-permute-start.15 = (bf16[256,1024]{1,0:T(8,128)(2,1)}, bf16[256,1024]{1,0:T(8,128)(2,1)}, u32[]{:S(2)}, u32[]{:S(2)}) collective-permute-start(bf16[256,1024]{1,0:T(8,128)(2,1)} %corner_quarter.1.refs_2_), channel_id=1, source_target_pairs={{0,2},{1,3},{2,0},{3,1},{4,6},{5,7},{6,4},{7,5},{8,10},{9,11},{10,... | collective-permute-start | bytes 1572872 | tf_op jit(solution)/shard_map/ppermute | solution.py:37
  599.9 126.7 %collective-permute-start.25 = (bf16[4,256,256]{2,1,0:T(8,128)(2,1)}, bf16[4,256,256]{2,1,0:T(8,128)(2,1)S(1)}, u32[]{:S(2)}, u32[]{:S(2)}) collective-permute-start(bf16[4,256,256]{2,1,0:T(8,128)(2,1)} %get-tuple-element.79), channel_id=1, source_target_pairs={{0,26},{1,27},{2,24},{3,25},{8,2},{9,3},{10,0},{11,1},{16,10},{17,... | collective-permute-start | bytes 1572872 | tf_op jit(solution)/shard_map/ppermute | solution.py:42
  647.7 89.9 %collective-permute-start.26 = (bf16[4,256,256]{2,1,0:T(8,128)(2,1)}, bf16[4,256,256]{2,1,0:T(8,128)(2,1)S(1)}, u32[]{:S(2)}, u32[]{:S(2)}) collective-permute-start(bf16[4,256,256]{2,1,0:T(8,128)(2,1)} %get-tuple-element.70.refs_0_), channel_id=1, source_target_pairs={{0,27},{1,26},{2,25},{3,24},{8,3},{9,2},{10,1},{11,0},{16,11},{17,... | collective-permute-start | bytes 1572872 | tf_op jit(solution)/shard_map/ppermute | solution.py:42
  715.2 41.0 %collective-permute-start.24 = (bf16[3,256,256]{2,1,0:T(8,128)(2,1)S(1)}, bf16[3,256,256]{2,1,0:T(8,128)(2,1)S(1)}, u32[]{:S(2)}, u32[]{:S(2)}) collective-permute-start(bf16[3,256,256]{2,1,0:T(8,128)(2,1)S(1)} %copy-done.16), channel_id=1, source_target_pairs={{0,27},{1,26},{2,25},{3,24},{8,3},{9,2},{10,1},{11,0},{16,11},{17,... | collective-permute-start | bytes 1179656 | tf_op jit(solution)/shard_map/ppermute | solution.py:42
  726.7 35.7 %collective-permute-start.21 = (bf16[1,256,256]{2,1,0:T(8,128)(2,1)}, bf16[1,256,256]{2,1,0:T(8,128)(2,1)S(1)}, u32[]{:S(2)}, u32[]{:S(2)}) collective-permute-start(bf16[1,256,256]{2,1,0:T(8,128)(2,1)} %get-tuple-element.76), channel_id=1, source_target_pairs={{0,26},{1,27},{2,24},{3,25},{8,2},{9,3},{10,0},{11,1},{16,10},{17,... | collective-permute-start | bytes 393224 | tf_op jit(solution)/shard_map/ppermute | solution.py:42
  (26 other events, 504.9 us)
